TPU v7x, 256 devices: a whole 4x4x8 slice. The times are simulated.
256 devices in a mesh: space: 16 (over z_lo, x), filt: 16 (over y, z_hi, core).
Axes of the slice: x: 4, y: 4, z: 8 (z_hi: 2, z_lo: 4; z = z_hi * 4 + z_lo), core: 2. Of those that a mesh axis runs over, the one named last changes fastest.
Arguments:
- volume: bfloat16 [256, 16, 4096], P('filt', 'space'), may hold values from -6 to 6
- filters: bfloat16 [3, 3, 3, 256, 256], P(None, None, None, 'space', 'filt'), may hold values from -0.078125 to 0.078125
- cotangent: bfloat16 [256, 16, 4096], P('filt', 'space'), may hold values from -6 to 6
Outputs:
- output: bfloat16 [256, 16, 4096], P('filt', 'space')
- input_grad: bfloat16 [256, 16, 4096], P('filt', 'space')
All inputs are finite; a program needn't handle non-finite values.
Results may differ from a plain program's by a relative error of at most 0.0013.
Values may be sent and summed in bfloat16 or wider, within the bound.
No kernel may reach another device: no remote copies, remote signals or barrier semaphores. Data moves between devices by JAX's collectives and lax.ppermute only.
A program may use at most 64 MiB of HBM per device.

v0:
```python
import jax
import jax.numpy as jnp
from jax import lax
from jax.sharding import PartitionSpec as P

NY = 64
NZ = 64


def padded_2(block, sides, width):
    for axis, dim in sides:
        count = lax.axis_size(axis)
        forward = [(i, i + 1) for i in range(count - 1)]
        backward = [(target, source) for source, target in forward]
        low = lax.ppermute(
            lax.slice_in_dim(block, block.shape[dim] - width, None, axis=dim), axis, forward
        )
        high = lax.ppermute(lax.slice_in_dim(block, 0, width, axis=dim), axis, backward)
        block = jnp.concatenate([low, block, high], axis=dim)
    return block


def convolve(volume_block, kernel):
    channels = volume_block.shape[0]
    planes = volume_block.shape[1]
    shaped = volume_block.reshape(channels, planes, NY, NZ)
    result = lax.conv_general_dilated(
        shaped[None],
        kernel,
        (1, 1, 1),
        [(0, 0), (1, 1), (1, 1)],
        dimension_numbers=("NCDHW", "DHWIO", "NCDHW"),
        preferred_element_type=jnp.float32,
    )[0]
    return result.reshape(result.shape[0], planes - 2, NY * NZ)


def flipped(kernel):
    return jnp.transpose(kernel[::-1, ::-1, ::-1], (0, 1, 2, 4, 3))


def local(volume, filters, cotangent):
    weights = lax.all_gather(filters, "space", axis=3, tiled=True)
    padded = padded_2(volume, (("space", 1),), 1)
    zero_carry = jnp.zeros(volume.shape, jnp.float32)
    kernel = weights
    output_sum = zero_carry + convolve(lax.all_gather(padded, "filt", axis=0, tiled=True), kernel)
    output = output_sum.astype(jnp.bfloat16)
    grad_padded = padded_2(cotangent, (("space", 1),), 1)
    kernel = flipped(weights)
    grad_sum = lax.psum_scatter(
        convolve(grad_padded, kernel), "filt", scatter_dimension=0, tiled=True
    )
    return (output, grad_sum.astype(jnp.bfloat16))


def solution(mesh):
    in_specs = (
        P("filt", "space", None),
        P(None, None, None, "space", "filt"),
        P("filt", "space", None),
    )
    out_specs = (P("filt", "space", None), P("filt", "space", None))
    return jax.shard_map(local, mesh=mesh, in_specs=in_specs, out_specs=out_specs, check_vma=False)
```

profile of v0, /device:TPU:32, one launch (start us, length us, event | category | flops | bytes accessed | tf_op | source)
XLA Modules:
  0.0 1548.1 jit_solution(611989725219796647)
XLA Ops:
  7.2 0.0 all-gather.2.cloned.1.call-start
  7.2 3.4 collective-permute-start
  10.6 4.6 collective-permute-start.1
  15.2 1.5 collective-permute-done
  16.7 1.3 collective-permute-done.1
  18.0 1.7 pad_maximum_fusion
  19.7 0.0 all-gather.2.cloned.1.call-update
  19.7 3.1 collective-permute-start.2
  22.8 5.2 collective-permute-start.3
  28.0 1.3 dynamic-slice
  29.9 61.6 %all_gather.7 = bf16[3,3,3,256,16]{4,3,2,1,0:T(8,128)(2,1)} all-gather(bf16[3,3,3,16,16]{4,3,2,1,0:T(8,128)(2,1)} %param.4), channel_id=1, replica_groups=mesh['space'=16,'filt'=16] {'space'}, dimensions={3}, use_global_device_ids=true | all-gather | bytes 235008 | tf_op jit(solution)/shard_map/all_gather | solution.py:43
  91.5 0.0 collective-permute-done.2
  91.5 0.0 collective-permute-done.3
  91.5 1.0 pad_maximum_fusion.1
  92.5 0.8 reshape.35
  93.3 0.0 copy-start.1
  93.3 0.6 copy.73
  94.0 1.1 pad.2.clone
  95.1 3.1 copy.67
  98.2 0.2 slice.6
  98.4 0.0 copy-done.1
  98.5 6.1 broadcast_select_fusion
  104.6 1.5 copy.68
  106.1 0.5 slice_bitcast_fusion
  106.6 4.5 copy.69
  111.1 10.2 copy.70
  121.3 1373.5 %all-reduce.2 = bf16[256,1,4096]{2,1,0:T(2,128)(2,1)} all-reduce(f32[256,1,4096]{2,1,0:T(1,128)} %copy.70), channel_id=2, replica_groups=mesh['space'=16,'filt'=16] {'filt'}, use_global_device_ids=true, to_apply=%region_0.0.clone | all-reduce | flops 1048576 | bytes 6291456
  1494.8 1.2 dynamic-slice_convert_fusion
  1496.0 0.8 copy.71
  1496.8 0.0 all-gather.2.cloned.1.call-done
  1496.8 8.6 copy.58
  1505.4 6.4 copy.72
  1511.8 1.2 pad.clone
  1513.0 4.1 copy.61
  1517.1 0.4 slice.4
  1517.4 0.0 copy-start
  1517.5 20.0 %fusion.3 = bf16[1,64,8,9,16]{4,2,3,1,0:T(8,128)(2,1)} fusion(bf16[3,3,3,256,16]{4,3,2,1,0:T(8,128)(2,1)} %all_gather.7, bf16[256,3,64,1,7,2]{0,4,5,2,1,3:T(8,128)(2,1)S(1)} %slice.4, bf16[256,3,64,1,8,9]{0,4,5,2,1,3:T(8,128)(2,1)S(1)} %copy.61), kind=kOutput, calls=%fused_computation.4 | convolution fusion | flops 1034551296 | bytes 8822784 | tf_op jit(solution)/shard_map/conv_general_dilated | solution.py:27
  1537.4 2.0 copy.62
  1539.4 0.0 copy-done
  1539.4 0.1 select_convert_fusion
  1539.6 0.3 copy.63
  1539.8 0.9 convert_element_type.18
  (1 shorter events, 0.0 us)
Async XLA Ops:
  7.2 1489.7 %all-gather.2.cloned.1.call-start = ((), (), s32[]{:S(2)}) async-start(), calls=%async_computation | async-start | bytes 6684672 | tf_op jit(solution)/shard_map/all_gather | solution.py:47
  7.2 9.4 collective-permute-start
  10.6 7.4 collective-permute-start.1
  19.7 71.8 %collective-permute-start.2 = (bf16[16,1,4096]{2,0,1:T(8,128)(2,1)}, bf16[16,1,4096]{2,0,1:T(8,128)(2,1)S(1)}, u32[]{:S(2)}, u32[]{:S(2)}) collective-permute-start(bf16[16,1,4096]{2,0,1:T(8,128)(2,1)} %param.5), channel_id=1, source_target_pairs={{0,16},{16,32},{32,48},{48,64},{64,80},{80,96},{96,112},{112,128},... | collective-permute-start | bytes 393224 | tf_op jit(solution)/shard_map/ppermute | solution.py:15
  22.8 68.7 %collective-permute-start.3 = (bf16[16,1,4096]{2,0,1:T(8,128)(2,1)}, bf16[16,1,4096]{2,0,1:T(8,128)(2,1)S(1)}, u32[]{:S(2)}, u32[]{:S(2)}) collective-permute-start(bf16[16,1,4096]{2,0,1:T(8,128)(2,1)} %param.5), channel_id=1, source_target_pairs={{16,0},{32,16},{48,32},{64,48},{80,64},{96,80},{112,96},{128,112},... | collective-permute-start | bytes 393224 | tf_op jit(solution)/shard_map/ppermute | solution.py:18
  93.3 5.1 copy-start.1
  1517.4 21.9 %copy-start = (pred[8,9]{1,0:T(8,128)(4,1)S(1)}, pred[8,9]{1,0:T(8,128)(4,1)}, u32[]{:S(2)}) copy-start(pred[8,9]{1,0:T(8,128)(4,1)} %constant.10) | copy-start | bytes 220
Sparse Core Ops, SparseCore 0:
  19.8 96.3 all-gather.1
where the time goes:
time: 1570 us; the launch traced here: 1550 us
  blocking collectives  1440 us (92%)
  local copies, waits for them, and re-layouts  49.7 us (3%)
  matrix products  26.1 us (2%)
  starting transfers between devices  16.3 us (1%)
    unnamed x1, blocking collectives  1370 us
    all_gather x1, blocking collectives, local(): weights = lax.all_gather(filters, 'space', axis=3, tiled=True)  61.6 us
  transfers between devices with their start and end apart: 5, of which 2 were waited for; matrix products, arithmetic and copies ran while one was open for 2% of the time, Pallas kernels for 0%

commit v1 on v0

v1 whole, which is shorter than its diff:
```python
import functools

import jax
import jax.numpy as jnp
from jax import lax
from jax.experimental import pallas as pl
from jax.experimental.pallas import tpu as pltpu
from jax.sharding import Mesh
from jax.sharding import PartitionSpec as P

AXES = ("zl", "x", "y", "zh", "core")
SPACE = ("zl", "x")
FILT = ("y", "zh", "core")
BF16 = jnp.bfloat16
F32 = jnp.float32
VMEM = pl.BlockSpec(memory_space=pltpu.VMEM)
PARAMS = pltpu.CompilerParams(vmem_limit_bytes=48 * 1024 * 1024)

GROUPS = 8
CELLS = 512
CHUNKS = 5
ROWS = CHUNKS * 16
OFFSETS = 27


def call(kernel, out_shape, flops=0, byte_count=1 << 20, scratch=()):
    single = not isinstance(out_shape, (tuple, list))
    count = 1 if single else len(out_shape)
    return functools.partial(
        pl.pallas_call,
        kernel,
        out_shape=out_shape,
        out_specs=VMEM if single else [VMEM] * count,
        scratch_shapes=list(scratch),
        compiler_params=PARAMS,
        cost_estimate=pl.CostEstimate(flops=flops, bytes_accessed=byte_count, transcendentals=0),
    )


def run(kernel, out_shape, *args, **options):
    return call(kernel, out_shape, **options)(in_specs=[VMEM] * len(args))(*args)


def pack_kernel(volume_ref, cotangent_ref, filters_ref, out_ref):
    lane = lax.broadcasted_iota(jnp.int32, (16, 128), 1)
    for part, ref in enumerate((volume_ref, cotangent_ref)):
        whole = pltpu.roll(ref[...].astype(F32), 64, 1)
        edge = whole[:, :128]
        pieces = [jnp.where(lane < 64, 0.0, edge)]
        pieces += [whole[:, 128 * j : 128 * (j + 1)] for j in range(1, 32)]
        pieces += [jnp.where(lane < 64, edge, 0.0)]
        pieces = [piece.astype(BF16) for piece in pieces]
        for slab in range(GROUPS):
            for chunk in range(CHUNKS):
                row = part * ROWS + chunk * 16
                out_ref[slab, row : row + 16, :] = pieces[4 * slab + chunk]
    for low in range(4):
        pieces = []
        for high in range(8):
            d = high * 4 + low
            pieces.append(filters_ref[d] if d < OFFSETS else jnp.zeros((16, 16), BF16))
        block = jnp.concatenate(pieces, axis=1)
        for slab in range(GROUPS):
            out_ref[slab, 2 * ROWS + 16 * low : 2 * ROWS + 16 * (low + 1), :] = block


def unpack_kernel(packed_ref, acts_ref, weights_ref):
    acts_ref[...] = packed_ref[:, : 2 * ROWS, :]
    for d in range(OFFSETS):
        high, low = divmod(d, 4)
        row = 2 * ROWS + 16 * low
        weights_ref[d] = jnp.concatenate(
            [packed_ref[g, row : row + 16, 16 * high : 16 * (high + 1)] for g in range(GROUPS)],
            axis=1,
        )


def shifted(pieces):
    whole = jnp.concatenate(pieces, axis=0)
    middle = pltpu.roll(whole.astype(F32), 640 - 64, 1).astype(BF16)
    return whole[:, :CELLS], middle[:, :CELLS], whole[:, 128:]


def block_of(ref, group, first):
    return jnp.concatenate(
        [ref[group, first + 16 * c : first + 16 * (c + 1), :] for c in range(CHUNKS)], axis=1
    )


def weight(weights_ref, d):
    return jnp.concatenate([weights_ref[s % 4, s // 4, d] for s in range(16)], axis=0)


def combine(before, middle, after):
    place = lax.broadcasted_iota(jnp.int32, middle.shape, 1) % 64
    left = jnp.where(place > 0, pltpu.roll(before, 1, 1), 0.0)
    right = jnp.where(place < 63, pltpu.roll(after, CELLS - 1, 1), 0.0)
    return middle + left + right


def grad_kernel(low_ref, own_ref, high_ref, weights_ref, core_ref, keep_ref, send_ref, stack_ref, result_ref):
    for dx, ref in enumerate((high_ref, own_ref, low_ref)):
        above, same, below = shifted([block_of(ref, g, ROWS) for g in range(GROUPS)])
        for dy, value in enumerate((below, same, above)):
            row = (dx * 3 + dy) * 128
            stack_ref[row : row + 128, :] = value
    terms = []
    for dz in range(3):
        left = jnp.concatenate([weight(weights_ref, k * 3 + dz) for k in range(9)], axis=1)
        terms.append(jnp.dot(left, stack_ref[...], preferred_element_type=F32))
    result_ref[...] = combine(terms[2], terms[1], terms[0]).reshape(GROUPS, 2, 16, CELLS)
    core = core_ref[0]
    keep_ref[...] = result_ref[:, core]
    send_ref[...] = result_ref[:, 1 - core]


def forward_kernel(low_ref, own_ref, high_ref, other_ref, weights_ref, core_ref, out_ref, stack_ref):
    first = core_ref[0] == 0
    for dx, ref in enumerate((low_ref, own_ref, high_ref)):
        pieces = []
        for g in range(GROUPS):
            mine = block_of(ref, g, 0)
            theirs = block_of(other_ref.at[dx], g, 0)
            pieces.append(jnp.where(first, mine, theirs))
            pieces.append(jnp.where(first, theirs, mine))
        for dy, value in enumerate(shifted(pieces)):
            row = (dx * 3 + dy) * 256
            stack_ref[row : row + 256, :] = value
    terms = []
    for dz in range(3):
        left = jnp.concatenate([weight(weights_ref, k * 3 + dz) for k in range(9)], axis=0)
        terms.append(
            lax.dot_general(left, stack_ref[...], (((0,), (0,)), ((), ())), preferred_element_type=F32)
        )
    out_ref[...] = combine(*terms).astype(BF16).reshape(GROUPS, 16, CELLS)


def merge_kernel(output_ref, keep_ref, got_ref, out_ref):
    out_ref[:, :16, :] = output_ref[...]
    out_ref[:, 16:, :] = (keep_ref[...] + got_ref[...]).astype(BF16)


def split_kernel(packed_ref, output_ref, grad_ref):
    for g in range(GROUPS):
        output_ref[:, g * CELLS : (g + 1) * CELLS] = packed_ref[g, :16, :]
        grad_ref[:, g * CELLS : (g + 1) * CELLS] = packed_ref[g, 16:, :]


def local(volume, filters, cotangent):
    swap = [(0, 1), (1, 0)]
    core = lax.axis_index("core").astype(jnp.int32).reshape(1)
    packed = run(
        pack_kernel,
        jax.ShapeDtypeStruct((GROUPS, 2 * ROWS + 64, 128), BF16),
        volume.reshape(16, 4096),
        cotangent.reshape(16, 4096),
        filters.reshape(OFFSETS, 16, 16),
    )
    packed = lax.all_to_all(packed, ("y", "zh"), 0, 0)
    own, weights = run(
        unpack_kernel,
        [
            jax.ShapeDtypeStruct((GROUPS, 2 * ROWS, 128), BF16),
            jax.ShapeDtypeStruct((OFFSETS, 16, 128), BF16),
        ],
        packed,
    )
    up = [(i, i + 1) for i in range(15)]
    down = [(b, a) for a, b in up]
    low = lax.ppermute(own, SPACE, up)
    high = lax.ppermute(own, SPACE, down)
    weights = lax.all_to_all(jnp.broadcast_to(weights, (4,) + weights.shape), "zl", 0, 0)
    weights = lax.all_to_all(jnp.broadcast_to(weights, (4,) + weights.shape), "x", 0, 0)
    other = lax.ppermute(jnp.stack([low[:, :ROWS], own[:, :ROWS], high[:, :ROWS]]), "core", swap)
    flops = 2 * 27 * 256 * 128 * CELLS
    piece = jax.ShapeDtypeStruct((GROUPS, 16, CELLS), F32)
    smem = pl.BlockSpec(memory_space=pltpu.SMEM)
    keep, send = call(
        grad_kernel,
        [piece, piece],
        flops=flops,
        byte_count=4 << 20,
        scratch=[pltpu.VMEM((9 * 128, CELLS), BF16), pltpu.VMEM((GROUPS, 2, 16, CELLS), F32)],
    )(in_specs=[VMEM] * 4 + [smem])(low, own, high, weights, core)
    got = lax.ppermute(send, "core", swap)
    output = call(
        forward_kernel,
        jax.ShapeDtypeStruct((GROUPS, 16, CELLS), BF16),
        flops=flops,
        byte_count=4 << 20,
        scratch=[pltpu.VMEM((9 * 256, CELLS), BF16)],
    )(in_specs=[VMEM] * 5 + [smem])(low, own, high, other, weights, core)
    merged = run(merge_kernel, jax.ShapeDtypeStruct((GROUPS, 32, CELLS), BF16), output, keep, got)
    merged = lax.all_to_all(merged, ("y", "zh"), 0, 0)
    plane = jax.ShapeDtypeStruct((16, 4096), BF16)
    output, grad = run(split_kernel, [plane, plane], merged)
    return output.reshape(16, 1, 4096), grad.reshape(16, 1, 4096)


def solution(mesh):
    split = Mesh(mesh.devices.reshape(4, 4, 4, 2, 2), AXES)
    act = P(FILT, SPACE, None)
    return jax.shard_map(
        local,
        mesh=split,
        in_specs=(act, P(None, None, None, SPACE, FILT), act),
        out_specs=(act, act),
        check_vma=False,
    )
```

time: 1570 us -> 103 us (0.07); the launches traced: 1550 us -> 102 us
  blocking collectives: 1440 us -> 59.1 us
  local copies, waits for them, and re-layouts: 49.7 us -> 4.24 us
  matrix products: 26.1 us -> 0 us
  waiting for transfers between devices: 2.84 us -> 20.5 us
    unnamed x1 -> x0, blocking collectives: 1370 us -> none
    all_gather x1 -> x0, blocking collectives: 61.6 us -> none  [local(): weights = lax.all_gather(filters, 'space', axis=3, tiled=True)]
    all_to_all x0 -> x3, blocking collectives: none -> 59.1 us  [the longest x1 28.2 us: local(): packed = lax.all_to_all(packed, ('y', 'zh'), 0, 0)]
    conv_general_dilated x2 -> x0, matrix products: 26.1 us -> none  [convolve(): lax.conv_general_dilated(shaped[None], kernel, (1, 1, 1), [(0, 0), (1, 1)...]
    ppermute x4, waiting for transfers between devices: 2.82 us -> 20.4 us  [the longest x1 20.3 us: local(): high = lax.ppermute(own, SPACE, down)]
    conv_general_dilated x8 -> x0, local copies, waits for them, and re-layouts: 16.2 us -> none  [convolve(): lax.conv_general_dilated(shaped[None], kernel, (1, 1, 1), [(0, 0), (1, 1)...]
  transfers between devices with their start and end apart: 5 -> 5, of which waited for: 2 -> 2; matrix products, arithmetic and copies ran while one was open for 2% -> 1% of each run, Pallas kernels for 0% -> 3%
where the time goes in v1:
time: 103 us; the launch traced here: 102 us
  blocking collectives  59.1 us (57%)
  waiting for transfers between devices  20.5 us (20%)
  starting transfers between devices  13 us (13%)
  local copies, waits for them, and re-layouts  4.24 us (4%)
  Pallas kernels  3.85 us (4%)
    all_to_all x1, blocking collectives, local(): packed = lax.all_to_all(packed, ('y', 'zh'), 0, 0)  28.2 us
    ppermute x1, waiting for transfers between devices, local(): high = lax.ppermute(own, SPACE, down)  20.3 us
    all_to_all x1, blocking collectives, local(): merged = lax.all_to_all(merged, ('y', 'zh'), 0, 0)  17 us
    all_to_all x1, blocking collectives, local(): lax.all_to_all(jnp.broadcast_to(weights, (4,) + weights.shape), 'zl', 0, 0)  13.9 us
    ppermute x1, starting transfers between devices, local(): high = lax.ppermute(own, SPACE, down)  6.16 us
    all_to_all x1, starting transfers between devices, local(): lax.all_to_all(jnp.broadcast_to(weights, (4,) + weights.shape), 'x', 0, 0)  4.29 us
    unnamed x6, local copies, waits for them, and re-layouts  2.7 us
  transfers between devices with their start and end apart: 5, of which 2 were waited for; matrix products, arithmetic and copies ran while one was open for 1% of the time, Pallas kernels for 3%

profile of v1, /device:TPU:32, one launch (start us, length us, event | category | flops | bytes accessed | tf_op | source)
XLA Modules:
  0.0 102.2 jit_solution(13998260443176025528)
XLA Ops:
  0.6 0.0 copy-start
  0.6 0.9 copy-done
  1.5 0.0 copy-start.1
  1.5 0.9 copy-done.1
  2.4 0.0 copy-start.2
  2.4 0.9 copy-done.2
  3.3 0.2 shard_map.50
  3.5 28.2 %all_to_all.20.packed_ref = bf16[8,224,128]{2,1,0:T(8,128)(2,1)S(1)} all-to-all(bf16[8,224,128]{2,1,0:T(8,128)(2,1)S(1)} %shard_map.50), channel_id=1, replica_groups=mesh['zl'=4,'x'=4,'y'=4,'zh'=2,'core'=2] {'y','zh'}, dimensions={0} | all-to-all | bytes 917504 | tf_op jit(solution)/shard_map/all_to_all | solution.py:159
  31.7 0.3 shard_map.51
  32.0 0.1 broadcast_in_dim.6
  32.1 13.9 %all_to_all.21 = bf16[4,27,16,128]{3,2,1,0:T(8,128)(2,1)S(1)} all-to-all(bf16[4,27,16,128]{3,2,1,0:T(8,128)(2,1)S(1)} %broadcast_in_dim.6), channel_id=1, replica_groups=mesh['zl'=4,'x'=4,'y'=4,'zh'=2,'core'=2] {'zl'}, dimensions={0} | all-to-all | bytes 884736 | tf_op jit(solution)/shard_map/all_to_all | solution.py:172
  46.0 1.4 %broadcast_in_dim.7 = bf16[4,4,27,16,128]{4,3,2,1,0:T(8,128)(2,1)} broadcast(bf16[4,27,16,128]{3,2,1,0:T(8,128)(2,1)S(1)} %all_to_all.21), dimensions={1,2,3,4} | broadcast | bytes 2211840 | tf_op jit(solution)/shard_map/broadcast_in_dim | solution.py:173
  47.4 4.3 %all-to-all-start.2 = ((bf16[4,4,27,16,128]{4,3,2,1,0:T(8,128)(2,1)}), bf16[4,4,27,16,128]{4,3,2,1,0:T(8,128)(2,1)S(1)}, u32[]{:S(2)}, u32[]{:S(2)}) async-start(bf16[4,4,27,16,128]{4,3,2,1,0:T(8,128)(2,1)} %broadcast_in_dim.7), calls=%async_computation.2 | async-start | bytes 3538944 | tf_op jit(solution)/shard_map/all_to_all | solution.py:173
  51.7 6.2 %collective-permute-start.1 = (bf16[8,160,128]{2,1,0:T(8,128)(2,1)S(1)}, bf16[8,160,128]{2,1,0:T(8,128)(2,1)S(1)}, u32[]{:S(2)}, u32[]{:S(2)}) collective-permute-start(bf16[8,160,128]{2,1,0:T(8,128)(2,1)S(1)} %get-tuple-element.8.own_ref), channel_id=1, source_target_pairs={{16,0},{32,16},{48,32},{64,48},{80,64},{96,80},{112,96},{128,112},... | collective-permute-start | bytes 983048 | tf_op jit(solution)/shard_map/ppermute | solution.py:171
  57.9 1.9 %collective-permute-start = (bf16[8,160,128]{2,1,0:T(8,128)(2,1)S(1)}, bf16[8,160,128]{2,1,0:T(8,128)(2,1)S(1)}, u32[]{:S(2)}, u32[]{:S(2)}) collective-permute-start(bf16[8,160,128]{2,1,0:T(8,128)(2,1)S(1)} %get-tuple-element.8.own_ref), channel_id=1, source_target_pairs={{0,16},{16,32},{32,48},{48,64},{64,80},{80,96},{96,112},{112,128},... | collective-permute-start | bytes 983048 | tf_op jit(solution)/shard_map/ppermute | solution.py:170
  59.8 20.3 %collective-permute-done.1.high_ref = bf16[8,160,128]{2,1,0:T(8,128)(2,1)S(1)} collective-permute-done((bf16[8,160,128]{2,1,0:T(8,128)(2,1)S(1)}, bf16[8,160,128]{2,1,0:T(8,128)(2,1)S(1)}, u32[]{:S(2)}, u32[]{:S(2)}) %collective-permute-start.1) | collective-permute-done | bytes 327712 | tf_op jit(solution)/shard_map/ppermute | solution.py:171
  80.1 0.0 collective-permute-done.low_ref
  80.1 0.9 pad_maximum_fusion
  81.0 0.0 collective-permute-start.2
  81.0 0.0 all-to-all-done.2.weights_ref
  81.0 1.3 %shard_map.53 = (f32[8,16,512]{2,1,0:T(8,128)S(1)}, f32[8,16,512]{2,1,0:T(8,128)S(1)}) custom-call(bf16[8,160,128]{2,1,0:T(8,128)(2,1)S(1)} %collective-permute-done.low_ref, bf16[8,160,128]{2,1,0:T(8,128)(2,1)S(1)} %get-tuple-element.8.own_ref, bf16[8,160,128]{2,1,0:T(8,128)(2,1)S(1)} %collective-permute-done.1.high_ref, ...), custom_call_target="tpu_custom_call" | custom-call | flops 905969664 | bytes 4194304 | tf_op jit(solution)/shard_map/pallas_call | solution.py:178
  82.3 0.6 collective-permute-start.3
  82.9 0.2 collective-permute-done.2.other_ref
  83.1 1.4 %shard_map.52.output_ref = bf16[8,16,512]{2,1,0:T(8,128)(2,1)S(1)} custom-call(bf16[8,160,128]{2,1,0:T(8,128)(2,1)S(1)} %collective-permute-done.low_ref, bf16[8,160,128]{2,1,0:T(8,128)(2,1)S(1)} %get-tuple-element.8.own_ref, bf16[8,160,128]{2,1,0:T(8,128)(2,1)S(1)} %collective-permute-done.1.high_ref, ...), custom_call_target="tpu_custom_call" | custom-call | flops 905969664 | bytes 4194304 | tf_op jit(solution)/shard_map/pallas_call | solution.py:186
  84.5 0.0 collective-permute-done.3.got_ref
  84.5 17.0 %all_to_all.22.packed_ref = bf16[8,32,512]{2,1,0:T(8,128)(2,1)S(1)} all-to-all(bf16[8,32,512]{2,1,0:T(8,128)(2,1)S(1)} %shard_map.54), channel_id=1, replica_groups=mesh['zl'=4,'x'=4,'y'=4,'zh'=2,'core'=2] {'y','zh'}, dimensions={0} | all-to-all | bytes 524288 | tf_op jit(solution)/shard_map/all_to_all | solution.py:194
  101.5 0.7 shard_map.55
  (4 shorter events, 0.1 us)
Async XLA Ops:
  0.6 0.9 copy-start
  1.5 0.9 copy-start.1
  2.4 0.9 copy-start.2
  47.4 33.6 %all-to-all-start.2 = ((bf16[4,4,27,16,128]{4,3,2,1,0:T(8,128)(2,1)}), bf16[4,4,27,16,128]{4,3,2,1,0:T(8,128)(2,1)S(1)}, u32[]{:S(2)}, u32[]{:S(2)}) async-start(bf16[4,4,27,16,128]{4,3,2,1,0:T(8,128)(2,1)} %broadcast_in_dim.7), calls=%async_computation.2 | async-start | bytes 3538944 | tf_op jit(solution)/shard_map/all_to_all | solution.py:173
  51.7 28.4 %collective-permute-start.1 = (bf16[8,160,128]{2,1,0:T(8,128)(2,1)S(1)}, bf16[8,160,128]{2,1,0:T(8,128)(2,1)S(1)}, u32[]{:S(2)}, u32[]{:S(2)}) collective-permute-start(bf16[8,160,128]{2,1,0:T(8,128)(2,1)S(1)} %get-tuple-element.8.own_ref), channel_id=1, source_target_pairs={{16,0},{32,16},{48,32},{64,48},{80,64},{96,80},{112,96},{128,112},... | collective-permute-start | bytes 983048 | tf_op jit(solution)/shard_map/ppermute | solution.py:171
  57.9 22.3 %collective-permute-start = (bf16[8,160,128]{2,1,0:T(8,128)(2,1)S(1)}, bf16[8,160,128]{2,1,0:T(8,128)(2,1)S(1)}, u32[]{:S(2)}, u32[]{:S(2)}) collective-permute-start(bf16[8,160,128]{2,1,0:T(8,128)(2,1)S(1)} %get-tuple-element.8.own_ref), channel_id=1, source_target_pairs={{0,16},{16,32},{32,48},{48,64},{64,80},{80,96},{96,112},{112,128},... | collective-permute-start | bytes 983048 | tf_op jit(solution)/shard_map/ppermute | solution.py:170
  81.0 2.1 %collective-permute-start.2 = (bf16[3,8,80,128]{3,2,1,0:T(8,128)(2,1)}, bf16[3,8,80,128]{3,2,1,0:T(8,128)(2,1)S(1)}, u32[]{:S(2)}, u32[]{:S(2)}) collective-permute-start(bf16[3,8,80,128]{3,2,1,0:T(8,128)(2,1)} %pad_maximum_fusion), channel_id=1, source_target_pairs={{0,1},{1,0},{2,3},{3,2},{4,5},{5,4},{6,7},{7,6},{8,9},{9,8},{10,11... | collective-permute-start | bytes 1474568 | tf_op jit(solution)/shard_map/ppermute | solution.py:174
  82.3 2.1 %collective-permute-start.3 = (f32[8,16,512]{2,1,0:T(8,128)S(1)}, f32[8,16,512]{2,1,0:T(8,128)S(1)}, u32[]{:S(2)}, u32[]{:S(2)}) collective-permute-start(f32[8,16,512]{2,1,0:T(8,128)S(1)} %get-tuple-element.11), channel_id=1, source_target_pairs={{0,1},{1,0},{2,3},{3,2},{4,5},{5,4},{6,7},{7,6},{8,9},{9,8},{10,11... | collective-permute-start | bytes 786440 | tf_op jit(solution)/shard_map/ppermute | solution.py:185

commit v2 on v1

--- a/solution.py
+++ b/solution.py
@@ -1,4 +1,5 @@
 import functools
+import itertools
 
 import jax
 import jax.numpy as jnp
@@ -21,6 +22,32 @@
 CHUNKS = 5
 ROWS = CHUNKS * 16
 OFFSETS = 27
+PART = 7
+
+
+def index_of(zl, x, y, zh, core):
+    return (((zl * 4 + x) * 4 + y) * 2 + zh) * 2 + core
+
+
+def everyone():
+    return itertools.product(range(4), range(4), range(4), range(2), range(2))
+
+
+def first_groups():
+    sides = itertools.product(range(4), range(4), range(2))
+    groups = []
+    for zl, other, zh in sides:
+        groups.append([index_of(zl, k, other, zh, 0) for k in range(4)])
+        groups.append([index_of(zl, other, k, zh, 1) for k in range(4)])
+    return groups
+
+
+def second_pairs(step):
+    pairs = []
+    for zl, x, y, zh, core in everyone():
+        to = (zl, x, (y + step) % 4, zh, 0) if core == 0 else (zl, (x + step) % 4, y, zh, 1)
+        pairs.append((index_of(zl, x, y, zh, core), index_of(*to)))
+    return pairs
 
 
 def call(kernel, out_shape, flops=0, byte_count=1 << 20, scratch=()):
@@ -54,25 +81,24 @@
             for chunk in range(CHUNKS):
                 row = part * ROWS + chunk * 16
                 out_ref[slab, row : row + 16, :] = pieces[4 * slab + chunk]
-    for low in range(4):
+    for quarter in range(4):
         pieces = []
-        for high in range(8):
-            d = high * 4 + low
-            pieces.append(filters_ref[d] if d < OFFSETS else jnp.zeros((16, 16), BF16))
+        for d in range(quarter * PART, quarter * PART + 8):
+            used = d < min(OFFSETS, (quarter + 1) * PART)
+            pieces.append(filters_ref[d] if used else jnp.zeros((16, 16), BF16))
         block = jnp.concatenate(pieces, axis=1)
-        for slab in range(GROUPS):
-            out_ref[slab, 2 * ROWS + 16 * low : 2 * ROWS + 16 * (low + 1), :] = block
+        for slab in (2 * quarter, 2 * quarter + 1):
+            out_ref[slab, 2 * ROWS :, :] = block
 
 
 def unpack_kernel(packed_ref, acts_ref, weights_ref):
     acts_ref[...] = packed_ref[:, : 2 * ROWS, :]
-    for d in range(OFFSETS):
-        high, low = divmod(d, 4)
-        row = 2 * ROWS + 16 * low
-        weights_ref[d] = jnp.concatenate(
-            [packed_ref[g, row : row + 16, 16 * high : 16 * (high + 1)] for g in range(GROUPS)],
-            axis=1,
+    for d in range(PART):
+        piece = jnp.concatenate(
+            [packed_ref[g, 2 * ROWS :, 16 * d : 16 * (d + 1)] for g in range(GROUPS)], axis=1
         )
+        for copy in range(4):
+            weights_ref[copy, d] = piece
 
 
 def shifted(pieces):
@@ -87,8 +113,15 @@
     )
 
 
-def weight(weights_ref, d):
-    return jnp.concatenate([weights_ref[s % 4, s // 4, d] for s in range(16)], axis=0)
+def weight(weights_ref, core, d):
+    quarter, part = divmod(d, PART)
+    rows = []
+    for s in range(16):
+        x = s % 4
+        outer = jnp.where(core == 0, quarter, x)
+        inner = jnp.where(core == 0, x, quarter)
+        rows.append(weights_ref[outer, inner, s // 4, part])
+    return jnp.concatenate(rows, axis=0)
 
 
 def combine(before, middle, after):
@@ -98,7 +131,16 @@
     return middle + left + right
 
 
-def grad_kernel(low_ref, own_ref, high_ref, weights_ref, core_ref, keep_ref, send_ref, stack_ref, result_ref):
+def grad_kernel(
+    low_ref, own_ref, high_ref, mine_ref, next_ref, last_ref, far_a_ref, far_b_ref, place_ref,
+    keep_ref, send_ref, weights_ref, stack_ref, result_ref,
+):
+    core, me = place_ref[0], place_ref[1]
+    weights_ref[me] = mine_ref[...]
+    weights_ref[lax.rem(me + 1, 4)] = next_ref[...]
+    weights_ref[lax.rem(me + 3, 4)] = last_ref[...]
+    weights_ref[lax.rem(me + 2, 4), :2] = far_a_ref[...]
+    weights_ref[lax.rem(me + 2, 4), 2:] = far_b_ref[...]
     for dx, ref in enumerate((high_ref, own_ref, low_ref)):
         above, same, below = shifted([block_of(ref, g, ROWS) for g in range(GROUPS)])
         for dy, value in enumerate((below, same, above)):
@@ -106,16 +148,16 @@
             stack_ref[row : row + 128, :] = value
     terms = []
     for dz in range(3):
-        left = jnp.concatenate([weight(weights_ref, k * 3 + dz) for k in range(9)], axis=1)
+        left = jnp.concatenate([weight(weights_ref, core, k * 3 + dz) for k in range(9)], axis=1)
         terms.append(jnp.dot(left, stack_ref[...], preferred_element_type=F32))
     result_ref[...] = combine(terms[2], terms[1], terms[0]).reshape(GROUPS, 2, 16, CELLS)
-    core = core_ref[0]
     keep_ref[...] = result_ref[:, core]
     send_ref[...] = result_ref[:, 1 - core]
 
 
-def forward_kernel(low_ref, own_ref, high_ref, other_ref, weights_ref, core_ref, out_ref, stack_ref):
-    first = core_ref[0] == 0
+def forward_kernel(low_ref, own_ref, high_ref, other_ref, weights_ref, place_ref, out_ref, stack_ref):
+    core = place_ref[0]
+    first = core == 0
     for dx, ref in enumerate((low_ref, own_ref, high_ref)):
         pieces = []
         for g in range(GROUPS):
@@ -128,7 +170,7 @@
             stack_ref[row : row + 256, :] = value
     terms = []
     for dz in range(3):
-        left = jnp.concatenate([weight(weights_ref, k * 3 + dz) for k in range(9)], axis=0)
+        left = jnp.concatenate([weight(weights_ref, core, k * 3 + dz) for k in range(9)], axis=0)
         terms.append(
             lax.dot_general(left, stack_ref[...], (((0,), (0,)), ((), ())), preferred_element_type=F32)
         )
@@ -148,10 +190,12 @@
 
 def local(volume, filters, cotangent):
     swap = [(0, 1), (1, 0)]
-    core = lax.axis_index("core").astype(jnp.int32).reshape(1)
+    core = lax.axis_index("core").astype(jnp.int32)
+    me = jnp.where(core == 0, lax.axis_index("y"), lax.axis_index("x")).astype(jnp.int32)
+    place = jnp.stack([core, me])
     packed = run(
         pack_kernel,
-        jax.ShapeDtypeStruct((GROUPS, 2 * ROWS + 64, 128), BF16),
+        jax.ShapeDtypeStruct((GROUPS, 2 * ROWS + 16, 128), BF16),
         volume.reshape(16, 4096),
         cotangent.reshape(16, 4096),
         filters.reshape(OFFSETS, 16, 16),
@@ -161,7 +205,7 @@
         unpack_kernel,
         [
             jax.ShapeDtypeStruct((GROUPS, 2 * ROWS, 128), BF16),
-            jax.ShapeDtypeStruct((OFFSETS, 16, 128), BF16),
+            jax.ShapeDtypeStruct((4, PART, 16, 128), BF16),
         ],
         packed,
     )
@@ -169,19 +213,24 @@
     down = [(b, a) for a, b in up]
     low = lax.ppermute(own, SPACE, up)
     high = lax.ppermute(own, SPACE, down)
-    weights = lax.all_to_all(jnp.broadcast_to(weights, (4,) + weights.shape), "zl", 0, 0)
-    weights = lax.all_to_all(jnp.broadcast_to(weights, (4,) + weights.shape), "x", 0, 0)
+    weights = lax.all_to_all(weights, "zl", 0, 0)
+    weights = jnp.broadcast_to(weights, (4,) + weights.shape)
+    mine = lax.all_to_all(weights, AXES, 0, 0, axis_index_groups=first_groups())
+    last = lax.ppermute(mine, AXES, second_pairs(1))
+    after = lax.ppermute(mine, AXES, second_pairs(3))
+    far_a = lax.ppermute(last[:2], AXES, second_pairs(1))
+    far_b = lax.ppermute(after[2:], AXES, second_pairs(3))
     other = lax.ppermute(jnp.stack([low[:, :ROWS], own[:, :ROWS], high[:, :ROWS]]), "core", swap)
     flops = 2 * 27 * 256 * 128 * CELLS
     piece = jax.ShapeDtypeStruct((GROUPS, 16, CELLS), F32)
     smem = pl.BlockSpec(memory_space=pltpu.SMEM)
-    keep, send = call(
+    keep, send, weights = call(
         grad_kernel,
-        [piece, piece],
+        [piece, piece, jax.ShapeDtypeStruct((4, 4, 4, PART, 16, 128), BF16)],
         flops=flops,
         byte_count=4 << 20,
         scratch=[pltpu.VMEM((9 * 128, CELLS), BF16), pltpu.VMEM((GROUPS, 2, 16, CELLS), F32)],
-    )(in_specs=[VMEM] * 4 + [smem])(low, own, high, weights, core)
+    )(in_specs=[VMEM] * 8 + [smem])(low, own, high, mine, after, last, far_a, far_b, place)
     got = lax.ppermute(send, "core", swap)
     output = call(
         forward_kernel,
@@ -189,7 +238,7 @@
         flops=flops,
         byte_count=4 << 20,
         scratch=[pltpu.VMEM((9 * 256, CELLS), BF16)],
-    )(in_specs=[VMEM] * 5 + [smem])(low, own, high, other, weights, core)
+    )(in_specs=[VMEM] * 5 + [smem])(low, own, high, other, weights, place)
     merged = run(merge_kernel, jax.ShapeDtypeStruct((GROUPS, 32, CELLS), BF16), output, keep, got)
     merged = lax.all_to_all(merged, ("y", "zh"), 0, 0)
     plane = jax.ShapeDtypeStruct((16, 4096), BF16)

time: 103 us -> 95.9 us (0.931)
  waiting for transfers between devices: 20.5 us -> 12.5 us
  blocking collectives: 59.1 us -> 53.7 us
  starting transfers between devices: 13 us -> 18.3 us
  Pallas kernels: 3.85 us -> 4.93 us
    ppermute x1, waiting for transfers between devices: 20.3 us -> 0.62 us  [local(): high = lax.ppermute(own, SPACE, down)]
    ppermute x0 -> x4, waiting for transfers between devices: none -> 6.55 us  [the longest x1 3.21 us: local(): far_a = lax.ppermute(last[:2], AXES, second_pairs(1))]
    ppermute x0 -> x4, starting transfers between devices: none -> 6.54 us  [the longest x1 3.23 us: local(): after = lax.ppermute(mine, AXES, second_pairs(3))]
    all_to_all x1, blocking collectives: 13.9 us -> 8.58 us  [local(): weights = lax.all_to_all(weights, 'zl', 0, 0)]
    all_to_all x1, waiting for transfers between devices: 0.01 us -> 3.12 us  [local(): mine = lax.all_to_all(weights, AXES, 0, 0, axis_index_groups=first_groups())]
    ppermute x1, waiting for transfers between devices: 0.01 us -> 2.19 us  [local(): low = lax.ppermute(own, SPACE, up)]
    all_to_all x1, blocking collectives: 28.2 us -> 26.2 us  [local(): packed = lax.all_to_all(packed, ('y', 'zh'), 0, 0)]
    all_to_all x1, blocking collectives: 17 us -> 18.9 us  [local(): merged = lax.all_to_all(merged, ('y', 'zh'), 0, 0)]
  transfers between devices with their start and end apart: 5 -> 9, of which waited for: 2 -> 6; matrix products, arithmetic and copies ran while one was open for 1% -> 2% of each run, Pallas kernels for 3% -> 4%
where the time goes in v2:
time: 95.9 us; the launch traced here: 95.4 us
  blocking collectives  53.7 us (56%)
  starting transfers between devices  18.3 us (19%)
  waiting for transfers between devices  12.5 us (13%)
  Pallas kernels  4.93 us (5%)
  local copies, waits for them, and re-layouts  4.27 us (4%)
    all_to_all x1, blocking collectives, local(): packed = lax.all_to_all(packed, ('y', 'zh'), 0, 0)  26.2 us
    all_to_all x1, blocking collectives, local(): merged = lax.all_to_all(merged, ('y', 'zh'), 0, 0)  18.9 us
    all_to_all x1, blocking collectives, local(): weights = lax.all_to_all(weights, 'zl', 0, 0)  8.58 us
    ppermute x1, starting transfers between devices, local(): high = lax.ppermute(own, SPACE, down)  5.41 us
    all_to_all x1, starting transfers between devices, local(): mine = lax.all_to_all(weights, AXES, 0, 0, axis_index_groups=first_groups())  4.29 us
    ppermute x1, starting transfers between devices, local(): after = lax.ppermute(mine, AXES, second_pairs(3))  3.23 us
    ppermute x1, starting transfers between devices, local(): far_b = lax.ppermute(after[2:], AXES, second_pairs(3))  3.22 us
    ppermute x1, waiting for transfers between devices, local(): far_a = lax.ppermute(last[:2], AXES, second_pairs(1))  3.21 us
  transfers between devices with their start and end apart: 9, of which 6 were waited for; matrix products, arithmetic and copies ran while one was open for 2% of the time, Pallas kernels for 4%

profile of v2, /device:TPU:32, one launch (start us, length us, event | category | flops | bytes accessed | tf_op | source)
XLA Modules:
  0.0 95.4 jit_solution(6956386392163008706)
XLA Ops:
  0.6 0.0 copy-start
  0.6 0.9 copy-done
  1.5 0.0 copy-start.1
  1.5 0.9 copy-done.1
  2.4 0.0 copy-start.2
  2.4 0.9 copy-done.2
  3.3 0.2 shard_map.50
  3.5 26.2 %all_to_all.20.packed_ref = bf16[8,176,128]{2,1,0:T(8,128)(2,1)S(1)} all-to-all(bf16[8,176,128]{2,1,0:T(8,128)(2,1)S(1)} %shard_map.50), channel_id=1, replica_groups=mesh['zl'=4,'x'=4,'y'=4,'zh'=2,'core'=2] {'y','zh'}, dimensions={0} | all-to-all | bytes 720896 | tf_op jit(solution)/shard_map/all_to_all | solution.py:203
  29.7 0.1 shard_map.51
  29.9 8.6 %all_to_all.21 = bf16[4,7,16,128]{3,2,1,0:T(8,128)(2,1)S(1)} all-to-all(bf16[4,7,16,128]{3,2,1,0:T(8,128)(2,1)S(1)} %get-tuple-element.10), channel_id=1, replica_groups=mesh['zl'=4,'x'=4,'y'=4,'zh'=2,'core'=2] {'zl'}, dimensions={0} | all-to-all | bytes 229376 | tf_op jit(solution)/shard_map/all_to_all | solution.py:216
  38.4 0.8 broadcast_in_dim.3
  39.3 4.3 %all-to-all-start.2 = ((bf16[4,4,7,16,128]{4,3,2,1,0:T(8,128)(2,1)}), bf16[4,4,7,16,128]{4,3,2,1,0:T(8,128)(2,1)S(1)}, u32[]{:S(2)}, u32[]{:S(2)}) async-start(bf16[4,4,7,16,128]{4,3,2,1,0:T(8,128)(2,1)} %broadcast_in_dim.3), calls=%async_computation.2 | async-start | bytes 917504 | tf_op jit(solution)/shard_map/all_to_all | solution.py:218
  43.6 5.4 %collective-permute-start.1 = (bf16[8,160,128]{2,1,0:T(8,128)(2,1)S(1)}, bf16[8,160,128]{2,1,0:T(8,128)(2,1)S(1)}, u32[]{:S(2)}, u32[]{:S(2)}) collective-permute-start(bf16[8,160,128]{2,1,0:T(8,128)(2,1)S(1)} %get-tuple-element.9.own_ref), channel_id=1, source_target_pairs={{16,0},{32,16},{48,32},{64,48},{80,64},{96,80},{112,96},{128,112},... | collective-permute-start | bytes 983048 | tf_op jit(solution)/shard_map/ppermute | solution.py:215
  49.0 1.9 %collective-permute-start = (bf16[8,160,128]{2,1,0:T(8,128)(2,1)S(1)}, bf16[8,160,128]{2,1,0:T(8,128)(2,1)S(1)}, u32[]{:S(2)}, u32[]{:S(2)}) collective-permute-start(bf16[8,160,128]{2,1,0:T(8,128)(2,1)S(1)} %get-tuple-element.9.own_ref), channel_id=1, source_target_pairs={{0,16},{16,32},{32,48},{48,64},{64,80},{80,96},{96,112},{112,128},... | collective-permute-start | bytes 983048 | tf_op jit(solution)/shard_map/ppermute | solution.py:214
  50.9 3.1 %all-to-all-done.2.mine_ref = bf16[4,4,7,16,128]{4,3,2,1,0:T(8,128)(2,1)S(1)} async-done(((bf16[4,4,7,16,128]{4,3,2,1,0:T(8,128)(2,1)}), bf16[4,4,7,16,128]{4,3,2,1,0:T(8,128)(2,1)S(1)}, u32[]{:S(2)}, u32[]{:S(2)}) %all-to-all-start.2) | async-done | bytes 458784 | tf_op jit(solution)/shard_map/all_to_all | solution.py:218
  54.0 0.0 collective-permute-start.4
  54.0 3.2 %collective-permute-start.3 = (bf16[4,4,7,16,128]{4,3,2,1,0:T(8,128)(2,1)S(1)}, bf16[4,4,7,16,128]{4,3,2,1,0:T(8,128)(2,1)S(1)}, u32[]{:S(2)}, u32[]{:S(2)}) collective-permute-start(bf16[4,4,7,16,128]{4,3,2,1,0:T(8,128)(2,1)S(1)} %all-to-all-done.2.mine_ref), channel_id=1, source_target_pairs={{0,12},{1,49},{2,14},{3,51},{4,0},{5,53},{6,2},{7,55},{8,4},{9,57}... | collective-permute-start | bytes 1376264 | tf_op jit(solution)/shard_map/ppermute | solution.py:220
  57.3 0.6 collective-permute-done.1.high_ref
  57.9 2.2 %collective-permute-done.low_ref = bf16[8,160,128]{2,1,0:T(8,128)(2,1)S(1)} collective-permute-done((bf16[8,160,128]{2,1,0:T(8,128)(2,1)S(1)}, bf16[8,160,128]{2,1,0:T(8,128)(2,1)S(1)}, u32[]{:S(2)}, u32[]{:S(2)}) %collective-permute-start) | collective-permute-done | bytes 327712 | tf_op jit(solution)/shard_map/ppermute | solution.py:214
  60.1 0.8 pad_maximum_fusion
  61.0 2.8 %collective-permute-done.4.last_ref = bf16[4,4,7,16,128]{4,3,2,1,0:T(8,128)(2,1)S(1)} collective-permute-done((bf16[4,4,7,16,128]{4,3,2,1,0:T(8,128)(2,1)S(1)}, bf16[4,4,7,16,128]{4,3,2,1,0:T(8,128)(2,1)S(1)}, u32[]{:S(2)}, u32[]{:S(2)}) %collective-permute-start.4) | collective-permute-done | bytes 458784 | tf_op jit(solution)/shard_map/ppermute | solution.py:219
  63.8 0.1 collective-permute-start.5
  63.8 0.0 collective-permute-done.3.next_ref
  63.9 0.7 slice.23
  64.6 3.2 %collective-permute-start.6 = (bf16[2,4,7,16,128]{4,3,2,1,0:T(8,128)(2,1)}, bf16[2,4,7,16,128]{4,3,2,1,0:T(8,128)(2,1)S(1)}, u32[]{:S(2)}, u32[]{:S(2)}) collective-permute-start(bf16[2,4,7,16,128]{4,3,2,1,0:T(8,128)(2,1)} %slice.23), channel_id=1, source_target_pairs={{0,12},{1,49},{2,14},{3,51},{4,0},{5,53},{6,2},{7,55},{8,4},{9,57}... | collective-permute-start | bytes 688136 | tf_op jit(solution)/shard_map/ppermute | solution.py:222
  67.8 0.0 collective-permute-start.2
  67.8 0.1 pad_add_fusion.place_ref
  67.9 3.2 %collective-permute-done.5.far_a_ref = bf16[2,4,7,16,128]{4,3,2,1,0:T(8,128)(2,1)S(1)} collective-permute-done((bf16[2,4,7,16,128]{4,3,2,1,0:T(8,128)(2,1)S(1)}, bf16[2,4,7,16,128]{4,3,2,1,0:T(8,128)(2,1)S(1)}, u32[]{:S(2)}, u32[]{:S(2)}) %collective-permute-start.5) | collective-permute-done | bytes 229408 | tf_op jit(solution)/shard_map/ppermute | solution.py:221
  71.1 0.6 collective-permute-done.6.far_b_ref
  71.6 1.9 %shard_map.52 = (f32[8,16,512]{2,1,0:T(8,128)S(1)}, f32[8,16,512]{2,1,0:T(8,128)S(1)}, bf16[4,4,4,7,16,128]{5,4,3,2,1,0:T(8,128)(2,1)S(1)}) custom-call(bf16[8,160,128]{2,1,0:T(8,128)(2,1)S(1)} %collective-permute-done.low_ref, bf16[8,160,128]{2,1,0:T(8,128)(2,1)S(1)} %get-tuple-element.9.own_ref, bf16[8,160,128]{2,1,0:T(8,128)(2,1)S(1)} %collective-permute-done.1.high_ref, ...), custom_call_target="tpu_custom_call" | custom-call | flops 905969664 | bytes 4194304 | tf_op jit(solution)/shard_map/pallas_call | solution.py:227
  73.6 0.1 collective-permute-start.7
  73.7 0.0 collective-permute-done.2.other_ref
  73.7 1.9 %shard_map.53.output_ref = bf16[8,16,512]{2,1,0:T(8,128)(2,1)S(1)} custom-call(bf16[8,160,128]{2,1,0:T(8,128)(2,1)S(1)} %collective-permute-done.low_ref, bf16[8,160,128]{2,1,0:T(8,128)(2,1)S(1)} %get-tuple-element.9.own_ref, bf16[8,160,128]{2,1,0:T(8,128)(2,1)S(1)} %collective-permute-done.1.high_ref, ...), custom_call_target="tpu_custom_call" | custom-call | flops 905969664 | bytes 4194304 | tf_op jit(solution)/shard_map/pallas_call | solution.py:235
  75.6 0.0 collective-permute-done.7.got_ref
  75.6 0.1 shard_map.54
  75.7 18.9 %all_to_all.22.packed_ref = bf16[8,32,512]{2,1,0:T(8,128)(2,1)S(1)} all-to-all(bf16[8,32,512]{2,1,0:T(8,128)(2,1)S(1)} %shard_map.54), channel_id=1, replica_groups=mesh['zl'=4,'x'=4,'y'=4,'zh'=2,'core'=2] {'y','zh'}, dimensions={0} | all-to-all | bytes 524288 | tf_op jit(solution)/shard_map/all_to_all | solution.py:243
  94.7 0.7 shard_map.55
  (4 shorter events, 0.1 us)
Async XLA Ops:
  0.6 0.9 copy-start
  1.5 0.9 copy-start.1
  2.4 0.9 copy-start.2
  39.3 14.8 %all-to-all-start.2 = ((bf16[4,4,7,16,128]{4,3,2,1,0:T(8,128)(2,1)}), bf16[4,4,7,16,128]{4,3,2,1,0:T(8,128)(2,1)S(1)}, u32[]{:S(2)}, u32[]{:S(2)}) async-start(bf16[4,4,7,16,128]{4,3,2,1,0:T(8,128)(2,1)} %broadcast_in_dim.3), calls=%async_computation.2 | async-start | bytes 917504 | tf_op jit(solution)/shard_map/all_to_all | solution.py:218
  43.6 14.4 %collective-permute-start.1 = (bf16[8,160,128]{2,1,0:T(8,128)(2,1)S(1)}, bf16[8,160,128]{2,1,0:T(8,128)(2,1)S(1)}, u32[]{:S(2)}, u32[]{:S(2)}) collective-permute-start(bf16[8,160,128]{2,1,0:T(8,128)(2,1)S(1)} %get-tuple-element.9.own_ref), channel_id=1, source_target_pairs={{16,0},{32,16},{48,32},{64,48},{80,64},{96,80},{112,96},{128,112},... | collective-permute-start | bytes 983048 | tf_op jit(solution)/shard_map/ppermute | solution.py:215
  49.0 11.1 %collective-permute-start = (bf16[8,160,128]{2,1,0:T(8,128)(2,1)S(1)}, bf16[8,160,128]{2,1,0:T(8,128)(2,1)S(1)}, u32[]{:S(2)}, u32[]{:S(2)}) collective-permute-start(bf16[8,160,128]{2,1,0:T(8,128)(2,1)S(1)} %get-tuple-element.9.own_ref), channel_id=1, source_target_pairs={{0,16},{16,32},{32,48},{48,64},{64,80},{80,96},{96,112},{112,128},... | collective-permute-start | bytes 983048 | tf_op jit(solution)/shard_map/ppermute | solution.py:214
  54.0 9.7 %collective-permute-start.4 = (bf16[4,4,7,16,128]{4,3,2,1,0:T(8,128)(2,1)S(1)}, bf16[4,4,7,16,128]{4,3,2,1,0:T(8,128)(2,1)S(1)}, u32[]{:S(2)}, u32[]{:S(2)}) collective-permute-start(bf16[4,4,7,16,128]{4,3,2,1,0:T(8,128)(2,1)S(1)} %all-to-all-done.2.mine_ref), channel_id=1, source_target_pairs={{0,4},{1,17},{2,6},{3,19},{4,8},{5,21},{6,10},{7,23},{8,12},{9,25}... | collective-permute-start | bytes 1376264 | tf_op jit(solution)/shard_map/ppermute | solution.py:219
  54.0 9.8 %collective-permute-start.3 = (bf16[4,4,7,16,128]{4,3,2,1,0:T(8,128)(2,1)S(1)}, bf16[4,4,7,16,128]{4,3,2,1,0:T(8,128)(2,1)S(1)}, u32[]{:S(2)}, u32[]{:S(2)}) collective-permute-start(bf16[4,4,7,16,128]{4,3,2,1,0:T(8,128)(2,1)S(1)} %all-to-all-done.2.mine_ref), channel_id=1, source_target_pairs={{0,12},{1,49},{2,14},{3,51},{4,0},{5,53},{6,2},{7,55},{8,4},{9,57}... | collective-permute-start | bytes 1376264 | tf_op jit(solution)/shard_map/ppermute | solution.py:220
  63.8 7.3 %collective-permute-start.5 = (bf16[2,4,7,16,128]{4,3,2,1,0:T(8,128)(2,1)S(1)}, bf16[2,4,7,16,128]{4,3,2,1,0:T(8,128)(2,1)S(1)}, u32[]{:S(2)}, u32[]{:S(2)}) collective-permute-start(bf16[2,4,7,16,128]{4,3,2,1,0:T(8,128)(2,1)S(1)} %slice.22), channel_id=1, source_target_pairs={{0,4},{1,17},{2,6},{3,19},{4,8},{5,21},{6,10},{7,23},{8,12},{9,25}... | collective-permute-start | bytes 688136 | tf_op jit(solution)/shard_map/ppermute | solution.py:221
  64.6 7.1 %collective-permute-start.6 = (bf16[2,4,7,16,128]{4,3,2,1,0:T(8,128)(2,1)}, bf16[2,4,7,16,128]{4,3,2,1,0:T(8,128)(2,1)S(1)}, u32[]{:S(2)}, u32[]{:S(2)}) collective-permute-start(bf16[2,4,7,16,128]{4,3,2,1,0:T(8,128)(2,1)} %slice.23), channel_id=1, source_target_pairs={{0,12},{1,49},{2,14},{3,51},{4,0},{5,53},{6,2},{7,55},{8,4},{9,57}... | collective-permute-start | bytes 688136 | tf_op jit(solution)/shard_map/ppermute | solution.py:222
  67.8 5.9 %collective-permute-start.2 = (bf16[3,8,80,128]{3,2,1,0:T(8,128)(2,1)}, bf16[3,8,80,128]{3,2,1,0:T(8,128)(2,1)S(1)}, u32[]{:S(2)}, u32[]{:S(2)}) collective-permute-start(bf16[3,8,80,128]{3,2,1,0:T(8,128)(2,1)} %pad_maximum_fusion), channel_id=1, source_target_pairs={{0,1},{1,0},{2,3},{3,2},{4,5},{5,4},{6,7},{7,6},{8,9},{9,8},{10,11... | collective-permute-start | bytes 1474568 | tf_op jit(solution)/shard_map/ppermute | solution.py:223
  73.6 2.1 %collective-permute-start.7 = (f32[8,16,512]{2,1,0:T(8,128)S(1)}, f32[8,16,512]{2,1,0:T(8,128)S(1)}, u32[]{:S(2)}, u32[]{:S(2)}) collective-permute-start(f32[8,16,512]{2,1,0:T(8,128)S(1)} %get-tuple-element.13), channel_id=1, source_target_pairs={{0,1},{1,0},{2,3},{3,2},{4,5},{5,4},{6,7},{7,6},{8,9},{9,8},{10,11... | collective-permute-start | bytes 786440 | tf_op jit(solution)/shard_map/ppermute | solution.py:234

commit v3 on v1

--- a/solution.py
+++ b/solution.py
@@ -1,4 +1,5 @@
 import functools
+import itertools
 
 import jax
 import jax.numpy as jnp
@@ -21,6 +22,28 @@
 CHUNKS = 5
 ROWS = CHUNKS * 16
 OFFSETS = 27
+PART = 7
+
+
+def index_of(zl, x, y, zh, core):
+    return (((zl * 4 + x) * 4 + y) * 2 + zh) * 2 + core
+
+
+def everyone():
+    return itertools.product(range(4), range(4), range(4), range(2), range(2))
+
+
+def pairs_of(move):
+    return [(index_of(*place), index_of(*move(*place))) for place in everyone()]
+
+
+def along(first, step):
+    def move(zl, x, y, zh, core):
+        if (core == 0) == first:
+            return zl, (x - step) % 4, y, zh, core
+        return zl, x, (y - step) % 4, zh, core
+
+    return pairs_of(move)
 
 
 def call(kernel, out_shape, flops=0, byte_count=1 << 20, scratch=()):
@@ -41,7 +64,20 @@
     return call(kernel, out_shape, **options)(in_specs=[VMEM] * len(args))(*args)
 
 
-def pack_kernel(volume_ref, cotangent_ref, filters_ref, out_ref):
+def pack_kernel(place_ref, volume_ref, cotangent_ref, filters_ref, out_ref, weights_ref):
+    zero = jnp.zeros((16, 16), BF16)
+    for outer in range(PART):
+        offsets = range(4 * outer, 4 * outer + 4)
+        parts = [filters_ref[d] if d < OFFSETS else zero for d in offsets]
+
+        @pl.when(place_ref[1] == 0)
+        def _():
+            weights_ref[outer] = jnp.concatenate([q for p in parts for q in (p, zero)], axis=1)
+
+        @pl.when(place_ref[1] == 1)
+        def _():
+            weights_ref[outer] = jnp.concatenate([q for p in parts for q in (zero, p)], axis=1)
+
     lane = lax.broadcasted_iota(jnp.int32, (16, 128), 1)
     for part, ref in enumerate((volume_ref, cotangent_ref)):
         whole = pltpu.roll(ref[...].astype(F32), 64, 1)
@@ -54,25 +90,6 @@
             for chunk in range(CHUNKS):
                 row = part * ROWS + chunk * 16
                 out_ref[slab, row : row + 16, :] = pieces[4 * slab + chunk]
-    for low in range(4):
-        pieces = []
-        for high in range(8):
-            d = high * 4 + low
-            pieces.append(filters_ref[d] if d < OFFSETS else jnp.zeros((16, 16), BF16))
-        block = jnp.concatenate(pieces, axis=1)
-        for slab in range(GROUPS):
-            out_ref[slab, 2 * ROWS + 16 * low : 2 * ROWS + 16 * (low + 1), :] = block
-
-
-def unpack_kernel(packed_ref, acts_ref, weights_ref):
-    acts_ref[...] = packed_ref[:, : 2 * ROWS, :]
-    for d in range(OFFSETS):
-        high, low = divmod(d, 4)
-        row = 2 * ROWS + 16 * low
-        weights_ref[d] = jnp.concatenate(
-            [packed_ref[g, row : row + 16, 16 * high : 16 * (high + 1)] for g in range(GROUPS)],
-            axis=1,
-        )
 
 
 def shifted(pieces):
@@ -89,6 +106,32 @@
 
 def weight(weights_ref, d):
     return jnp.concatenate([weights_ref[s % 4, s // 4, d] for s in range(16)], axis=0)
+
+
+def turned(value, by):
+    return jnp.concatenate([value[:, 128 - by :], value[:, : 128 - by]], axis=1)
+
+
+def assemble(place_ref, parts, held_ref, weights_ref):
+    core, y, x, zl = place_ref[0], place_ref[2], place_ref[3], place_ref[4]
+    for late, ref in enumerate(parts):
+        for early in range(4):
+            dy = jnp.where(core == 0, late, early)
+            dx = jnp.where(core == 0, early, late)
+            to_y, to_x = lax.rem(y + dy, 4), lax.rem(x + dx, 4)
+            for k in range(4):
+                held_ref[to_y, to_x, lax.rem(zl + k, 4)] = ref[early, k]
+    lane = lax.broadcasted_iota(jnp.int32, (16, 128), 1)
+    half, even = lane < 64, lane % 64 < 32
+    for s in range(16):
+        for outer in range(PART):
+            a, b, c, d = (held_ref[k, s % 4, s // 4, outer] for k in range(4))
+            a, c = jnp.where(half, a, turned(c, 64)), jnp.where(half, turned(a, 64), c)
+            b, d = jnp.where(half, b, turned(d, 64)), jnp.where(half, turned(b, 64), d)
+            weights_ref[s % 4, s // 4, 4 * outer] = jnp.where(even, a, turned(b, 32))
+            weights_ref[s % 4, s // 4, 4 * outer + 1] = jnp.where(even, turned(a, 96), b)
+            weights_ref[s % 4, s // 4, 4 * outer + 2] = jnp.where(even, c, turned(d, 32))
+            weights_ref[s % 4, s // 4, 4 * outer + 3] = jnp.where(even, turned(c, 96), d)
 
 
 def combine(before, middle, after):
@@ -98,7 +141,11 @@
     return middle + left + right
 
 
-def grad_kernel(low_ref, own_ref, high_ref, weights_ref, core_ref, keep_ref, send_ref, stack_ref, result_ref):
+def grad_kernel(
+    place_ref, low_ref, own_ref, high_ref, part_0, part_1, part_2, part_3,
+    keep_ref, send_ref, weights_ref, held_ref, stack_ref, result_ref,
+):
+    assemble(place_ref, (part_0, part_1, part_2, part_3), held_ref, weights_ref)
     for dx, ref in enumerate((high_ref, own_ref, low_ref)):
         above, same, below = shifted([block_of(ref, g, ROWS) for g in range(GROUPS)])
         for dy, value in enumerate((below, same, above)):
@@ -109,13 +156,13 @@
         left = jnp.concatenate([weight(weights_ref, k * 3 + dz) for k in range(9)], axis=1)
         terms.append(jnp.dot(left, stack_ref[...], preferred_element_type=F32))
     result_ref[...] = combine(terms[2], terms[1], terms[0]).reshape(GROUPS, 2, 16, CELLS)
-    core = core_ref[0]
+    core = place_ref[0]
     keep_ref[...] = result_ref[:, core]
     send_ref[...] = result_ref[:, 1 - core]
 
 
-def forward_kernel(low_ref, own_ref, high_ref, other_ref, weights_ref, core_ref, out_ref, stack_ref):
-    first = core_ref[0] == 0
+def forward_kernel(place_ref, low_ref, own_ref, high_ref, other_ref, weights_ref, out_ref, stack_ref):
+    first = place_ref[0] == 0
     for dx, ref in enumerate((low_ref, own_ref, high_ref)):
         pieces = []
         for g in range(GROUPS):
@@ -148,40 +195,50 @@
 
 def local(volume, filters, cotangent):
     swap = [(0, 1), (1, 0)]
-    core = lax.axis_index("core").astype(jnp.int32).reshape(1)
-    packed = run(
+    place = jnp.stack([lax.axis_index(name) for name in ("core", "zh", "y", "x", "zl")]).astype(jnp.int32)
+    smem = pl.BlockSpec(memory_space=pltpu.SMEM)
+    own, unit = call(
         pack_kernel,
-        jax.ShapeDtypeStruct((GROUPS, 2 * ROWS + 64, 128), BF16),
+        [
+            jax.ShapeDtypeStruct((GROUPS, 2 * ROWS, 128), BF16),
+            jax.ShapeDtypeStruct((PART, 16, 128), BF16),
+        ],
+    )(in_specs=[smem] + [VMEM] * 3)(
+        place,
         volume.reshape(16, 4096),
         cotangent.reshape(16, 4096),
         filters.reshape(OFFSETS, 16, 16),
     )
-    packed = lax.all_to_all(packed, ("y", "zh"), 0, 0)
-    own, weights = run(
-        unpack_kernel,
-        [
-            jax.ShapeDtypeStruct((GROUPS, 2 * ROWS, 128), BF16),
-            jax.ShapeDtypeStruct((OFFSETS, 16, 128), BF16),
-        ],
-        packed,
-    )
+    unit = unit + lax.ppermute(unit, "zh", swap)
+    own = lax.all_to_all(own, ("y", "zh"), 0, 0)
+
+    def gather(block, pairs):
+        return [block] + [lax.ppermute(block, AXES, pairs(step)) for step in (1, 2, 3)]
+
+    def line(step):
+        return pairs_of(lambda zl, x, y, zh, core: ((zl - step) % 4, x, y, zh, core))
+
+    unit = jnp.stack(gather(unit, line))
+    unit = jnp.stack(gather(unit, functools.partial(along, True)))
+    parts = gather(unit, functools.partial(along, False))
     up = [(i, i + 1) for i in range(15)]
     down = [(b, a) for a, b in up]
     low = lax.ppermute(own, SPACE, up)
     high = lax.ppermute(own, SPACE, down)
-    weights = lax.all_to_all(jnp.broadcast_to(weights, (4,) + weights.shape), "zl", 0, 0)
-    weights = lax.all_to_all(jnp.broadcast_to(weights, (4,) + weights.shape), "x", 0, 0)
     other = lax.ppermute(jnp.stack([low[:, :ROWS], own[:, :ROWS], high[:, :ROWS]]), "core", swap)
     flops = 2 * 27 * 256 * 128 * CELLS
     piece = jax.ShapeDtypeStruct((GROUPS, 16, CELLS), F32)
-    smem = pl.BlockSpec(memory_space=pltpu.SMEM)
-    keep, send = call(
+    keep, send, weights = call(
         grad_kernel,
-        [piece, piece],
+        [piece, piece, jax.ShapeDtypeStruct((4, 4, 4 * PART, 16, 128), BF16)],
         flops=flops,
         byte_count=4 << 20,
-        scratch=[pltpu.VMEM((9 * 128, CELLS), BF16), pltpu.VMEM((GROUPS, 2, 16, CELLS), F32)],
-    )(in_specs=[VMEM] * 4 + [smem])(low, own, high, weights, core)
+        scratch=[
+            pltpu.VMEM((4, 4, 4, PART, 16, 128), BF16),
+            pltpu.VMEM((9 * 128, CELLS), BF16),
+            pltpu.VMEM((GROUPS, 2, 16, CELLS), F32),
+        ],
+    )(in_specs=[smem] + [VMEM] * 7)(place, low, own, high, *parts)
     got = lax.ppermute(send, "core", swap)
     output = call(
         forward_kernel,
@@ -189,7 +246,7 @@
         flops=flops,
         byte_count=4 << 20,
         scratch=[pltpu.VMEM((9 * 256, CELLS), BF16)],
-    )(in_specs=[VMEM] * 5 + [smem])(low, own, high, other, weights, core)
+    )(in_specs=[smem] + [VMEM] * 5)(place, low, own, high, other, weights)
     merged = run(merge_kernel, jax.ShapeDtypeStruct((GROUPS, 32, CELLS), BF16), output, keep, got)
     merged = lax.all_to_all(merged, ("y", "zh"), 0, 0)
     plane = jax.ShapeDtypeStruct((16, 4096), BF16)

time: 103 us -> 90.9 us (0.88)
  blocking collectives: 59.1 us -> 16.9 us
  starting transfers between devices: 13 us -> 38.3 us
  Pallas kernels: 3.85 us -> 9.11 us
  waiting for transfers between devices: 20.5 us -> 22.5 us
  local copies, waits for them, and re-layouts: 4.24 us -> 2.83 us
    all_to_all x2 -> x0, blocking collectives: 42.1 us -> none  [the longest x1 28.2 us: local(): packed = lax.all_to_all(packed, ('y', 'zh'), 0, 0)]
    ppermute x1, waiting for transfers between devices: 20.3 us -> 0.01 us  [local(): high = lax.ppermute(own, SPACE, down)]
    ppermute x0 -> x10, starting transfers between devices: none -> 18.4 us  [the longest x9 12.5 us: gather(): lax.ppermute(block, AXES, pairs(step))]
    ppermute x0 -> x10, waiting for transfers between devices: none -> 13.3 us  [the longest x1 8.58 us: local(): unit = unit + lax.ppermute(unit, 'zh', swap)]
    ppermute x1, waiting for transfers between devices: 0.01 us -> 9.21 us  [local(): low = lax.ppermute(own, SPACE, up)]
    all_to_all x1, starting transfers between devices: 4.29 us -> 10.2 us  [local(): own = lax.all_to_all(own, ('y', 'zh'), 0, 0)]
    pallas_call x1 -> x2, Pallas kernels: 1.31 us -> 6.43 us  [the longest x1 4.49 us: local(): call(grad_kernel, [piece, piece, jax.ShapeDtypeStruct((4, 4, 4 * PART, 16...]
    broadcast_in_dim x2 -> x0, local copies, waits for them, and re-layouts: 1.51 us -> none  [local(): jnp.broadcast_to(weights, (4,) + weights.shape)]
  transfers between devices with their start and end apart: 5 -> 15, of which waited for: 2 -> 6; matrix products, arithmetic and copies ran while one was open for 1% -> 0% of each run, Pallas kernels for 3% -> 7%
where the time goes in v3:
time: 90.9 us; the launch traced here: 90.5 us
  starting transfers between devices  38.3 us (42%)
  waiting for transfers between devices  22.5 us (25%)
  blocking collectives  16.9 us (19%)
  Pallas kernels  9.11 us (10%)
  local copies, waits for them, and re-layouts  2.83 us (3%)
    all_to_all x1, blocking collectives, local(): merged = lax.all_to_all(merged, ('y', 'zh'), 0, 0)  16.9 us
    ppermute x9, starting transfers between devices, gather(): lax.ppermute(block, AXES, pairs(step))  12.5 us
    all_to_all x1, starting transfers between devices, local(): own = lax.all_to_all(own, ('y', 'zh'), 0, 0)  10.2 us
    ppermute x1, waiting for transfers between devices, local(): low = lax.ppermute(own, SPACE, up)  9.21 us
    ppermute x1, waiting for transfers between devices, local(): unit = unit + lax.ppermute(unit, 'zh', swap)  8.58 us
    ppermute x1, starting transfers between devices, local(): high = lax.ppermute(own, SPACE, down)  6.49 us
    ppermute x1, starting transfers between devices, local(): unit = unit + lax.ppermute(unit, 'zh', swap)  5.93 us
    ppermute x9, waiting for transfers between devices, gather(): lax.ppermute(block, AXES, pairs(step))  4.71 us
  transfers between devices with their start and end apart: 15, of which 6 were waited for; matrix products, arithmetic and copies ran while one was open for 0% of the time, Pallas kernels for 7%

profile of v3, /device:TPU:32, one launch (start us, length us, event | category | flops | bytes accessed | tf_op | source)
XLA Modules:
  0.0 90.5 jit_solution(1565716315876839426)
XLA Ops:
  0.6 0.1 stack.65.place_ref
  0.7 0.0 copy-start
  0.7 0.9 copy-done
  1.6 0.0 copy-start.1
  1.6 0.9 copy-done.1
  2.5 0.0 copy-start.2
  2.5 0.9 copy-done.2
  3.4 1.9 %shard_map.50 = (bf16[8,160,128]{2,1,0:T(8,128)(2,1)}, bf16[7,16,128]{2,1,0:T(8,128)(2,1)S(1)}) custom-call(s32[5]{0:T(128)S(1)} %stack.65.place_ref, bf16[16,4096]{1,0:T(8,128)(2,1)S(1)} %bitcast.25, bf16[16,4096]{1,0:T(8,128)(2,1)S(1)} %bitcast.26, bf16[27,16,16]{2,1,0:T(8,128)(2,1)S(1)} %bitcast.27), custom_call_target="tpu_custom_call" | custom-call | bytes 1048576 | tf_op jit(solution)/shard_map/pallas_call | solution.py:200
  5.4 10.2 %all-to-all-start = ((bf16[8,160,128]{2,1,0:T(8,128)(2,1)}), bf16[8,160,128]{2,1,0:T(8,128)(2,1)S(1)}, u32[]{:S(2)}, u32[]{:S(2)}) async-start(bf16[8,160,128]{2,1,0:T(8,128)(2,1)} %get-tuple-element.9), calls=%async_computation | async-start | bytes 655360 | tf_op jit(solution)/shard_map/all_to_all | solution.py:213
  15.6 5.9 %collective-permute-start.3 = (bf16[7,16,128]{2,1,0:T(8,128)(2,1)S(1)}, bf16[7,16,128]{2,1,0:T(8,128)(2,1)S(1)}, u32[]{:S(2)}, u32[]{:S(2)}) collective-permute-start(bf16[7,16,128]{2,1,0:T(8,128)(2,1)S(1)} %get-tuple-element.10), channel_id=1, source_target_pairs={{0,2},{2,0},{1,3},{3,1},{4,6},{6,4},{5,7},{7,5},{8,10},{10,8},{9,1... | collective-permute-start | bytes 86024 | tf_op jit(solution)/shard_map/ppermute | solution.py:212
  21.5 8.6 %collective-permute-done.3 = bf16[7,16,128]{2,1,0:T(8,128)(2,1)S(1)} collective-permute-done((bf16[7,16,128]{2,1,0:T(8,128)(2,1)S(1)}, bf16[7,16,128]{2,1,0:T(8,128)(2,1)S(1)}, u32[]{:S(2)}, u32[]{:S(2)}) %collective-permute-start.3) | collective-permute-done | bytes 28704 | tf_op jit(solution)/shard_map/ppermute | solution.py:212
  30.1 0.1 collective-permute-start.4
  30.2 2.4 %collective-permute-start.5 = (bf16[7,16,128]{2,1,0:T(8,128)(2,1)S(1)}, bf16[7,16,128]{2,1,0:T(8,128)(2,1)S(1)}, u32[]{:S(2)}, u32[]{:S(2)}) collective-permute-start(bf16[7,16,128]{2,1,0:T(8,128)(2,1)S(1)} %add.3), channel_id=1, source_target_pairs={{0,128},{1,129},{2,130},{3,131},{4,132},{5,133},{6,134},{7,135},{8... | collective-permute-start | bytes 86024 | tf_op jit(solution)/shard_map/ppermute | solution.py:216
  32.7 1.0 %collective-permute-start.6 = (bf16[7,16,128]{2,1,0:T(8,128)(2,1)S(1)}, bf16[7,16,128]{2,1,0:T(8,128)(2,1)S(1)}, u32[]{:S(2)}, u32[]{:S(2)}) collective-permute-start(bf16[7,16,128]{2,1,0:T(8,128)(2,1)S(1)} %add.3), channel_id=1, source_target_pairs={{0,64},{1,65},{2,66},{3,67},{4,68},{5,69},{6,70},{7,71},{8,72},{9,... | collective-permute-start | bytes 86024 | tf_op jit(solution)/shard_map/ppermute | solution.py:216
  33.6 0.4 collective-permute-done.4
  34.0 1.1 %collective-permute-done.5 = bf16[7,16,128]{2,1,0:T(8,128)(2,1)S(1)} collective-permute-done((bf16[7,16,128]{2,1,0:T(8,128)(2,1)S(1)}, bf16[7,16,128]{2,1,0:T(8,128)(2,1)S(1)}, u32[]{:S(2)}, u32[]{:S(2)}) %collective-permute-start.5) | collective-permute-done | bytes 28704 | tf_op jit(solution)/shard_map/ppermute | solution.py:216
  35.1 1.4 %collective-permute-done.6 = bf16[7,16,128]{2,1,0:T(8,128)(2,1)S(1)} collective-permute-done((bf16[7,16,128]{2,1,0:T(8,128)(2,1)S(1)}, bf16[7,16,128]{2,1,0:T(8,128)(2,1)S(1)}, u32[]{:S(2)}, u32[]{:S(2)}) %collective-permute-start.6) | collective-permute-done | bytes 28704 | tf_op jit(solution)/shard_map/ppermute | solution.py:216
  36.6 2.8 %collective-permute-start.7 = (bf16[4,7,16,128]{3,2,1,0:T(8,128)(2,1)S(1)}, bf16[4,7,16,128]{3,2,1,0:T(8,128)(2,1)S(1)}, u32[]{:S(2)}, u32[]{:S(2)}) collective-permute-start(bf16[4,7,16,128]{3,2,1,0:T(8,128)(2,1)S(1)} %get-tuple-element.17), channel_id=1, source_target_pairs={{0,48},{1,13},{2,50},{3,15},{4,52},{5,1},{6,54},{7,3},{8,56},{9,5}... | collective-permute-start | bytes 344072 | tf_op jit(solution)/shard_map/ppermute | solution.py:216
  39.4 0.8 collective-permute-start.8
  40.2 0.9 collective-permute-start.9
  41.1 0.0 all-to-all-done.own_ref
  41.1 6.5 %collective-permute-start.1 = (bf16[8,160,128]{2,1,0:T(8,128)(2,1)S(1)}, bf16[8,160,128]{2,1,0:T(8,128)(2,1)S(1)}, u32[]{:S(2)}, u32[]{:S(2)}) collective-permute-start(bf16[8,160,128]{2,1,0:T(8,128)(2,1)S(1)} %all-to-all-done.own_ref), channel_id=1, source_target_pairs={{16,0},{32,16},{48,32},{64,48},{80,64},{96,80},{112,96},{128,112},... | collective-permute-start | bytes 983048 | tf_op jit(solution)/shard_map/ppermute | solution.py:227
  47.6 0.0 collective-permute-done.7
  47.6 0.0 collective-permute-done.8
  47.6 0.0 collective-permute-done.9
  47.6 0.1 pad_maximum_fusion.1.part_0
  47.7 2.8 %collective-permute-start.10 = (bf16[4,4,7,16,128]{4,3,2,1,0:T(8,128)(2,1)S(1)}, bf16[4,4,7,16,128]{4,3,2,1,0:T(8,128)(2,1)S(1)}, u32[]{:S(2)}, u32[]{:S(2)}) collective-permute-start(bf16[4,4,7,16,128]{4,3,2,1,0:T(8,128)(2,1)S(1)} %pad_maximum_fusion.1.part_0), channel_id=1, source_target_pairs={{0,12},{1,49},{2,14},{3,51},{4,0},{5,53},{6,2},{7,55},{8,4},{9,57}... | collective-permute-start | bytes 1376264 | tf_op jit(solution)/shard_map/ppermute | solution.py:216
  50.4 0.9 collective-permute-start.11
  51.3 0.9 collective-permute-start.12
  52.1 1.9 %collective-permute-start = (bf16[8,160,128]{2,1,0:T(8,128)(2,1)S(1)}, bf16[8,160,128]{2,1,0:T(8,128)(2,1)S(1)}, u32[]{:S(2)}, u32[]{:S(2)}) collective-permute-start(bf16[8,160,128]{2,1,0:T(8,128)(2,1)S(1)} %all-to-all-done.own_ref), channel_id=1, source_target_pairs={{0,16},{16,32},{32,48},{48,64},{64,80},{80,96},{96,112},{112,128},... | collective-permute-start | bytes 983048 | tf_op jit(solution)/shard_map/ppermute | solution.py:226
  54.1 0.0 collective-permute-done.1.high_ref
  54.1 9.2 %collective-permute-done.low_ref = bf16[8,160,128]{2,1,0:T(8,128)(2,1)S(1)} collective-permute-done((bf16[8,160,128]{2,1,0:T(8,128)(2,1)S(1)}, bf16[8,160,128]{2,1,0:T(8,128)(2,1)S(1)}, u32[]{:S(2)}, u32[]{:S(2)}) %collective-permute-start) | collective-permute-done | bytes 327712 | tf_op jit(solution)/shard_map/ppermute | solution.py:226
  63.3 0.1 pad_maximum_fusion
  63.4 0.1 collective-permute-start.2
  63.5 0.0 collective-permute-done.10.part_1
  63.6 0.0 collective-permute-done.11.part_2
  63.6 1.8 %collective-permute-done.12.part_3 = bf16[4,4,7,16,128]{4,3,2,1,0:T(8,128)(2,1)S(1)} collective-permute-done((bf16[4,4,7,16,128]{4,3,2,1,0:T(8,128)(2,1)S(1)}, bf16[4,4,7,16,128]{4,3,2,1,0:T(8,128)(2,1)S(1)}, u32[]{:S(2)}, u32[]{:S(2)}) %collective-permute-start.12) | collective-permute-done | bytes 458784 | tf_op jit(solution)/shard_map/ppermute | solution.py:216
  65.3 4.5 %shard_map.51 = (f32[8,16,512]{2,1,0:T(8,128)S(1)}, f32[8,16,512]{2,1,0:T(8,128)S(1)}, bf16[4,4,28,16,128]{4,3,2,1,0:T(8,128)(2,1)S(1)}) custom-call(s32[5]{0:T(128)S(1)} %stack.65.place_ref, bf16[8,160,128]{2,1,0:T(8,128)(2,1)S(1)} %collective-permute-done.low_ref, bf16[8,160,128]{2,1,0:T(8,128)(2,1)S(1)} %all-to-all-done.own_ref, ...), custom_call_target="tpu_custom_call" | custom-call | flops 905969664 | bytes 4194304 | tf_op jit(solution)/shard_map/pallas_call | solution.py:231
  69.8 1.1 %collective-permute-start.13 = (f32[8,16,512]{2,1,0:T(8,128)S(1)}, f32[8,16,512]{2,1,0:T(8,128)S(1)}, u32[]{:S(2)}, u32[]{:S(2)}) collective-permute-start(f32[8,16,512]{2,1,0:T(8,128)S(1)} %get-tuple-element.13), channel_id=1, source_target_pairs={{0,1},{1,0},{2,3},{3,2},{4,5},{5,4},{6,7},{7,6},{8,9},{9,8},{10,11... | collective-permute-start | bytes 786440 | tf_op jit(solution)/shard_map/ppermute | solution.py:242
  71.0 0.0 collective-permute-done.2.other_ref
  71.0 1.9 %shard_map.52.output_ref = bf16[8,16,512]{2,1,0:T(8,128)(2,1)S(1)} custom-call(s32[5]{0:T(128)S(1)} %stack.65.place_ref, bf16[8,160,128]{2,1,0:T(8,128)(2,1)S(1)} %collective-permute-done.low_ref, bf16[8,160,128]{2,1,0:T(8,128)(2,1)S(1)} %all-to-all-done.own_ref, bf16[8,160,128]{2,1,0:T(8,128)(2,1)S(1)} %collective-permute-done.1.high_ref, ...), custom_call_target="tpu_custom_call" | custom-call | flops 905969664 | bytes 4194304 | tf_op jit(solution)/shard_map/pallas_call | solution.py:243
  72.9 0.0 collective-permute-done.13.got_ref
  73.0 16.9 %all_to_all.10.packed_ref = bf16[8,32,512]{2,1,0:T(8,128)(2,1)S(1)} all-to-all(bf16[8,32,512]{2,1,0:T(8,128)(2,1)S(1)} %shard_map.53), channel_id=1, replica_groups=mesh['zl'=4,'x'=4,'y'=4,'zh'=2,'core'=2] {'y','zh'}, dimensions={0} | all-to-all | bytes 524288 | tf_op jit(solution)/shard_map/all_to_all | solution.py:251
  89.8 0.7 shard_map.54
  (6 shorter events, 0.1 us)
Async XLA Ops:
  0.7 0.9 copy-start
  1.6 0.9 copy-start.1
  2.5 0.9 copy-start.2
  5.4 35.7 %all-to-all-start = ((bf16[8,160,128]{2,1,0:T(8,128)(2,1)}), bf16[8,160,128]{2,1,0:T(8,128)(2,1)S(1)}, u32[]{:S(2)}, u32[]{:S(2)}) async-start(bf16[8,160,128]{2,1,0:T(8,128)(2,1)} %get-tuple-element.9), calls=%async_computation | async-start | bytes 655360 | tf_op jit(solution)/shard_map/all_to_all | solution.py:213
  15.6 14.5 %collective-permute-start.3 = (bf16[7,16,128]{2,1,0:T(8,128)(2,1)S(1)}, bf16[7,16,128]{2,1,0:T(8,128)(2,1)S(1)}, u32[]{:S(2)}, u32[]{:S(2)}) collective-permute-start(bf16[7,16,128]{2,1,0:T(8,128)(2,1)S(1)} %get-tuple-element.10), channel_id=1, source_target_pairs={{0,2},{2,0},{1,3},{3,1},{4,6},{6,4},{5,7},{7,5},{8,10},{10,8},{9,1... | collective-permute-start | bytes 86024 | tf_op jit(solution)/shard_map/ppermute | solution.py:212
  30.1 3.9 %collective-permute-start.4 = (bf16[7,16,128]{2,1,0:T(8,128)(2,1)S(1)}, bf16[7,16,128]{2,1,0:T(8,128)(2,1)S(1)}, u32[]{:S(2)}, u32[]{:S(2)}) collective-permute-start(bf16[7,16,128]{2,1,0:T(8,128)(2,1)S(1)} %add.3), channel_id=1, source_target_pairs={{0,192},{1,193},{2,194},{3,195},{4,196},{5,197},{6,198},{7,199},{8... | collective-permute-start | bytes 86024 | tf_op jit(solution)/shard_map/ppermute | solution.py:216
  30.2 4.9 %collective-permute-start.5 = (bf16[7,16,128]{2,1,0:T(8,128)(2,1)S(1)}, bf16[7,16,128]{2,1,0:T(8,128)(2,1)S(1)}, u32[]{:S(2)}, u32[]{:S(2)}) collective-permute-start(bf16[7,16,128]{2,1,0:T(8,128)(2,1)S(1)} %add.3), channel_id=1, source_target_pairs={{0,128},{1,129},{2,130},{3,131},{4,132},{5,133},{6,134},{7,135},{8... | collective-permute-start | bytes 86024 | tf_op jit(solution)/shard_map/ppermute | solution.py:216
  32.7 3.9 %collective-permute-start.6 = (bf16[7,16,128]{2,1,0:T(8,128)(2,1)S(1)}, bf16[7,16,128]{2,1,0:T(8,128)(2,1)S(1)}, u32[]{:S(2)}, u32[]{:S(2)}) collective-permute-start(bf16[7,16,128]{2,1,0:T(8,128)(2,1)S(1)} %add.3), channel_id=1, source_target_pairs={{0,64},{1,65},{2,66},{3,67},{4,68},{5,69},{6,70},{7,71},{8,72},{9,... | collective-permute-start | bytes 86024 | tf_op jit(solution)/shard_map/ppermute | solution.py:216
  36.6 11.0 %collective-permute-start.7 = (bf16[4,7,16,128]{3,2,1,0:T(8,128)(2,1)S(1)}, bf16[4,7,16,128]{3,2,1,0:T(8,128)(2,1)S(1)}, u32[]{:S(2)}, u32[]{:S(2)}) collective-permute-start(bf16[4,7,16,128]{3,2,1,0:T(8,128)(2,1)S(1)} %get-tuple-element.17), channel_id=1, source_target_pairs={{0,48},{1,13},{2,50},{3,15},{4,52},{5,1},{6,54},{7,3},{8,56},{9,5}... | collective-permute-start | bytes 344072 | tf_op jit(solution)/shard_map/ppermute | solution.py:216
  39.4 8.2 %collective-permute-start.8 = (bf16[4,7,16,128]{3,2,1,0:T(8,128)(2,1)S(1)}, bf16[4,7,16,128]{3,2,1,0:T(8,128)(2,1)S(1)}, u32[]{:S(2)}, u32[]{:S(2)}) collective-permute-start(bf16[4,7,16,128]{3,2,1,0:T(8,128)(2,1)S(1)} %get-tuple-element.17), channel_id=1, source_target_pairs={{0,32},{1,9},{2,34},{3,11},{4,36},{5,13},{6,38},{7,15},{8,40},{9,1... | collective-permute-start | bytes 344072 | tf_op jit(solution)/shard_map/ppermute | solution.py:216
  40.2 7.4 %collective-permute-start.9 = (bf16[4,7,16,128]{3,2,1,0:T(8,128)(2,1)S(1)}, bf16[4,7,16,128]{3,2,1,0:T(8,128)(2,1)S(1)}, u32[]{:S(2)}, u32[]{:S(2)}) collective-permute-start(bf16[4,7,16,128]{3,2,1,0:T(8,128)(2,1)S(1)} %get-tuple-element.17), channel_id=1, source_target_pairs={{0,16},{1,5},{2,18},{3,7},{4,20},{5,9},{6,22},{7,11},{8,24},{9,13}... | collective-permute-start | bytes 344072 | tf_op jit(solution)/shard_map/ppermute | solution.py:216
  41.1 13.0 %collective-permute-start.1 = (bf16[8,160,128]{2,1,0:T(8,128)(2,1)S(1)}, bf16[8,160,128]{2,1,0:T(8,128)(2,1)S(1)}, u32[]{:S(2)}, u32[]{:S(2)}) collective-permute-start(bf16[8,160,128]{2,1,0:T(8,128)(2,1)S(1)} %all-to-all-done.own_ref), channel_id=1, source_target_pairs={{16,0},{32,16},{48,32},{64,48},{80,64},{96,80},{112,96},{128,112},... | collective-permute-start | bytes 983048 | tf_op jit(solution)/shard_map/ppermute | solution.py:227
  47.7 15.9 %collective-permute-start.10 = (bf16[4,4,7,16,128]{4,3,2,1,0:T(8,128)(2,1)S(1)}, bf16[4,4,7,16,128]{4,3,2,1,0:T(8,128)(2,1)S(1)}, u32[]{:S(2)}, u32[]{:S(2)}) collective-permute-start(bf16[4,4,7,16,128]{4,3,2,1,0:T(8,128)(2,1)S(1)} %pad_maximum_fusion.1.part_0), channel_id=1, source_target_pairs={{0,12},{1,49},{2,14},{3,51},{4,0},{5,53},{6,2},{7,55},{8,4},{9,57}... | collective-permute-start | bytes 1376264 | tf_op jit(solution)/shard_map/ppermute | solution.py:216
  50.4 13.1 %collective-permute-start.11 = (bf16[4,4,7,16,128]{4,3,2,1,0:T(8,128)(2,1)S(1)}, bf16[4,4,7,16,128]{4,3,2,1,0:T(8,128)(2,1)S(1)}, u32[]{:S(2)}, u32[]{:S(2)}) collective-permute-start(bf16[4,4,7,16,128]{4,3,2,1,0:T(8,128)(2,1)S(1)} %pad_maximum_fusion.1.part_0), channel_id=1, source_target_pairs={{0,8},{1,33},{2,10},{3,35},{4,12},{5,37},{6,14},{7,39},{8,0},{9,41... | collective-permute-start | bytes 1376264 | tf_op jit(solution)/shard_map/ppermute | solution.py:216
  51.3 14.0 %collective-permute-start.12 = (bf16[4,4,7,16,128]{4,3,2,1,0:T(8,128)(2,1)S(1)}, bf16[4,4,7,16,128]{4,3,2,1,0:T(8,128)(2,1)S(1)}, u32[]{:S(2)}, u32[]{:S(2)}) collective-permute-start(bf16[4,4,7,16,128]{4,3,2,1,0:T(8,128)(2,1)S(1)} %pad_maximum_fusion.1.part_0), channel_id=1, source_target_pairs={{0,4},{1,17},{2,6},{3,19},{4,8},{5,21},{6,10},{7,23},{8,12},{9,25}... | collective-permute-start | bytes 1376264 | tf_op jit(solution)/shard_map/ppermute | solution.py:216
  52.1 11.2 %collective-permute-start = (bf16[8,160,128]{2,1,0:T(8,128)(2,1)S(1)}, bf16[8,160,128]{2,1,0:T(8,128)(2,1)S(1)}, u32[]{:S(2)}, u32[]{:S(2)}) collective-permute-start(bf16[8,160,128]{2,1,0:T(8,128)(2,1)S(1)} %all-to-all-done.own_ref), channel_id=1, source_target_pairs={{0,16},{16,32},{32,48},{48,64},{64,80},{80,96},{96,112},{112,128},... | collective-permute-start | bytes 983048 | tf_op jit(solution)/shard_map/ppermute | solution.py:226
  63.4 7.6 %collective-permute-start.2 = (bf16[3,8,80,128]{3,2,1,0:T(8,128)(2,1)S(1)}, bf16[3,8,80,128]{3,2,1,0:T(8,128)(2,1)S(1)}, u32[]{:S(2)}, u32[]{:S(2)}) collective-permute-start(bf16[3,8,80,128]{3,2,1,0:T(8,128)(2,1)S(1)} %pad_maximum_fusion), channel_id=1, source_target_pairs={{0,1},{1,0},{2,3},{3,2},{4,5},{5,4},{6,7},{7,6},{8,9},{9,8},{10,11... | collective-permute-start | bytes 1474568 | tf_op jit(solution)/shard_map/ppermute | solution.py:228
  69.8 3.1 %collective-permute-start.13 = (f32[8,16,512]{2,1,0:T(8,128)S(1)}, f32[8,16,512]{2,1,0:T(8,128)S(1)}, u32[]{:S(2)}, u32[]{:S(2)}) collective-permute-start(f32[8,16,512]{2,1,0:T(8,128)S(1)} %get-tuple-element.13), channel_id=1, source_target_pairs={{0,1},{1,0},{2,3},{3,2},{4,5},{5,4},{6,7},{7,6},{8,9},{9,8},{10,11... | collective-permute-start | bytes 786440 | tf_op jit(solution)/shard_map/ppermute | solution.py:242

commit v4 on v3

--- a/solution.py
+++ b/solution.py
@@ -64,20 +64,26 @@
     return call(kernel, out_shape, **options)(in_specs=[VMEM] * len(args))(*args)
 
 
-def pack_kernel(place_ref, volume_ref, cotangent_ref, filters_ref, out_ref, weights_ref):
+def pack_filters_kernel(filters_ref, out_ref):
     zero = jnp.zeros((16, 16), BF16)
-    for outer in range(PART):
-        offsets = range(4 * outer, 4 * outer + 4)
-        parts = [filters_ref[d] if d < OFFSETS else zero for d in offsets]
-
-        @pl.when(place_ref[1] == 0)
-        def _():
-            weights_ref[outer] = jnp.concatenate([q for p in parts for q in (p, zero)], axis=1)
-
-        @pl.when(place_ref[1] == 1)
-        def _():
-            weights_ref[outer] = jnp.concatenate([q for p in parts for q in (zero, p)], axis=1)
-
+    for outer in range(4):
+        offsets = range(8 * outer, 8 * outer + 8)
+        block = jnp.concatenate([filters_ref[d] if d < OFFSETS else zero for d in offsets], axis=1)
+        for copy in range(8):
+            out_ref[copy, outer] = block
+
+
+def regroup_kernel(packed_ref, out_ref):
+    for zl in range(4):
+        for outer in range(PART):
+            pieces = []
+            for d in range(4 * outer, 4 * outer + 4):
+                lane = 16 * (d % 8)
+                pieces += [packed_ref[2 * zl + zh, d // 8, :, lane : lane + 16] for zh in range(2)]
+            out_ref[zl, outer] = jnp.concatenate(pieces, axis=1)
+
+
+def pack_kernel(volume_ref, cotangent_ref, out_ref):
     lane = lax.broadcasted_iota(jnp.int32, (16, 128), 1)
     for part, ref in enumerate((volume_ref, cotangent_ref)):
         whole = pltpu.roll(ref[...].astype(F32), 64, 1)
@@ -112,15 +118,13 @@
     return jnp.concatenate([value[:, 128 - by :], value[:, : 128 - by]], axis=1)
 
 
-def assemble(place_ref, parts, held_ref, weights_ref):
-    core, y, x, zl = place_ref[0], place_ref[2], place_ref[3], place_ref[4]
-    for late, ref in enumerate(parts):
+def assemble_kernel(part_0, part_1, part_2, part_3, weights_ref, held_ref):
+    core, y, x = (lax.axis_index(name) for name in ("core", "y", "x"))
+    for late, ref in enumerate((part_0, part_1, part_2, part_3)):
         for early in range(4):
             dy = jnp.where(core == 0, late, early)
             dx = jnp.where(core == 0, early, late)
-            to_y, to_x = lax.rem(y + dy, 4), lax.rem(x + dx, 4)
-            for k in range(4):
-                held_ref[to_y, to_x, lax.rem(zl + k, 4)] = ref[early, k]
+            held_ref[lax.rem(y + dy, 4), lax.rem(x + dx, 4)] = ref[early]
     lane = lax.broadcasted_iota(jnp.int32, (16, 128), 1)
     half, even = lane < 64, lane % 64 < 32
     for s in range(16):
@@ -141,11 +145,7 @@
     return middle + left + right
 
 
-def grad_kernel(
-    place_ref, low_ref, own_ref, high_ref, part_0, part_1, part_2, part_3,
-    keep_ref, send_ref, weights_ref, held_ref, stack_ref, result_ref,
-):
-    assemble(place_ref, (part_0, part_1, part_2, part_3), held_ref, weights_ref)
+def grad_kernel(low_ref, own_ref, high_ref, weights_ref, keep_ref, send_ref, stack_ref, result_ref):
     for dx, ref in enumerate((high_ref, own_ref, low_ref)):
         above, same, below = shifted([block_of(ref, g, ROWS) for g in range(GROUPS)])
         for dy, value in enumerate((below, same, above)):
@@ -156,13 +156,13 @@
         left = jnp.concatenate([weight(weights_ref, k * 3 + dz) for k in range(9)], axis=1)
         terms.append(jnp.dot(left, stack_ref[...], preferred_element_type=F32))
     result_ref[...] = combine(terms[2], terms[1], terms[0]).reshape(GROUPS, 2, 16, CELLS)
-    core = place_ref[0]
+    core = lax.axis_index("core")
     keep_ref[...] = result_ref[:, core]
     send_ref[...] = result_ref[:, 1 - core]
 
 
-def forward_kernel(place_ref, low_ref, own_ref, high_ref, other_ref, weights_ref, out_ref, stack_ref):
-    first = place_ref[0] == 0
+def forward_kernel(low_ref, own_ref, high_ref, other_ref, weights_ref, out_ref, stack_ref):
+    first = lax.axis_index("core") == 0
     for dx, ref in enumerate((low_ref, own_ref, high_ref)):
         pieces = []
         for g in range(GROUPS):
@@ -195,31 +195,27 @@
 
 def local(volume, filters, cotangent):
     swap = [(0, 1), (1, 0)]
-    place = jnp.stack([lax.axis_index(name) for name in ("core", "zh", "y", "x", "zl")]).astype(jnp.int32)
-    smem = pl.BlockSpec(memory_space=pltpu.SMEM)
-    own, unit = call(
+    packed = run(
+        pack_filters_kernel,
+        jax.ShapeDtypeStruct((8, 4, 16, 128), BF16),
+        filters.reshape(OFFSETS, 16, 16),
+    )
+    packed = lax.all_to_all(packed, ("zl", "zh"), 0, 0)
+    own = run(
         pack_kernel,
-        [
-            jax.ShapeDtypeStruct((GROUPS, 2 * ROWS, 128), BF16),
-            jax.ShapeDtypeStruct((PART, 16, 128), BF16),
-        ],
-    )(in_specs=[smem] + [VMEM] * 3)(
-        place,
+        jax.ShapeDtypeStruct((GROUPS, 2 * ROWS, 128), BF16),
         volume.reshape(16, 4096),
         cotangent.reshape(16, 4096),
-        filters.reshape(OFFSETS, 16, 16),
-    )
-    unit = unit + lax.ppermute(unit, "zh", swap)
+    )
+    own, packed = lax.optimization_barrier((own, packed))
     own = lax.all_to_all(own, ("y", "zh"), 0, 0)
+    unit = run(regroup_kernel, jax.ShapeDtypeStruct((4, PART, 16, 128), BF16), packed)
 
     def gather(block, pairs):
         return [block] + [lax.ppermute(block, AXES, pairs(step)) for step in (1, 2, 3)]
 
-    def line(step):
-        return pairs_of(lambda zl, x, y, zh, core: ((zl - step) % 4, x, y, zh, core))
-
-    unit = jnp.stack(gather(unit, line))
     unit = jnp.stack(gather(unit, functools.partial(along, True)))
+    own, _ = lax.optimization_barrier((own, unit))
     parts = gather(unit, functools.partial(along, False))
     up = [(i, i + 1) for i in range(15)]
     down = [(b, a) for a, b in up]
@@ -228,25 +224,37 @@
     other = lax.ppermute(jnp.stack([low[:, :ROWS], own[:, :ROWS], high[:, :ROWS]]), "core", swap)
     flops = 2 * 27 * 256 * 128 * CELLS
     piece = jax.ShapeDtypeStruct((GROUPS, 16, CELLS), F32)
-    keep, send, weights = call(
+    weights = run(
+        assemble_kernel,
+        jax.ShapeDtypeStruct((4, 4, 4 * PART, 16, 128), BF16),
+        *parts,
+        byte_count=8 << 20,
+        scratch=[pltpu.VMEM((4, 4, 4, PART, 16, 128), BF16)],
+    )
+    keep, send = run(
         grad_kernel,
-        [piece, piece, jax.ShapeDtypeStruct((4, 4, 4 * PART, 16, 128), BF16)],
+        [piece, piece],
+        low,
+        own,
+        high,
+        weights,
         flops=flops,
         byte_count=4 << 20,
-        scratch=[
-            pltpu.VMEM((4, 4, 4, PART, 16, 128), BF16),
-            pltpu.VMEM((9 * 128, CELLS), BF16),
-            pltpu.VMEM((GROUPS, 2, 16, CELLS), F32),
-        ],
-    )(in_specs=[smem] + [VMEM] * 7)(place, low, own, high, *parts)
+        scratch=[pltpu.VMEM((9 * 128, CELLS), BF16), pltpu.VMEM((GROUPS, 2, 16, CELLS), F32)],
+    )
     got = lax.ppermute(send, "core", swap)
-    output = call(
+    output = run(
         forward_kernel,
         jax.ShapeDtypeStruct((GROUPS, 16, CELLS), BF16),
+        low,
+        own,
+        high,
+        other,
+        weights,
         flops=flops,
         byte_count=4 << 20,
         scratch=[pltpu.VMEM((9 * 256, CELLS), BF16)],
-    )(in_specs=[smem] + [VMEM] * 5)(place, low, own, high, other, weights)
+    )
     merged = run(merge_kernel, jax.ShapeDtypeStruct((GROUPS, 32, CELLS), BF16), output, keep, got)
     merged = lax.all_to_all(merged, ("y", "zh"), 0, 0)
     plane = jax.ShapeDtypeStruct((16, 4096), BF16)

time: 90.9 us -> 91.5 us (level)
  starting transfers between devices: 38.3 us -> 31.5 us
  Pallas kernels: 9.11 us -> 12.8 us
  blocking collectives: 16.9 us -> 20.2 us
    pallas_call x2 -> x8, Pallas kernels: 0.75 us -> 12.8 us  [run(): call(kernel, out_shape, **options)(in_specs=[VMEM] * len(args))(*args)]
    ppermute x1 -> x0, waiting for transfers between devices: 8.58 us -> none  [local(): unit = unit + lax.ppermute(unit, 'zh', swap)]
    all_to_all x0 -> x1, starting transfers between devices: none -> 8.57 us  [local(): packed = lax.all_to_all(packed, ('zl', 'zh'), 0, 0)]
    pallas_call x3 -> x0, Pallas kernels: 8.36 us -> none  [the longest x1 4.49 us: local(): call(grad_kernel, [piece, piece, jax.ShapeDtypeStruct((4, 4, 4 * PART, 16...]
    ppermute x1 -> x0, starting transfers between devices: 5.93 us -> none  [local(): unit = unit + lax.ppermute(unit, 'zh', swap)]
    all_to_all x0 -> x1, waiting for transfers between devices: none -> 4.77 us  [local(): packed = lax.all_to_all(packed, ('zl', 'zh'), 0, 0)]
    all_to_all x1, starting transfers between devices: 10.2 us -> 5.53 us  [local(): own = lax.all_to_all(own, ('y', 'zh'), 0, 0)]
    all_to_all x1, blocking collectives: 16.9 us -> 20.2 us  [local(): merged = lax.all_to_all(merged, ('y', 'zh'), 0, 0)]
  transfers between devices with their start and end apart: 15 -> 12, of which waited for: 6 -> 8; matrix products, arithmetic and copies ran while one was open for 0% -> 0% of each run, Pallas kernels for 7% -> 12%
where the time goes in v4:
time: 91.5 us; the launch traced here: 91.1 us
  starting transfers between devices  31.5 us (34%)
  waiting for transfers between devices  23 us (25%)
  blocking collectives  20.2 us (22%)
  Pallas kernels  12.8 us (14%)
  local copies, waits for them, and re-layouts  2.73 us (3%)
    all_to_all x1, blocking collectives, local(): merged = lax.all_to_all(merged, ('y', 'zh'), 0, 0)  20.2 us
    pallas_call x8, Pallas kernels, run(): call(kernel, out_shape, **options)(in_specs=[VMEM] * len(args))(*args)  12.8 us
    ppermute x6, starting transfers between devices, gather(): lax.ppermute(block, AXES, pairs(step))  9.13 us
    all_to_all x1, starting transfers between devices, local(): packed = lax.all_to_all(packed, ('zl', 'zh'), 0, 0)  8.57 us
    ppermute x6, waiting for transfers between devices, gather(): lax.ppermute(block, AXES, pairs(step))  7.08 us
    ppermute x1, waiting for transfers between devices, local(): low = lax.ppermute(own, SPACE, up)  6.68 us
    all_to_all x1, starting transfers between devices, local(): own = lax.all_to_all(own, ('y', 'zh'), 0, 0)  5.53 us
    all_to_all x1, waiting for transfers between devices, local(): packed = lax.all_to_all(packed, ('zl', 'zh'), 0, 0)  4.77 us
  transfers between devices with their start and end apart: 12, of which 8 were waited for; matrix products, arithmetic and copies ran while one was open for 0% of the time, Pallas kernels for 12%

profile of v4, /device:TPU:32, one launch (start us, length us, event | category | flops | bytes accessed | tf_op | source)
XLA Modules:
  0.0 91.1 jit_solution(4099023565702553032)
XLA Ops:
  0.6 0.0 copy-start.2
  0.6 0.9 copy-done.2
  1.5 0.8 shard_map.51
  2.3 8.6 %all-to-all-start = ((bf16[8,4,16,128]{3,2,1,0:T(8,128)(2,1)}), bf16[8,4,16,128]{3,2,1,0:T(8,128)(2,1)S(1)}, u32[]{:S(2)}, u32[]{:S(2)}) async-start(bf16[8,4,16,128]{3,2,1,0:T(8,128)(2,1)} %shard_map.51), calls=%async_computation | async-start | bytes 262144 | tf_op jit(solution)/shard_map/all_to_all | solution.py:203
  10.9 0.0 copy-start
  10.9 0.9 copy-done
  11.8 0.0 copy-start.1
  11.8 0.9 copy-done.1
  12.7 0.9 shard_map.50
  13.5 4.8 %all-to-all-done.packed_ref = bf16[8,4,16,128]{3,2,1,0:T(8,128)(2,1)S(1)} async-done(((bf16[8,4,16,128]{3,2,1,0:T(8,128)(2,1)}), bf16[8,4,16,128]{3,2,1,0:T(8,128)(2,1)S(1)}, u32[]{:S(2)}, u32[]{:S(2)}) %all-to-all-start) | async-done | bytes 131104 | tf_op jit(solution)/shard_map/all_to_all | solution.py:203
  18.3 5.5 %all-to-all-start.1 = ((bf16[8,160,128]{2,1,0:T(8,128)(2,1)}), bf16[8,160,128]{2,1,0:T(8,128)(2,1)S(1)}, u32[]{:S(2)}, u32[]{:S(2)}) async-start(bf16[8,160,128]{2,1,0:T(8,128)(2,1)} %shard_map.50), calls=%async_computation.1 | async-start | bytes 655360 | tf_op jit(solution)/shard_map/all_to_all | solution.py:211
  23.8 0.3 shard_map.52
  24.1 2.8 %collective-permute-start = (bf16[4,7,16,128]{3,2,1,0:T(8,128)(2,1)S(1)}, bf16[4,7,16,128]{3,2,1,0:T(8,128)(2,1)S(1)}, u32[]{:S(2)}, u32[]{:S(2)}) collective-permute-start(bf16[4,7,16,128]{3,2,1,0:T(8,128)(2,1)S(1)} %shard_map.52), channel_id=1, source_target_pairs={{0,48},{1,13},{2,50},{3,15},{4,52},{5,1},{6,54},{7,3},{8,56},{9,5}... | collective-permute-start | bytes 344072 | tf_op jit(solution)/shard_map/ppermute | solution.py:215
  26.9 0.8 collective-permute-start.1
  27.7 0.9 collective-permute-start.2
  28.6 0.7 collective-permute-done
  29.4 4.0 %collective-permute-done.1 = bf16[4,7,16,128]{3,2,1,0:T(8,128)(2,1)S(1)} collective-permute-done((bf16[4,7,16,128]{3,2,1,0:T(8,128)(2,1)S(1)}, bf16[4,7,16,128]{3,2,1,0:T(8,128)(2,1)S(1)}, u32[]{:S(2)}, u32[]{:S(2)}) %collective-permute-start.1) | collective-permute-done | bytes 114720 | tf_op jit(solution)/shard_map/ppermute | solution.py:215
  33.3 1.2 %collective-permute-done.2 = bf16[4,7,16,128]{3,2,1,0:T(8,128)(2,1)S(1)} collective-permute-done((bf16[4,7,16,128]{3,2,1,0:T(8,128)(2,1)S(1)}, bf16[4,7,16,128]{3,2,1,0:T(8,128)(2,1)S(1)}, u32[]{:S(2)}, u32[]{:S(2)}) %collective-permute-start.2) | collective-permute-done | bytes 114720 | tf_op jit(solution)/shard_map/ppermute | solution.py:215
  34.5 0.1 pad_maximum_fusion.1.part_0
  34.5 2.0 %all-to-all-done.1.own_ref = bf16[8,160,128]{2,1,0:T(8,128)(2,1)S(1)} async-done(((bf16[8,160,128]{2,1,0:T(8,128)(2,1)}), bf16[8,160,128]{2,1,0:T(8,128)(2,1)S(1)}, u32[]{:S(2)}, u32[]{:S(2)}) %all-to-all-start.1) | async-done | bytes 327712 | tf_op jit(solution)/shard_map/all_to_all | solution.py:211
  36.5 3.5 %collective-permute-start.4 = (bf16[8,160,128]{2,1,0:T(8,128)(2,1)S(1)}, bf16[8,160,128]{2,1,0:T(8,128)(2,1)S(1)}, u32[]{:S(2)}, u32[]{:S(2)}) collective-permute-start(bf16[8,160,128]{2,1,0:T(8,128)(2,1)S(1)} %all-to-all-done.1.own_ref), channel_id=1, source_target_pairs={{16,0},{32,16},{48,32},{64,48},{80,64},{96,80},{112,96},{128,112},... | collective-permute-start | bytes 983048 | tf_op jit(solution)/shard_map/ppermute | solution.py:223
  40.0 3.3 %collective-permute-start.6 = (bf16[4,4,7,16,128]{4,3,2,1,0:T(8,128)(2,1)S(1)}, bf16[4,4,7,16,128]{4,3,2,1,0:T(8,128)(2,1)S(1)}, u32[]{:S(2)}, u32[]{:S(2)}) collective-permute-start(bf16[4,4,7,16,128]{4,3,2,1,0:T(8,128)(2,1)S(1)} %pad_maximum_fusion.1.part_0), channel_id=1, source_target_pairs={{0,12},{1,49},{2,14},{3,51},{4,0},{5,53},{6,2},{7,55},{8,4},{9,57}... | collective-permute-start | bytes 1376264 | tf_op jit(solution)/shard_map/ppermute | solution.py:215
  43.3 1.3 %collective-permute-start.7 = (bf16[4,4,7,16,128]{4,3,2,1,0:T(8,128)(2,1)S(1)}, bf16[4,4,7,16,128]{4,3,2,1,0:T(8,128)(2,1)S(1)}, u32[]{:S(2)}, u32[]{:S(2)}) collective-permute-start(bf16[4,4,7,16,128]{4,3,2,1,0:T(8,128)(2,1)S(1)} %pad_maximum_fusion.1.part_0), channel_id=1, source_target_pairs={{0,8},{1,33},{2,10},{3,35},{4,12},{5,37},{6,14},{7,39},{8,0},{9,41... | collective-permute-start | bytes 1376264 | tf_op jit(solution)/shard_map/ppermute | solution.py:215
  44.6 0.0 collective-permute-start.8
  44.6 1.9 %collective-permute-start.3 = (bf16[8,160,128]{2,1,0:T(8,128)(2,1)S(1)}, bf16[8,160,128]{2,1,0:T(8,128)(2,1)S(1)}, u32[]{:S(2)}, u32[]{:S(2)}) collective-permute-start(bf16[8,160,128]{2,1,0:T(8,128)(2,1)S(1)} %all-to-all-done.1.own_ref), channel_id=1, source_target_pairs={{0,16},{16,32},{32,48},{48,64},{64,80},{80,96},{96,112},{112,128},... | collective-permute-start | bytes 983048 | tf_op jit(solution)/shard_map/ppermute | solution.py:222
  46.5 2.5 %collective-permute-done.4.high_ref = bf16[8,160,128]{2,1,0:T(8,128)(2,1)S(1)} collective-permute-done((bf16[8,160,128]{2,1,0:T(8,128)(2,1)S(1)}, bf16[8,160,128]{2,1,0:T(8,128)(2,1)S(1)}, u32[]{:S(2)}, u32[]{:S(2)}) %collective-permute-start.4) | collective-permute-done | bytes 327712 | tf_op jit(solution)/shard_map/ppermute | solution.py:223
  49.0 6.7 %collective-permute-done.3.low_ref = bf16[8,160,128]{2,1,0:T(8,128)(2,1)S(1)} collective-permute-done((bf16[8,160,128]{2,1,0:T(8,128)(2,1)S(1)}, bf16[8,160,128]{2,1,0:T(8,128)(2,1)S(1)}, u32[]{:S(2)}, u32[]{:S(2)}) %collective-permute-start.3) | collective-permute-done | bytes 327712 | tf_op jit(solution)/shard_map/ppermute | solution.py:222
  55.7 0.1 pad_maximum_fusion
  55.8 1.1 %collective-permute-start.5 = (bf16[3,8,80,128]{3,2,1,0:T(8,128)(2,1)S(1)}, bf16[3,8,80,128]{3,2,1,0:T(8,128)(2,1)S(1)}, u32[]{:S(2)}, u32[]{:S(2)}) collective-permute-start(bf16[3,8,80,128]{3,2,1,0:T(8,128)(2,1)S(1)} %pad_maximum_fusion), channel_id=1, source_target_pairs={{0,1},{1,0},{2,3},{3,2},{4,5},{5,4},{6,7},{7,6},{8,9},{9,8},{10,11... | collective-permute-start | bytes 1474568 | tf_op jit(solution)/shard_map/ppermute | solution.py:224
  56.9 0.0 collective-permute-done.6.part_1
  56.9 0.0 collective-permute-done.7.part_2
  56.9 1.2 %collective-permute-done.8.part_3 = bf16[4,4,7,16,128]{4,3,2,1,0:T(8,128)(2,1)S(1)} collective-permute-done((bf16[4,4,7,16,128]{4,3,2,1,0:T(8,128)(2,1)S(1)}, bf16[4,4,7,16,128]{4,3,2,1,0:T(8,128)(2,1)S(1)}, u32[]{:S(2)}, u32[]{:S(2)}) %collective-permute-start.8) | collective-permute-done | bytes 458784 | tf_op jit(solution)/shard_map/ppermute | solution.py:215
  58.2 7.4 %shard_map.53.weights_ref = bf16[4,4,28,16,128]{4,3,2,1,0:T(8,128)(2,1)S(1)} custom-call(bf16[4,4,7,16,128]{4,3,2,1,0:T(8,128)(2,1)S(1)} %pad_maximum_fusion.1.part_0, bf16[4,4,7,16,128]{4,3,2,1,0:T(8,128)(2,1)S(1)} %collective-permute-done.6.part_1, bf16[4,4,7,16,128]{4,3,2,1,0:T(8,128)(2,1)S(1)} %collective-permute-done.7.part_2, ...), custom_call_target="tpu_custom_call" | custom-call | bytes 8388608 | tf_op jit(solution)/shard_map/pallas_call | solution.py:64
  65.6 1.4 %shard_map.55 = (f32[8,16,512]{2,1,0:T(8,128)S(1)}, f32[8,16,512]{2,1,0:T(8,128)S(1)}) custom-call(bf16[8,160,128]{2,1,0:T(8,128)(2,1)S(1)} %collective-permute-done.3.low_ref, bf16[8,160,128]{2,1,0:T(8,128)(2,1)S(1)} %all-to-all-done.1.own_ref, bf16[8,160,128]{2,1,0:T(8,128)(2,1)S(1)} %collective-permute-done.4.high_ref, ...), custom_call_target="tpu_custom_call" | custom-call | flops 905969664 | bytes 4194304 | tf_op jit(solution)/shard_map/pallas_call | solution.py:64
  67.0 1.7 %collective-permute-start.9 = (f32[8,16,512]{2,1,0:T(8,128)S(1)}, f32[8,16,512]{2,1,0:T(8,128)S(1)}, u32[]{:S(2)}, u32[]{:S(2)}) collective-permute-start(f32[8,16,512]{2,1,0:T(8,128)S(1)} %get-tuple-element.13), channel_id=1, source_target_pairs={{0,1},{1,0},{2,3},{3,2},{4,5},{5,4},{6,7},{7,6},{8,9},{9,8},{10,11... | collective-permute-start | bytes 786440 | tf_op jit(solution)/shard_map/ppermute | solution.py:245
  68.7 0.0 collective-permute-done.5.other_ref
  68.8 1.4 %shard_map.54.output_ref = bf16[8,16,512]{2,1,0:T(8,128)(2,1)S(1)} custom-call(bf16[8,160,128]{2,1,0:T(8,128)(2,1)S(1)} %collective-permute-done.3.low_ref, bf16[8,160,128]{2,1,0:T(8,128)(2,1)S(1)} %all-to-all-done.1.own_ref, bf16[8,160,128]{2,1,0:T(8,128)(2,1)S(1)} %collective-permute-done.4.high_ref, ...), custom_call_target="tpu_custom_call" | custom-call | flops 905969664 | bytes 4194304 | tf_op jit(solution)/shard_map/pallas_call | solution.py:64
  70.1 0.0 collective-permute-done.9.got_ref
  70.2 20.2 %all_to_all.15.packed_ref = bf16[8,32,512]{2,1,0:T(8,128)(2,1)S(1)} all-to-all(bf16[8,32,512]{2,1,0:T(8,128)(2,1)S(1)} %shard_map.56), channel_id=1, replica_groups=mesh['zl'=4,'x'=4,'y'=4,'zh'=2,'core'=2] {'y','zh'}, dimensions={0} | all-to-all | bytes 524288 | tf_op jit(solution)/shard_map/all_to_all | solution.py:259
  90.4 0.7 shard_map.57
  (4 shorter events, 0.1 us)
Async XLA Ops:
  0.6 0.9 copy-start.2
  2.3 16.0 %all-to-all-start = ((bf16[8,4,16,128]{3,2,1,0:T(8,128)(2,1)}), bf16[8,4,16,128]{3,2,1,0:T(8,128)(2,1)S(1)}, u32[]{:S(2)}, u32[]{:S(2)}) async-start(bf16[8,4,16,128]{3,2,1,0:T(8,128)(2,1)} %shard_map.51), calls=%async_computation | async-start | bytes 262144 | tf_op jit(solution)/shard_map/all_to_all | solution.py:203
  10.9 0.9 copy-start
  11.8 0.9 copy-start.1
  18.3 18.2 %all-to-all-start.1 = ((bf16[8,160,128]{2,1,0:T(8,128)(2,1)}), bf16[8,160,128]{2,1,0:T(8,128)(2,1)S(1)}, u32[]{:S(2)}, u32[]{:S(2)}) async-start(bf16[8,160,128]{2,1,0:T(8,128)(2,1)} %shard_map.50), calls=%async_computation.1 | async-start | bytes 655360 | tf_op jit(solution)/shard_map/all_to_all | solution.py:211
  24.1 5.3 %collective-permute-start = (bf16[4,7,16,128]{3,2,1,0:T(8,128)(2,1)S(1)}, bf16[4,7,16,128]{3,2,1,0:T(8,128)(2,1)S(1)}, u32[]{:S(2)}, u32[]{:S(2)}) collective-permute-start(bf16[4,7,16,128]{3,2,1,0:T(8,128)(2,1)S(1)} %shard_map.52), channel_id=1, source_target_pairs={{0,48},{1,13},{2,50},{3,15},{4,52},{5,1},{6,54},{7,3},{8,56},{9,5}... | collective-permute-start | bytes 344072 | tf_op jit(solution)/shard_map/ppermute | solution.py:215
  26.9 6.4 %collective-permute-start.1 = (bf16[4,7,16,128]{3,2,1,0:T(8,128)(2,1)S(1)}, bf16[4,7,16,128]{3,2,1,0:T(8,128)(2,1)S(1)}, u32[]{:S(2)}, u32[]{:S(2)}) collective-permute-start(bf16[4,7,16,128]{3,2,1,0:T(8,128)(2,1)S(1)} %shard_map.52), channel_id=1, source_target_pairs={{0,32},{1,9},{2,34},{3,11},{4,36},{5,13},{6,38},{7,15},{8,40},{9,1... | collective-permute-start | bytes 344072 | tf_op jit(solution)/shard_map/ppermute | solution.py:215
  27.7 6.7 %collective-permute-start.2 = (bf16[4,7,16,128]{3,2,1,0:T(8,128)(2,1)S(1)}, bf16[4,7,16,128]{3,2,1,0:T(8,128)(2,1)S(1)}, u32[]{:S(2)}, u32[]{:S(2)}) collective-permute-start(bf16[4,7,16,128]{3,2,1,0:T(8,128)(2,1)S(1)} %shard_map.52), channel_id=1, source_target_pairs={{0,16},{1,5},{2,18},{3,7},{4,20},{5,9},{6,22},{7,11},{8,24},{9,13}... | collective-permute-start | bytes 344072 | tf_op jit(solution)/shard_map/ppermute | solution.py:215
  36.5 12.5 %collective-permute-start.4 = (bf16[8,160,128]{2,1,0:T(8,128)(2,1)S(1)}, bf16[8,160,128]{2,1,0:T(8,128)(2,1)S(1)}, u32[]{:S(2)}, u32[]{:S(2)}) collective-permute-start(bf16[8,160,128]{2,1,0:T(8,128)(2,1)S(1)} %all-to-all-done.1.own_ref), channel_id=1, source_target_pairs={{16,0},{32,16},{48,32},{64,48},{80,64},{96,80},{112,96},{128,112},... | collective-permute-start | bytes 983048 | tf_op jit(solution)/shard_map/ppermute | solution.py:223
  40.0 17.0 %collective-permute-start.6 = (bf16[4,4,7,16,128]{4,3,2,1,0:T(8,128)(2,1)S(1)}, bf16[4,4,7,16,128]{4,3,2,1,0:T(8,128)(2,1)S(1)}, u32[]{:S(2)}, u32[]{:S(2)}) collective-permute-start(bf16[4,4,7,16,128]{4,3,2,1,0:T(8,128)(2,1)S(1)} %pad_maximum_fusion.1.part_0), channel_id=1, source_target_pairs={{0,12},{1,49},{2,14},{3,51},{4,0},{5,53},{6,2},{7,55},{8,4},{9,57}... | collective-permute-start | bytes 1376264 | tf_op jit(solution)/shard_map/ppermute | solution.py:215
  43.3 13.7 %collective-permute-start.7 = (bf16[4,4,7,16,128]{4,3,2,1,0:T(8,128)(2,1)S(1)}, bf16[4,4,7,16,128]{4,3,2,1,0:T(8,128)(2,1)S(1)}, u32[]{:S(2)}, u32[]{:S(2)}) collective-permute-start(bf16[4,4,7,16,128]{4,3,2,1,0:T(8,128)(2,1)S(1)} %pad_maximum_fusion.1.part_0), channel_id=1, source_target_pairs={{0,8},{1,33},{2,10},{3,35},{4,12},{5,37},{6,14},{7,39},{8,0},{9,41... | collective-permute-start | bytes 1376264 | tf_op jit(solution)/shard_map/ppermute | solution.py:215
  44.6 13.6 %collective-permute-start.8 = (bf16[4,4,7,16,128]{4,3,2,1,0:T(8,128)(2,1)S(1)}, bf16[4,4,7,16,128]{4,3,2,1,0:T(8,128)(2,1)S(1)}, u32[]{:S(2)}, u32[]{:S(2)}) collective-permute-start(bf16[4,4,7,16,128]{4,3,2,1,0:T(8,128)(2,1)S(1)} %pad_maximum_fusion.1.part_0), channel_id=1, source_target_pairs={{0,4},{1,17},{2,6},{3,19},{4,8},{5,21},{6,10},{7,23},{8,12},{9,25}... | collective-permute-start | bytes 1376264 | tf_op jit(solution)/shard_map/ppermute | solution.py:215
  44.6 11.1 %collective-permute-start.3 = (bf16[8,160,128]{2,1,0:T(8,128)(2,1)S(1)}, bf16[8,160,128]{2,1,0:T(8,128)(2,1)S(1)}, u32[]{:S(2)}, u32[]{:S(2)}) collective-permute-start(bf16[8,160,128]{2,1,0:T(8,128)(2,1)S(1)} %all-to-all-done.1.own_ref), channel_id=1, source_target_pairs={{0,16},{16,32},{32,48},{48,64},{64,80},{80,96},{96,112},{112,128},... | collective-permute-start | bytes 983048 | tf_op jit(solution)/shard_map/ppermute | solution.py:222
  55.8 13.0 %collective-permute-start.5 = (bf16[3,8,80,128]{3,2,1,0:T(8,128)(2,1)S(1)}, bf16[3,8,80,128]{3,2,1,0:T(8,128)(2,1)S(1)}, u32[]{:S(2)}, u32[]{:S(2)}) collective-permute-start(bf16[3,8,80,128]{3,2,1,0:T(8,128)(2,1)S(1)} %pad_maximum_fusion), channel_id=1, source_target_pairs={{0,1},{1,0},{2,3},{3,2},{4,5},{5,4},{6,7},{7,6},{8,9},{9,8},{10,11... | collective-permute-start | bytes 1474568 | tf_op jit(solution)/shard_map/ppermute | solution.py:224
  67.0 3.1 %collective-permute-start.9 = (f32[8,16,512]{2,1,0:T(8,128)S(1)}, f32[8,16,512]{2,1,0:T(8,128)S(1)}, u32[]{:S(2)}, u32[]{:S(2)}) collective-permute-start(f32[8,16,512]{2,1,0:T(8,128)S(1)} %get-tuple-element.13), channel_id=1, source_target_pairs={{0,1},{1,0},{2,3},{3,2},{4,5},{5,4},{6,7},{7,6},{8,9},{9,8},{10,11... | collective-permute-start | bytes 786440 | tf_op jit(solution)/shard_map/ppermute | solution.py:245

commit v5 on v4

v5 whole, which is shorter than its diff:
```python
import functools
import itertools

import jax
import jax.numpy as jnp
from jax import lax
from jax.experimental import pallas as pl
from jax.experimental.pallas import tpu as pltpu
from jax.sharding import Mesh
from jax.sharding import PartitionSpec as P

AXES = ("zl", "x", "y", "zh", "core")
SPACE = ("zl", "x")
FILT = ("y", "zh", "core")
BF16 = jnp.bfloat16
F32 = jnp.float32
VMEM = pl.BlockSpec(memory_space=pltpu.VMEM)

GROUPS = 8
CELLS = 512
CHUNKS = 5
ROWS = CHUNKS * 16
OFFSETS = 27
PART = 7


def index_of(zl, x, y, zh, core):
    return (((zl * 4 + x) * 4 + y) * 2 + zh) * 2 + core


def everyone():
    return itertools.product(range(4), range(4), range(4), range(2), range(2))


def pairs_of(move):
    return [(index_of(*place), index_of(*move(*place))) for place in everyone()]


def along(first, step):
    def move(zl, x, y, zh, core):
        if (core == 0) == first:
            return zl, (x - step) % 4, y, zh, core
        return zl, x, (y - step) % 4, zh, core

    return pairs_of(move)


def call(kernel, out_shape, flops=0, byte_count=1 << 20, scratch=(), mib=48):
    single = not isinstance(out_shape, (tuple, list))
    count = 1 if single else len(out_shape)
    return functools.partial(
        pl.pallas_call,
        kernel,
        out_shape=out_shape,
        out_specs=VMEM if single else [VMEM] * count,
        scratch_shapes=list(scratch),
        compiler_params=pltpu.CompilerParams(vmem_limit_bytes=mib << 20),
        cost_estimate=pl.CostEstimate(flops=flops, bytes_accessed=byte_count, transcendentals=0),
    )


def run(kernel, out_shape, *args, **options):
    return call(kernel, out_shape, **options)(in_specs=[VMEM] * len(args))(*args)


def pack_kernel(
    volume_ref, cotangent_ref, filters_ref, packed_ref, keep_ref, send_ref,
    volume, cotangent, filters, slabs_ref, sems,
):
    pairs = ((filters_ref, filters), (volume_ref, volume), (cotangent_ref, cotangent))
    copies = [pltpu.make_async_copy(a, b, sems.at[k]) for k, (a, b) in enumerate(pairs)]
    for copy in copies:
        copy.start()
    copies[0].wait()
    zero = jnp.zeros((16, 16), BF16)
    for outer in range(4):
        offsets = range(8 * outer, 8 * outer + 8)
        block = jnp.concatenate([filters[d] if d < OFFSETS else zero for d in offsets], axis=1)
        for copy in range(8):
            packed_ref[copy, outer] = block
    lane = lax.broadcasted_iota(jnp.int32, (16, 128), 1)
    for part, ref in enumerate((volume, cotangent)):
        copies[1 + part].wait()
        whole = pltpu.roll(ref[...].astype(F32), 64, 1)
        edge = whole[:, :128]
        pieces = [jnp.where(lane < 64, 0.0, edge)]
        pieces += [whole[:, 128 * j : 128 * (j + 1)] for j in range(1, 32)]
        pieces += [jnp.where(lane < 64, edge, 0.0)]
        pieces = [piece.astype(BF16) for piece in pieces]
        for slab in range(GROUPS):
            for chunk in range(CHUNKS):
                row = part * ROWS + chunk * 16
                slabs_ref[slab, row : row + 16, :] = pieces[4 * slab + chunk]
    zh = lax.axis_index("zh")
    for y in range(4):
        keep_ref[y] = slabs_ref[2 * y + zh]
        send_ref[y] = slabs_ref[2 * y + 1 - zh]


def route_kernel(keep_ref, got_ref, *out_refs):
    y, zh = lax.axis_index("y"), lax.axis_index("zh")
    for step, ref in enumerate(out_refs):
        to = lax.rem(y + 4 - step, 4)
        ref[zh] = keep_ref[to]
        ref[1 - zh] = got_ref[to]


def regroup_kernel(packed_ref, out_ref):
    for zl in range(4):
        for outer in range(PART):
            pieces = []
            for d in range(4 * outer, 4 * outer + 4):
                lane = 16 * (d % 8)
                pieces += [packed_ref[2 * zl + zh, d // 8, :, lane : lane + 16] for zh in range(2)]
            out_ref[zl, outer] = jnp.concatenate(pieces, axis=1)


def shifted(pieces):
    whole = jnp.concatenate(pieces, axis=0)
    middle = pltpu.roll(whole.astype(F32), 640 - 64, 1).astype(BF16)
    return whole[:, :CELLS], middle[:, :CELLS], whole[:, 128:]


def block_of(ref, group, first):
    return jnp.concatenate(
        [ref[group, first + 16 * c : first + 16 * (c + 1), :] for c in range(CHUNKS)], axis=1
    )


def turned(value, by):
    return jnp.concatenate([value[:, 128 - by :], value[:, : 128 - by]], axis=1)


def assemble(parts, weights_ref):
    lane = lax.broadcasted_iota(jnp.int32, (16, 128), 1)
    half, even = lane < 64, lane % 64 < 32

    def turn(pick):
        for zl in range(4):
            for x in range(4):
                row = 16 * (4 * zl + x)
                for outer in range(PART):
                    a, b, c, d = (pick(y, x)[zl, outer] for y in range(4))
                    a, c = jnp.where(half, a, turned(c, 64)), jnp.where(half, turned(a, 64), c)
                    b, d = jnp.where(half, b, turned(d, 64)), jnp.where(half, turned(b, 64), d)
                    for k, value in enumerate((
                        jnp.where(even, a, turned(b, 32)),
                        jnp.where(even, turned(a, 96), b),
                        jnp.where(even, c, turned(d, 32)),
                        jnp.where(even, turned(c, 96), d),
                    )):
                        weights_ref[4 * outer + k, row : row + 16, :] = value

    @pl.when(lax.axis_index("core") == 0)
    def _():
        turn(lambda y, x: parts[y].at[x])

    @pl.when(lax.axis_index("core") == 1)
    def _():
        turn(lambda y, x: parts[x].at[y])


def combine(before, middle, after):
    place = lax.broadcasted_iota(jnp.int32, middle.shape, 1) % 64
    left = jnp.where(place > 0, pltpu.roll(before, 1, 1), 0.0)
    right = jnp.where(place < 63, pltpu.roll(after, CELLS - 1, 1), 0.0)
    return middle + left + right


def grad_kernel(
    low_ref, own_ref, high_ref, part_0, part_1, part_2, part_3,
    keep_ref, send_ref, weights_ref, stack_ref, result_ref,
):
    assemble((part_0, part_1, part_2, part_3), weights_ref)
    for dx, ref in enumerate((high_ref, own_ref, low_ref)):
        above, same, below = shifted([block_of(ref, g, ROWS) for g in range(GROUPS)])
        for dy, value in enumerate((below, same, above)):
            row = (dx * 3 + dy) * 128
            stack_ref[row : row + 128, :] = value
    terms = []
    for dz in range(3):
        left = jnp.concatenate([weights_ref[k * 3 + dz] for k in range(9)], axis=1)
        terms.append(jnp.dot(left, stack_ref[...], preferred_element_type=F32))
    total = combine(terms[2], terms[1], terms[0])
    core, my_x = lax.axis_index("core"), lax.axis_index("x")
    for zl in range(4):
        for step in range(4):
            x = lax.rem(my_x + step, 4)
            row = 16 * (4 * zl + step)
            result_ref[2 * zl + x // 2, lax.rem(x, 2)] = total[row : row + 16]
    keep_ref[...] = result_ref[:, core]
    send_ref[...] = result_ref[:, 1 - core]


def forward_kernel(low_ref, own_ref, high_ref, other_ref, weights_ref, out_ref, volume_ref, stack_ref):
    core, my_x, my_y = (lax.axis_index(name) for name in ("core", "x", "y"))
    for dx, ref in enumerate((low_ref, own_ref, high_ref)):
        for g in range(GROUPS):
            volume_ref[dx, 2 * g + core] = block_of(ref, g, 0)
            volume_ref[dx, 2 * g + 1 - core] = block_of(other_ref.at[dx], g, 0)
        pieces = []
        for zl in range(4):
            for step in range(4):
                x = lax.rem(my_x + step, 4)
                pieces.append(volume_ref[dx, 4 * lax.rem(zl + 4 - my_y, 4) + x])
        for dy, value in enumerate(shifted(pieces)):
            row = (dx * 3 + dy) * 256
            stack_ref[row : row + 256, :] = value
    terms = []
    for dz in range(3):
        left = jnp.concatenate([weights_ref[k * 3 + dz] for k in range(9)], axis=0)
        terms.append(
            lax.dot_general(left, stack_ref[...], (((0,), (0,)), ((), ())), preferred_element_type=F32)
        )
    total = combine(*terms).astype(BF16)
    for step in range(4):
        y = lax.rem(my_y + step, 4)
        for zh in range(2):
            row = 16 * (2 * step + zh)
            out_ref[2 * y + zh] = total[row : row + 16]


def merge_kernel(output_ref, keep_ref, got_ref, out_ref):
    out_ref[:, :16, :] = output_ref[...]
    out_ref[:, 16:, :] = (keep_ref[...] + got_ref[...]).astype(BF16)


def split_kernel(packed_ref, output_ref, grad_ref):
    for g in range(GROUPS):
        output_ref[:, g * CELLS : (g + 1) * CELLS] = packed_ref[g, :16, :]
        grad_ref[:, g * CELLS : (g + 1) * CELLS] = packed_ref[g, 16:, :]


def local(volume, filters, cotangent):
    swap = [(0, 1), (1, 0)]
    half = jax.ShapeDtypeStruct((4, 2 * ROWS, 128), BF16)
    packed, keep, send = call(
        pack_kernel,
        [jax.ShapeDtypeStruct((8, 4, 16, 128), BF16), half, half],
        scratch=[
            pltpu.VMEM((16, 4096), BF16),
            pltpu.VMEM((16, 4096), BF16),
            pltpu.VMEM((OFFSETS, 16, 16), BF16),
            pltpu.VMEM((GROUPS, 2 * ROWS, 128), BF16),
            pltpu.SemaphoreType.DMA((3,)),
        ],
        mib=60,
    )(in_specs=[pl.BlockSpec(memory_space=pl.ANY)] * 3)(
        volume.reshape(16, 4096),
        cotangent.reshape(16, 4096),
        filters.reshape(OFFSETS, 16, 16),
    )
    got = lax.ppermute(send, "zh", swap)
    packed = lax.all_to_all(packed, ("zl", "zh"), 0, 0)
    routed = run(route_kernel, [jax.ShapeDtypeStruct((2, 2 * ROWS, 128), BF16)] * 4, keep, got)
    own = [routed[0]]
    for step in (1, 2, 3):
        own.append(lax.ppermute(routed[step], "y", [(i, (i - step) % 4) for i in range(4)]))
    own = jnp.stack(own).reshape(GROUPS, 2 * ROWS, 128)
    unit = run(regroup_kernel, jax.ShapeDtypeStruct((4, PART, 16, 128), BF16), packed)

    def gather(block, pairs):
        return [block] + [lax.ppermute(block, AXES, pairs(step)) for step in (1, 2, 3)]

    unit = jnp.stack(gather(unit, functools.partial(along, True)))
    parts = gather(unit, functools.partial(along, False))
    up = [(i, i + 1) for i in range(15)]
    down = [(b, a) for a, b in up]
    low = lax.ppermute(own, SPACE, up)
    high = lax.ppermute(own, SPACE, down)
    other = lax.ppermute(jnp.stack([low[:, :ROWS], own[:, :ROWS], high[:, :ROWS]]), "core", swap)
    flops = 2 * 27 * 256 * 128 * CELLS
    piece = jax.ShapeDtypeStruct((GROUPS, 16, CELLS), F32)
    keep, send, weights = run(
        grad_kernel,
        [piece, piece, jax.ShapeDtypeStruct((4 * PART, 256, 128), BF16)],
        low,
        own,
        high,
        *parts,
        flops=flops,
        byte_count=4 << 20,
        scratch=[pltpu.VMEM((9 * 128, CELLS), BF16), pltpu.VMEM((GROUPS, 2, 16, CELLS), F32)],
    )
    got = lax.ppermute(send, "core", swap)
    output = run(
        forward_kernel,
        jax.ShapeDtypeStruct((GROUPS, 16, CELLS), BF16),
        low,
        own,
        high,
        other,
        weights,
        flops=flops,
        byte_count=4 << 20,
        scratch=[
            pltpu.VMEM((3, 16, 16, CHUNKS * 128), BF16),
            pltpu.VMEM((9 * 256, CELLS), BF16),
        ],
    )
    merged = run(merge_kernel, jax.ShapeDtypeStruct((GROUPS, 32, CELLS), BF16), output, keep, got)
    merged = lax.all_to_all(merged, ("y", "zh"), 0, 0)
    plane = jax.ShapeDtypeStruct((16, 4096), BF16)
    output, grad = run(split_kernel, [plane, plane], merged)
    return output.reshape(16, 1, 4096), grad.reshape(16, 1, 4096)


def solution(mesh):
    split = Mesh(mesh.devices.reshape(4, 4, 4, 2, 2), AXES)
    act = P(FILT, SPACE, None)
    return jax.shard_map(
        local,
        mesh=split,
        in_specs=(act, P(None, None, None, SPACE, FILT), act),
        out_specs=(act, act),
        check_vma=False,
    )
```

time: 91.5 us -> 94.3 us (1.031)
  starting transfers between devices: 31.5 us -> 40.1 us
  waiting for transfers between devices: 23 us -> 18.3 us
  local copies, waits for them, and re-layouts: 2.73 us -> 0.95 us
    ppermute x0 -> x4, starting transfers between devices: none -> 11.1 us  [the longest x1 6.38 us: local(): got = lax.ppermute(send, 'zh', swap)]
    ppermute x6, starting transfers between devices: 9.13 us -> 16.6 us  [gather(): lax.ppermute(block, AXES, pairs(step))]
    ppermute x0 -> x4, waiting for transfers between devices: none -> 7.13 us  [the longest x1 4.84 us: local(): got = lax.ppermute(send, 'zh', swap)]
    ppermute x1, waiting for transfers between devices: 6.68 us -> 0.01 us  [local(): low = lax.ppermute(own, SPACE, up)]
    all_to_all x1 -> x0, starting transfers between devices: 5.53 us -> none  [local(): own = lax.all_to_all(own, ('y', 'zh'), 0, 0)]
    all_to_all x1, waiting for transfers between devices: 4.77 us -> 0.01 us  [local(): packed = lax.all_to_all(packed, ('zl', 'zh'), 0, 0)]
    all_to_all x1, starting transfers between devices: 8.57 us -> 4.29 us  [local(): packed = lax.all_to_all(packed, ('zl', 'zh'), 0, 0)]
    ppermute x6, waiting for transfers between devices: 7.08 us -> 11.2 us  [gather(): lax.ppermute(block, AXES, pairs(step))]
  transfers between devices with their start and end apart: 12 -> 15, of which waited for: 8 -> 6; matrix products, arithmetic and copies ran while one was open for 0% -> 0% of each run, Pallas kernels for 12% -> 11%
where the time goes in v5:
time: 94.3 us; the launch traced here: 94 us
  starting transfers between devices  40.1 us (43%)
  blocking collectives  20.2 us (21%)
  waiting for transfers between devices  18.3 us (19%)
  Pallas kernels  13.5 us (14%)
  local copies, waits for them, and re-layouts  0.95 us (1%)
    all_to_all x1, blocking collectives, local(): merged = lax.all_to_all(merged, ('y', 'zh'), 0, 0)  20.2 us
    ppermute x6, starting transfers between devices, gather(): lax.ppermute(block, AXES, pairs(step))  16.6 us
    pallas_call x6, Pallas kernels, run(): call(kernel, out_shape, **options)(in_specs=[VMEM] * len(args))(*args)  11.5 us
    ppermute x6, waiting for transfers between devices, gather(): lax.ppermute(block, AXES, pairs(step))  11.2 us
    ppermute x1, starting transfers between devices, local(): got = lax.ppermute(send, 'zh', swap)  6.38 us
    ppermute x1, waiting for transfers between devices, local(): got = lax.ppermute(send, 'zh', swap)  4.84 us
    ppermute x3, starting transfers between devices, local(): lax.ppermute(routed[step], 'y', [(i, (i - step) % 4) for i in range(4)])  4.69 us
    ppermute x1, starting transfers between devices, local(): high = lax.ppermute(own, SPACE, down)  4.55 us
  transfers between devices with their start and end apart: 15, of which 6 were waited for; matrix products, arithmetic and copies ran while one was open for 0% of the time, Pallas kernels for 11%

profile of v5, /device:TPU:32, one launch (start us, length us, event | category | flops | bytes accessed | tf_op | source)
XLA Modules:
  0.0 94.0 jit_solution(15311472359329840980)
XLA Ops:
  0.6 2.0 %shard_map.50 = (bf16[8,4,16,128]{3,2,1,0:T(8,128)(2,1)}, bf16[4,160,128]{2,1,0:T(8,128)(2,1)}, bf16[4,160,128]{2,1,0:T(8,128)(2,1)}) custom-call(bf16[16,4096]{1,0:T(8,128)(2,1)} %bitcast.27, bf16[16,4096]{1,0:T(8,128)(2,1)} %bitcast.28, bf16[27,16,16]{2,1,0:T(8,128)(2,1)} %bitcast.32), custom_call_target="tpu_custom_call" | custom-call | bytes 1048576 | tf_op jit(solution)/shard_map/pallas_call | solution.py:237
  2.6 6.4 %collective-permute-start = (bf16[4,160,128]{2,1,0:T(8,128)(2,1)}, bf16[4,160,128]{2,1,0:T(8,128)(2,1)S(1)}, u32[]{:S(2)}, u32[]{:S(2)}) collective-permute-start(bf16[4,160,128]{2,1,0:T(8,128)(2,1)} %get-tuple-element.15), channel_id=1, source_target_pairs={{0,2},{2,0},{1,3},{3,1},{4,6},{6,4},{5,7},{7,5},{8,10},{10,8},{9,1... | collective-permute-start | bytes 491528 | tf_op jit(solution)/shard_map/ppermute | solution.py:253
  9.0 4.3 %all-to-all-start = ((bf16[8,4,16,128]{3,2,1,0:T(8,128)(2,1)}), bf16[8,4,16,128]{3,2,1,0:T(8,128)(2,1)S(1)}, u32[]{:S(2)}, u32[]{:S(2)}) async-start(bf16[8,4,16,128]{3,2,1,0:T(8,128)(2,1)} %get-tuple-element.20), calls=%async_computation | async-start | bytes 262144 | tf_op jit(solution)/shard_map/all_to_all | solution.py:254
  13.3 4.8 %collective-permute-done.got_ref = bf16[4,160,128]{2,1,0:T(8,128)(2,1)S(1)} collective-permute-done((bf16[4,160,128]{2,1,0:T(8,128)(2,1)}, bf16[4,160,128]{2,1,0:T(8,128)(2,1)S(1)}, u32[]{:S(2)}, u32[]{:S(2)}) %collective-permute-start) | collective-permute-done | bytes 163872 | tf_op jit(solution)/shard_map/ppermute | solution.py:253
  18.1 0.0 copy-start
  18.1 0.9 copy-done
  19.1 3.1 %collective-permute-start.1 = (bf16[2,160,128]{2,1,0:T(8,128)(2,1)S(1)}, bf16[2,160,128]{2,1,0:T(8,128)(2,1)S(1)}, u32[]{:S(2)}, u32[]{:S(2)}) collective-permute-start(bf16[2,160,128]{2,1,0:T(8,128)(2,1)S(1)} %get-tuple-element.17), channel_id=1, source_target_pairs={{0,12},{4,0},{8,4},{12,8},{1,13},{5,1},{9,5},{13,9},{2,14},{6,2},{... | collective-permute-start | bytes 245768 | tf_op jit(solution)/shard_map/ppermute | solution.py:258
  22.2 0.6 collective-permute-start.2
  22.8 1.0 %collective-permute-start.3 = (bf16[2,160,128]{2,1,0:T(8,128)(2,1)S(1)}, bf16[2,160,128]{2,1,0:T(8,128)(2,1)S(1)}, u32[]{:S(2)}, u32[]{:S(2)}) collective-permute-start(bf16[2,160,128]{2,1,0:T(8,128)(2,1)S(1)} %get-tuple-element.19), channel_id=1, source_target_pairs={{0,4},{4,8},{8,12},{12,0},{1,5},{5,9},{9,13},{13,1},{2,6},{6,10},{... | collective-permute-start | bytes 245768 | tf_op jit(solution)/shard_map/ppermute | solution.py:258
  23.8 0.0 all-to-all-done.packed_ref
  23.8 0.3 shard_map.52
  24.1 2.8 %collective-permute-start.7 = (bf16[4,7,16,128]{3,2,1,0:T(8,128)(2,1)S(1)}, bf16[4,7,16,128]{3,2,1,0:T(8,128)(2,1)S(1)}, u32[]{:S(2)}, u32[]{:S(2)}) collective-permute-start(bf16[4,7,16,128]{3,2,1,0:T(8,128)(2,1)S(1)} %shard_map.52), channel_id=1, source_target_pairs={{0,48},{1,13},{2,50},{3,15},{4,52},{5,1},{6,54},{7,3},{8,56},{9,5}... | collective-permute-start | bytes 344072 | tf_op jit(solution)/shard_map/ppermute | solution.py:263
  26.9 0.8 collective-permute-start.8
  27.7 0.0 collective-permute-done.1
  27.7 0.9 collective-permute-start.9
  28.6 0.5 collective-permute-done.2
  29.1 1.8 %collective-permute-done.3 = bf16[2,160,128]{2,1,0:T(8,128)(2,1)S(1)} collective-permute-done((bf16[2,160,128]{2,1,0:T(8,128)(2,1)S(1)}, bf16[2,160,128]{2,1,0:T(8,128)(2,1)S(1)}, u32[]{:S(2)}, u32[]{:S(2)}) %collective-permute-start.3) | collective-permute-done | bytes 81952 | tf_op jit(solution)/shard_map/ppermute | solution.py:258
  30.9 3.4 %collective-permute-start.4 = (bf16[8,160,128]{2,1,0:T(8,128)(2,1)S(1)}, bf16[8,160,128]{2,1,0:T(8,128)(2,1)S(1)}, u32[]{:S(2)}, u32[]{:S(2)}) collective-permute-start(bf16[8,160,128]{2,1,0:T(8,128)(2,1)S(1)} %bitcast.20), channel_id=1, source_target_pairs={{0,16},{16,32},{32,48},{48,64},{64,80},{80,96},{96,112},{112,128},... | collective-permute-start | bytes 983048 | tf_op jit(solution)/shard_map/ppermute | solution.py:269
  34.3 4.6 %collective-permute-start.5 = (bf16[8,160,128]{2,1,0:T(8,128)(2,1)S(1)}, bf16[8,160,128]{2,1,0:T(8,128)(2,1)S(1)}, u32[]{:S(2)}, u32[]{:S(2)}) collective-permute-start(bf16[8,160,128]{2,1,0:T(8,128)(2,1)S(1)} %bitcast.21), channel_id=1, source_target_pairs={{16,0},{32,16},{48,32},{64,48},{80,64},{96,80},{112,96},{128,112},... | collective-permute-start | bytes 983048 | tf_op jit(solution)/shard_map/ppermute | solution.py:270
  38.9 0.0 collective-permute-done.7
  38.9 0.0 collective-permute-done.8
  38.9 0.0 collective-permute-done.9
  38.9 0.1 pad_maximum_fusion.1.part_0
  39.0 7.2 %collective-permute-start.10 = (bf16[4,4,7,16,128]{4,3,2,1,0:T(8,128)(2,1)S(1)}, bf16[4,4,7,16,128]{4,3,2,1,0:T(8,128)(2,1)S(1)}, u32[]{:S(2)}, u32[]{:S(2)}) collective-permute-start(bf16[4,4,7,16,128]{4,3,2,1,0:T(8,128)(2,1)S(1)} %pad_maximum_fusion.1.part_0), channel_id=1, source_target_pairs={{0,12},{1,49},{2,14},{3,51},{4,0},{5,53},{6,2},{7,55},{8,4},{9,57}... | collective-permute-start | bytes 1376264 | tf_op jit(solution)/shard_map/ppermute | solution.py:263
  46.2 4.9 %collective-permute-start.11 = (bf16[4,4,7,16,128]{4,3,2,1,0:T(8,128)(2,1)S(1)}, bf16[4,4,7,16,128]{4,3,2,1,0:T(8,128)(2,1)S(1)}, u32[]{:S(2)}, u32[]{:S(2)}) collective-permute-start(bf16[4,4,7,16,128]{4,3,2,1,0:T(8,128)(2,1)S(1)} %pad_maximum_fusion.1.part_0), channel_id=1, source_target_pairs={{0,8},{1,33},{2,10},{3,35},{4,12},{5,37},{6,14},{7,39},{8,0},{9,41... | collective-permute-start | bytes 1376264 | tf_op jit(solution)/shard_map/ppermute | solution.py:263
  51.1 0.0 collective-permute-start.12
  51.1 0.0 collective-permute-done.5.high_ref
  51.1 0.0 collective-permute-done.4.low_ref
  51.1 0.1 pad_maximum_fusion
  51.2 0.1 collective-permute-start.6
  51.3 4.2 %collective-permute-done.10.part_1 = bf16[4,4,7,16,128]{4,3,2,1,0:T(8,128)(2,1)S(1)} collective-permute-done((bf16[4,4,7,16,128]{4,3,2,1,0:T(8,128)(2,1)S(1)}, bf16[4,4,7,16,128]{4,3,2,1,0:T(8,128)(2,1)S(1)}, u32[]{:S(2)}, u32[]{:S(2)}) %collective-permute-start.10) | collective-permute-done | bytes 458784 | tf_op jit(solution)/shard_map/ppermute | solution.py:263
  55.5 2.2 %collective-permute-done.11.part_2 = bf16[4,4,7,16,128]{4,3,2,1,0:T(8,128)(2,1)S(1)} collective-permute-done((bf16[4,4,7,16,128]{4,3,2,1,0:T(8,128)(2,1)S(1)}, bf16[4,4,7,16,128]{4,3,2,1,0:T(8,128)(2,1)S(1)}, u32[]{:S(2)}, u32[]{:S(2)}) %collective-permute-start.11) | collective-permute-done | bytes 458784 | tf_op jit(solution)/shard_map/ppermute | solution.py:263
  57.6 4.8 %collective-permute-done.12.part_3 = bf16[4,4,7,16,128]{4,3,2,1,0:T(8,128)(2,1)S(1)} collective-permute-done((bf16[4,4,7,16,128]{4,3,2,1,0:T(8,128)(2,1)S(1)}, bf16[4,4,7,16,128]{4,3,2,1,0:T(8,128)(2,1)S(1)}, u32[]{:S(2)}, u32[]{:S(2)}) %collective-permute-start.12) | collective-permute-done | bytes 458784 | tf_op jit(solution)/shard_map/ppermute | solution.py:263
  62.5 9.0 %shard_map.53 = (f32[8,16,512]{2,1,0:T(8,128)S(1)}, f32[8,16,512]{2,1,0:T(8,128)S(1)}, bf16[28,256,128]{2,1,0:T(8,128)(2,1)S(1)}) custom-call(bf16[8,160,128]{2,1,0:T(8,128)(2,1)S(1)} %collective-permute-done.4.low_ref, bf16[8,160,128]{2,1,0:T(8,128)(2,1)S(1)} %bitcast.23, bf16[8,160,128]{2,1,0:T(8,128)(2,1)S(1)} %collective-permute-done.5.high_ref, ...), custom_call_target="tpu_custom_call" | custom-call | flops 905969664 | bytes 4194304 | tf_op jit(solution)/shard_map/pallas_call | solution.py:63
  71.4 0.1 collective-permute-start.13
  71.5 0.0 collective-permute-done.6.other_ref
  71.5 1.5 %shard_map.54.output_ref = bf16[8,16,512]{2,1,0:T(8,128)(2,1)S(1)} custom-call(bf16[8,160,128]{2,1,0:T(8,128)(2,1)S(1)} %collective-permute-done.4.low_ref, bf16[8,160,128]{2,1,0:T(8,128)(2,1)S(1)} %bitcast.24, bf16[8,160,128]{2,1,0:T(8,128)(2,1)S(1)} %collective-permute-done.5.high_ref, bf16[3,8,80,128]{3,2,1,0:T(8,128)(2,1)S(1)} %collective-permute-done.6.other_ref, ...), custom_call_target="tpu_custom_call" | custom-call | flops 905969664 | bytes 4194304 | tf_op jit(solution)/shard_map/pallas_call | solution.py:63
  73.0 0.0 collective-permute-done.13.got_ref
  73.1 20.2 %all_to_all.10.packed_ref = bf16[8,32,512]{2,1,0:T(8,128)(2,1)S(1)} all-to-all(bf16[8,32,512]{2,1,0:T(8,128)(2,1)S(1)} %shard_map.55), channel_id=1, replica_groups=mesh['zl'=4,'x'=4,'y'=4,'zh'=2,'core'=2] {'y','zh'}, dimensions={0} | all-to-all | bytes 524288 | tf_op jit(solution)/shard_map/all_to_all | solution.py:302
  93.3 0.7 shard_map.56
  (6 shorter events, 0.1 us)
Async XLA Ops:
  2.6 15.5 %collective-permute-start = (bf16[4,160,128]{2,1,0:T(8,128)(2,1)}, bf16[4,160,128]{2,1,0:T(8,128)(2,1)S(1)}, u32[]{:S(2)}, u32[]{:S(2)}) collective-permute-start(bf16[4,160,128]{2,1,0:T(8,128)(2,1)} %get-tuple-element.15), channel_id=1, source_target_pairs={{0,2},{2,0},{1,3},{3,1},{4,6},{6,4},{5,7},{7,5},{8,10},{10,8},{9,1... | collective-permute-start | bytes 491528 | tf_op jit(solution)/shard_map/ppermute | solution.py:253
  9.0 14.8 %all-to-all-start = ((bf16[8,4,16,128]{3,2,1,0:T(8,128)(2,1)}), bf16[8,4,16,128]{3,2,1,0:T(8,128)(2,1)S(1)}, u32[]{:S(2)}, u32[]{:S(2)}) async-start(bf16[8,4,16,128]{3,2,1,0:T(8,128)(2,1)} %get-tuple-element.20), calls=%async_computation | async-start | bytes 262144 | tf_op jit(solution)/shard_map/all_to_all | solution.py:254
  18.1 0.9 copy-start
  19.1 8.6 %collective-permute-start.1 = (bf16[2,160,128]{2,1,0:T(8,128)(2,1)S(1)}, bf16[2,160,128]{2,1,0:T(8,128)(2,1)S(1)}, u32[]{:S(2)}, u32[]{:S(2)}) collective-permute-start(bf16[2,160,128]{2,1,0:T(8,128)(2,1)S(1)} %get-tuple-element.17), channel_id=1, source_target_pairs={{0,12},{4,0},{8,4},{12,8},{1,13},{5,1},{9,5},{13,9},{2,14},{6,2},{... | collective-permute-start | bytes 245768 | tf_op jit(solution)/shard_map/ppermute | solution.py:258
  22.2 6.9 %collective-permute-start.2 = (bf16[2,160,128]{2,1,0:T(8,128)(2,1)S(1)}, bf16[2,160,128]{2,1,0:T(8,128)(2,1)S(1)}, u32[]{:S(2)}, u32[]{:S(2)}) collective-permute-start(bf16[2,160,128]{2,1,0:T(8,128)(2,1)S(1)} %get-tuple-element.18), channel_id=1, source_target_pairs={{0,8},{4,12},{8,0},{12,4},{1,9},{5,13},{9,1},{13,5},{2,10},{6,14},... | collective-permute-start | bytes 245768 | tf_op jit(solution)/shard_map/ppermute | solution.py:258
  22.8 8.1 %collective-permute-start.3 = (bf16[2,160,128]{2,1,0:T(8,128)(2,1)S(1)}, bf16[2,160,128]{2,1,0:T(8,128)(2,1)S(1)}, u32[]{:S(2)}, u32[]{:S(2)}) collective-permute-start(bf16[2,160,128]{2,1,0:T(8,128)(2,1)S(1)} %get-tuple-element.19), channel_id=1, source_target_pairs={{0,4},{4,8},{8,12},{12,0},{1,5},{5,9},{9,13},{13,1},{2,6},{6,10},{... | collective-permute-start | bytes 245768 | tf_op jit(solution)/shard_map/ppermute | solution.py:258
  24.1 14.8 %collective-permute-start.7 = (bf16[4,7,16,128]{3,2,1,0:T(8,128)(2,1)S(1)}, bf16[4,7,16,128]{3,2,1,0:T(8,128)(2,1)S(1)}, u32[]{:S(2)}, u32[]{:S(2)}) collective-permute-start(bf16[4,7,16,128]{3,2,1,0:T(8,128)(2,1)S(1)} %shard_map.52), channel_id=1, source_target_pairs={{0,48},{1,13},{2,50},{3,15},{4,52},{5,1},{6,54},{7,3},{8,56},{9,5}... | collective-permute-start | bytes 344072 | tf_op jit(solution)/shard_map/ppermute | solution.py:263
  26.9 12.0 %collective-permute-start.8 = (bf16[4,7,16,128]{3,2,1,0:T(8,128)(2,1)S(1)}, bf16[4,7,16,128]{3,2,1,0:T(8,128)(2,1)S(1)}, u32[]{:S(2)}, u32[]{:S(2)}) collective-permute-start(bf16[4,7,16,128]{3,2,1,0:T(8,128)(2,1)S(1)} %shard_map.52), channel_id=1, source_target_pairs={{0,32},{1,9},{2,34},{3,11},{4,36},{5,13},{6,38},{7,15},{8,40},{9,1... | collective-permute-start | bytes 344072 | tf_op jit(solution)/shard_map/ppermute | solution.py:263
  27.7 11.2 %collective-permute-start.9 = (bf16[4,7,16,128]{3,2,1,0:T(8,128)(2,1)S(1)}, bf16[4,7,16,128]{3,2,1,0:T(8,128)(2,1)S(1)}, u32[]{:S(2)}, u32[]{:S(2)}) collective-permute-start(bf16[4,7,16,128]{3,2,1,0:T(8,128)(2,1)S(1)} %shard_map.52), channel_id=1, source_target_pairs={{0,16},{1,5},{2,18},{3,7},{4,20},{5,9},{6,22},{7,11},{8,24},{9,13}... | collective-permute-start | bytes 344072 | tf_op jit(solution)/shard_map/ppermute | solution.py:263
  30.9 20.2 %collective-permute-start.4 = (bf16[8,160,128]{2,1,0:T(8,128)(2,1)S(1)}, bf16[8,160,128]{2,1,0:T(8,128)(2,1)S(1)}, u32[]{:S(2)}, u32[]{:S(2)}) collective-permute-start(bf16[8,160,128]{2,1,0:T(8,128)(2,1)S(1)} %bitcast.20), channel_id=1, source_target_pairs={{0,16},{16,32},{32,48},{48,64},{64,80},{80,96},{96,112},{112,128},... | collective-permute-start | bytes 983048 | tf_op jit(solution)/shard_map/ppermute | solution.py:269
  34.3 16.8 %collective-permute-start.5 = (bf16[8,160,128]{2,1,0:T(8,128)(2,1)S(1)}, bf16[8,160,128]{2,1,0:T(8,128)(2,1)S(1)}, u32[]{:S(2)}, u32[]{:S(2)}) collective-permute-start(bf16[8,160,128]{2,1,0:T(8,128)(2,1)S(1)} %bitcast.21), channel_id=1, source_target_pairs={{16,0},{32,16},{48,32},{64,48},{80,64},{96,80},{112,96},{128,112},... | collective-permute-start | bytes 983048 | tf_op jit(solution)/shard_map/ppermute | solution.py:270
  39.0 16.5 %collective-permute-start.10 = (bf16[4,4,7,16,128]{4,3,2,1,0:T(8,128)(2,1)S(1)}, bf16[4,4,7,16,128]{4,3,2,1,0:T(8,128)(2,1)S(1)}, u32[]{:S(2)}, u32[]{:S(2)}) collective-permute-start(bf16[4,4,7,16,128]{4,3,2,1,0:T(8,128)(2,1)S(1)} %pad_maximum_fusion.1.part_0), channel_id=1, source_target_pairs={{0,12},{1,49},{2,14},{3,51},{4,0},{5,53},{6,2},{7,55},{8,4},{9,57}... | collective-permute-start | bytes 1376264 | tf_op jit(solution)/shard_map/ppermute | solution.py:263
  46.2 11.4 %collective-permute-start.11 = (bf16[4,4,7,16,128]{4,3,2,1,0:T(8,128)(2,1)S(1)}, bf16[4,4,7,16,128]{4,3,2,1,0:T(8,128)(2,1)S(1)}, u32[]{:S(2)}, u32[]{:S(2)}) collective-permute-start(bf16[4,4,7,16,128]{4,3,2,1,0:T(8,128)(2,1)S(1)} %pad_maximum_fusion.1.part_0), channel_id=1, source_target_pairs={{0,8},{1,33},{2,10},{3,35},{4,12},{5,37},{6,14},{7,39},{8,0},{9,41... | collective-permute-start | bytes 1376264 | tf_op jit(solution)/shard_map/ppermute | solution.py:263
  51.1 11.4 %collective-permute-start.12 = (bf16[4,4,7,16,128]{4,3,2,1,0:T(8,128)(2,1)S(1)}, bf16[4,4,7,16,128]{4,3,2,1,0:T(8,128)(2,1)S(1)}, u32[]{:S(2)}, u32[]{:S(2)}) collective-permute-start(bf16[4,4,7,16,128]{4,3,2,1,0:T(8,128)(2,1)S(1)} %pad_maximum_fusion.1.part_0), channel_id=1, source_target_pairs={{0,4},{1,17},{2,6},{3,19},{4,8},{5,21},{6,10},{7,23},{8,12},{9,25}... | collective-permute-start | bytes 1376264 | tf_op jit(solution)/shard_map/ppermute | solution.py:263
  51.2 20.3 %collective-permute-start.6 = (bf16[3,8,80,128]{3,2,1,0:T(8,128)(2,1)S(1)}, bf16[3,8,80,128]{3,2,1,0:T(8,128)(2,1)S(1)}, u32[]{:S(2)}, u32[]{:S(2)}) collective-permute-start(bf16[3,8,80,128]{3,2,1,0:T(8,128)(2,1)S(1)} %pad_maximum_fusion), channel_id=1, source_target_pairs={{0,1},{1,0},{2,3},{3,2},{4,5},{5,4},{6,7},{7,6},{8,9},{9,8},{10,11... | collective-permute-start | bytes 1474568 | tf_op jit(solution)/shard_map/ppermute | solution.py:271
  71.4 1.6 %collective-permute-start.13 = (f32[8,16,512]{2,1,0:T(8,128)S(1)}, f32[8,16,512]{2,1,0:T(8,128)S(1)}, u32[]{:S(2)}, u32[]{:S(2)}) collective-permute-start(f32[8,16,512]{2,1,0:T(8,128)S(1)} %get-tuple-element.23), channel_id=1, source_target_pairs={{0,1},{1,0},{2,3},{3,2},{4,5},{5,4},{6,7},{7,6},{8,9},{9,8},{10,11... | collective-permute-start | bytes 786440 | tf_op jit(solution)/shard_map/ppermute | solution.py:285

commit v6 on v5

--- a/solution.py
+++ b/solution.py
@@ -132,24 +132,25 @@
 
 
 def assemble(parts, weights_ref):
-    lane = lax.broadcasted_iota(jnp.int32, (16, 128), 1)
+    lane = lax.broadcasted_iota(jnp.int32, (PART * 16, 128), 1)
     half, even = lane < 64, lane % 64 < 32
 
     def turn(pick):
         for zl in range(4):
             for x in range(4):
                 row = 16 * (4 * zl + x)
+                a, b, c, d = (pick(y, x)[zl].reshape(PART * 16, 128) for y in range(4))
+                a, c = jnp.where(half, a, turned(c, 64)), jnp.where(half, turned(a, 64), c)
+                b, d = jnp.where(half, b, turned(d, 64)), jnp.where(half, turned(b, 64), d)
+                values = (
+                    jnp.where(even, a, turned(b, 32)),
+                    jnp.where(even, turned(a, 96), b),
+                    jnp.where(even, c, turned(d, 32)),
+                    jnp.where(even, turned(c, 96), d),
+                )
                 for outer in range(PART):
-                    a, b, c, d = (pick(y, x)[zl, outer] for y in range(4))
-                    a, c = jnp.where(half, a, turned(c, 64)), jnp.where(half, turned(a, 64), c)
-                    b, d = jnp.where(half, b, turned(d, 64)), jnp.where(half, turned(b, 64), d)
-                    for k, value in enumerate((
-                        jnp.where(even, a, turned(b, 32)),
-                        jnp.where(even, turned(a, 96), b),
-                        jnp.where(even, c, turned(d, 32)),
-                        jnp.where(even, turned(c, 96), d),
-                    )):
-                        weights_ref[4 * outer + k, row : row + 16, :] = value
+                    for k, value in enumerate(values):
+                        weights_ref[4 * outer + k, row : row + 16, :] = value[16 * outer : 16 * (outer + 1)]
 
     @pl.when(lax.axis_index("core") == 0)
     def _():

time: 94.3 us -> 88.5 us (0.938)
  Pallas kernels: 13.5 us -> 7.69 us
    pallas_call x6, Pallas kernels: 11.5 us -> 5.69 us  [run(): call(kernel, out_shape, **options)(in_specs=[VMEM] * len(args))(*args)]
  transfers between devices with their start and end apart: 15 -> 15, of which waited for: 6 -> 6; matrix products, arithmetic and copies ran while one was open for 0% -> 0% of each run, Pallas kernels for 11% -> 6%
where the time goes in v6:
time: 88.5 us; the launch traced here: 88.2 us
  starting transfers between devices  40.1 us (45%)
  blocking collectives  20.2 us (23%)
  waiting for transfers between devices  18.3 us (21%)
  Pallas kernels  7.69 us (9%)
  local copies, waits for them, and re-layouts  0.95 us (1%)
    all_to_all x1, blocking collectives, local(): merged = lax.all_to_all(merged, ('y', 'zh'), 0, 0)  20.2 us
    ppermute x6, starting transfers between devices, gather(): lax.ppermute(block, AXES, pairs(step))  16.6 us
    ppermute x6, waiting for transfers between devices, gather(): lax.ppermute(block, AXES, pairs(step))  11.2 us
    ppermute x1, starting transfers between devices, local(): got = lax.ppermute(send, 'zh', swap)  6.38 us
    pallas_call x6, Pallas kernels, run(): call(kernel, out_shape, **options)(in_specs=[VMEM] * len(args))(*args)  5.69 us
    ppermute x1, waiting for transfers between devices, local(): got = lax.ppermute(send, 'zh', swap)  4.84 us
    ppermute x3, starting transfers between devices, local(): lax.ppermute(routed[step], 'y', [(i, (i - step) % 4) for i in range(4)])  4.69 us
    ppermute x1, starting transfers between devices, local(): high = lax.ppermute(own, SPACE, down)  4.55 us
  transfers between devices with their start and end apart: 15, of which 6 were waited for; matrix products, arithmetic and copies ran while one was open for 0% of the time, Pallas kernels for 6%

profile of v6, /device:TPU:32, one launch (start us, length us, event | category | flops | bytes accessed | tf_op | source)
XLA Modules:
  0.0 88.2 jit_solution(2164430161074561394)
XLA Ops:
  0.6 2.0 %shard_map.50 = (bf16[8,4,16,128]{3,2,1,0:T(8,128)(2,1)}, bf16[4,160,128]{2,1,0:T(8,128)(2,1)}, bf16[4,160,128]{2,1,0:T(8,128)(2,1)}) custom-call(bf16[16,4096]{1,0:T(8,128)(2,1)} %bitcast.27, bf16[16,4096]{1,0:T(8,128)(2,1)} %bitcast.28, bf16[27,16,16]{2,1,0:T(8,128)(2,1)} %bitcast.32), custom_call_target="tpu_custom_call" | custom-call | bytes 1048576 | tf_op jit(solution)/shard_map/pallas_call | solution.py:238
  2.6 6.4 %collective-permute-start = (bf16[4,160,128]{2,1,0:T(8,128)(2,1)}, bf16[4,160,128]{2,1,0:T(8,128)(2,1)S(1)}, u32[]{:S(2)}, u32[]{:S(2)}) collective-permute-start(bf16[4,160,128]{2,1,0:T(8,128)(2,1)} %get-tuple-element.15), channel_id=1, source_target_pairs={{0,2},{2,0},{1,3},{3,1},{4,6},{6,4},{5,7},{7,5},{8,10},{10,8},{9,1... | collective-permute-start | bytes 491528 | tf_op jit(solution)/shard_map/ppermute | solution.py:254
  9.0 4.3 %all-to-all-start = ((bf16[8,4,16,128]{3,2,1,0:T(8,128)(2,1)}), bf16[8,4,16,128]{3,2,1,0:T(8,128)(2,1)S(1)}, u32[]{:S(2)}, u32[]{:S(2)}) async-start(bf16[8,4,16,128]{3,2,1,0:T(8,128)(2,1)} %get-tuple-element.20), calls=%async_computation | async-start | bytes 262144 | tf_op jit(solution)/shard_map/all_to_all | solution.py:255
  13.3 4.8 %collective-permute-done.got_ref = bf16[4,160,128]{2,1,0:T(8,128)(2,1)S(1)} collective-permute-done((bf16[4,160,128]{2,1,0:T(8,128)(2,1)}, bf16[4,160,128]{2,1,0:T(8,128)(2,1)S(1)}, u32[]{:S(2)}, u32[]{:S(2)}) %collective-permute-start) | collective-permute-done | bytes 163872 | tf_op jit(solution)/shard_map/ppermute | solution.py:254
  18.1 0.0 copy-start
  18.1 0.9 %copy-done = bf16[4,160,128]{2,1,0:T(8,128)(2,1)S(1)} copy-done((bf16[4,160,128]{2,1,0:T(8,128)(2,1)S(1)}, bf16[4,160,128]{2,1,0:T(8,128)(2,1)}, u32[]{:S(2)}) %copy-start) | copy-done | bytes 163864
  19.1 3.1 %collective-permute-start.1 = (bf16[2,160,128]{2,1,0:T(8,128)(2,1)S(1)}, bf16[2,160,128]{2,1,0:T(8,128)(2,1)S(1)}, u32[]{:S(2)}, u32[]{:S(2)}) collective-permute-start(bf16[2,160,128]{2,1,0:T(8,128)(2,1)S(1)} %get-tuple-element.17), channel_id=1, source_target_pairs={{0,12},{4,0},{8,4},{12,8},{1,13},{5,1},{9,5},{13,9},{2,14},{6,2},{... | collective-permute-start | bytes 245768 | tf_op jit(solution)/shard_map/ppermute | solution.py:259
  22.2 0.6 collective-permute-start.2
  22.8 1.0 %collective-permute-start.3 = (bf16[2,160,128]{2,1,0:T(8,128)(2,1)S(1)}, bf16[2,160,128]{2,1,0:T(8,128)(2,1)S(1)}, u32[]{:S(2)}, u32[]{:S(2)}) collective-permute-start(bf16[2,160,128]{2,1,0:T(8,128)(2,1)S(1)} %get-tuple-element.19), channel_id=1, source_target_pairs={{0,4},{4,8},{8,12},{12,0},{1,5},{5,9},{9,13},{13,1},{2,6},{6,10},{... | collective-permute-start | bytes 245768 | tf_op jit(solution)/shard_map/ppermute | solution.py:259
  23.8 0.0 all-to-all-done.packed_ref
  23.8 0.3 shard_map.52
  24.1 2.8 %collective-permute-start.7 = (bf16[4,7,16,128]{3,2,1,0:T(8,128)(2,1)S(1)}, bf16[4,7,16,128]{3,2,1,0:T(8,128)(2,1)S(1)}, u32[]{:S(2)}, u32[]{:S(2)}) collective-permute-start(bf16[4,7,16,128]{3,2,1,0:T(8,128)(2,1)S(1)} %shard_map.52), channel_id=1, source_target_pairs={{0,48},{1,13},{2,50},{3,15},{4,52},{5,1},{6,54},{7,3},{8,56},{9,5}... | collective-permute-start | bytes 344072 | tf_op jit(solution)/shard_map/ppermute | solution.py:264
  26.9 0.8 collective-permute-start.8
  27.7 0.0 collective-permute-done.1
  27.7 0.9 %collective-permute-start.9 = (bf16[4,7,16,128]{3,2,1,0:T(8,128)(2,1)S(1)}, bf16[4,7,16,128]{3,2,1,0:T(8,128)(2,1)S(1)}, u32[]{:S(2)}, u32[]{:S(2)}) collective-permute-start(bf16[4,7,16,128]{3,2,1,0:T(8,128)(2,1)S(1)} %shard_map.52), channel_id=1, source_target_pairs={{0,16},{1,5},{2,18},{3,7},{4,20},{5,9},{6,22},{7,11},{8,24},{9,13}... | collective-permute-start | bytes 344072 | tf_op jit(solution)/shard_map/ppermute | solution.py:264
  28.6 0.5 collective-permute-done.2
  29.1 1.8 %collective-permute-done.3 = bf16[2,160,128]{2,1,0:T(8,128)(2,1)S(1)} collective-permute-done((bf16[2,160,128]{2,1,0:T(8,128)(2,1)S(1)}, bf16[2,160,128]{2,1,0:T(8,128)(2,1)S(1)}, u32[]{:S(2)}, u32[]{:S(2)}) %collective-permute-start.3) | collective-permute-done | bytes 81952 | tf_op jit(solution)/shard_map/ppermute | solution.py:259
  30.9 3.4 %collective-permute-start.4 = (bf16[8,160,128]{2,1,0:T(8,128)(2,1)S(1)}, bf16[8,160,128]{2,1,0:T(8,128)(2,1)S(1)}, u32[]{:S(2)}, u32[]{:S(2)}) collective-permute-start(bf16[8,160,128]{2,1,0:T(8,128)(2,1)S(1)} %bitcast.20), channel_id=1, source_target_pairs={{0,16},{16,32},{32,48},{48,64},{64,80},{80,96},{96,112},{112,128},... | collective-permute-start | bytes 983048 | tf_op jit(solution)/shard_map/ppermute | solution.py:270
  34.3 4.6 %collective-permute-start.5 = (bf16[8,160,128]{2,1,0:T(8,128)(2,1)S(1)}, bf16[8,160,128]{2,1,0:T(8,128)(2,1)S(1)}, u32[]{:S(2)}, u32[]{:S(2)}) collective-permute-start(bf16[8,160,128]{2,1,0:T(8,128)(2,1)S(1)} %bitcast.21), channel_id=1, source_target_pairs={{16,0},{32,16},{48,32},{64,48},{80,64},{96,80},{112,96},{128,112},... | collective-permute-start | bytes 983048 | tf_op jit(solution)/shard_map/ppermute | solution.py:271
  38.9 0.0 collective-permute-done.7
  38.9 0.0 collective-permute-done.8
  38.9 0.0 collective-permute-done.9
  38.9 0.1 pad_maximum_fusion.1.part_0
  39.0 7.2 %collective-permute-start.10 = (bf16[4,4,7,16,128]{4,3,2,1,0:T(8,128)(2,1)S(1)}, bf16[4,4,7,16,128]{4,3,2,1,0:T(8,128)(2,1)S(1)}, u32[]{:S(2)}, u32[]{:S(2)}) collective-permute-start(bf16[4,4,7,16,128]{4,3,2,1,0:T(8,128)(2,1)S(1)} %pad_maximum_fusion.1.part_0), channel_id=1, source_target_pairs={{0,12},{1,49},{2,14},{3,51},{4,0},{5,53},{6,2},{7,55},{8,4},{9,57}... | collective-permute-start | bytes 1376264 | tf_op jit(solution)/shard_map/ppermute | solution.py:264
  46.2 4.9 %collective-permute-start.11 = (bf16[4,4,7,16,128]{4,3,2,1,0:T(8,128)(2,1)S(1)}, bf16[4,4,7,16,128]{4,3,2,1,0:T(8,128)(2,1)S(1)}, u32[]{:S(2)}, u32[]{:S(2)}) collective-permute-start(bf16[4,4,7,16,128]{4,3,2,1,0:T(8,128)(2,1)S(1)} %pad_maximum_fusion.1.part_0), channel_id=1, source_target_pairs={{0,8},{1,33},{2,10},{3,35},{4,12},{5,37},{6,14},{7,39},{8,0},{9,41... | collective-permute-start | bytes 1376264 | tf_op jit(solution)/shard_map/ppermute | solution.py:264
  51.1 0.0 collective-permute-start.12
  51.1 0.0 collective-permute-done.5.high_ref
  51.1 0.0 collective-permute-done.4.low_ref
  51.1 0.1 pad_maximum_fusion
  51.2 0.1 collective-permute-start.6
  51.3 4.2 %collective-permute-done.10.part_1 = bf16[4,4,7,16,128]{4,3,2,1,0:T(8,128)(2,1)S(1)} collective-permute-done((bf16[4,4,7,16,128]{4,3,2,1,0:T(8,128)(2,1)S(1)}, bf16[4,4,7,16,128]{4,3,2,1,0:T(8,128)(2,1)S(1)}, u32[]{:S(2)}, u32[]{:S(2)}) %collective-permute-start.10) | collective-permute-done | bytes 458784 | tf_op jit(solution)/shard_map/ppermute | solution.py:264
  55.5 2.2 %collective-permute-done.11.part_2 = bf16[4,4,7,16,128]{4,3,2,1,0:T(8,128)(2,1)S(1)} collective-permute-done((bf16[4,4,7,16,128]{4,3,2,1,0:T(8,128)(2,1)S(1)}, bf16[4,4,7,16,128]{4,3,2,1,0:T(8,128)(2,1)S(1)}, u32[]{:S(2)}, u32[]{:S(2)}) %collective-permute-start.11) | collective-permute-done | bytes 458784 | tf_op jit(solution)/shard_map/ppermute | solution.py:264
  57.6 4.8 %collective-permute-done.12.part_3 = bf16[4,4,7,16,128]{4,3,2,1,0:T(8,128)(2,1)S(1)} collective-permute-done((bf16[4,4,7,16,128]{4,3,2,1,0:T(8,128)(2,1)S(1)}, bf16[4,4,7,16,128]{4,3,2,1,0:T(8,128)(2,1)S(1)}, u32[]{:S(2)}, u32[]{:S(2)}) %collective-permute-start.12) | collective-permute-done | bytes 458784 | tf_op jit(solution)/shard_map/ppermute | solution.py:264
  62.5 3.2 %shard_map.53 = (f32[8,16,512]{2,1,0:T(8,128)S(1)}, f32[8,16,512]{2,1,0:T(8,128)S(1)}, bf16[28,256,128]{2,1,0:T(8,128)(2,1)S(1)}) custom-call(bf16[8,160,128]{2,1,0:T(8,128)(2,1)S(1)} %collective-permute-done.4.low_ref, bf16[8,160,128]{2,1,0:T(8,128)(2,1)S(1)} %bitcast.23, bf16[8,160,128]{2,1,0:T(8,128)(2,1)S(1)} %collective-permute-done.5.high_ref, ...), custom_call_target="tpu_custom_call" | custom-call | flops 905969664 | bytes 4194304 | tf_op jit(solution)/shard_map/pallas_call | solution.py:63
  65.6 0.1 collective-permute-start.13
  65.7 0.0 collective-permute-done.6.other_ref
  65.7 1.5 %shard_map.54.output_ref = bf16[8,16,512]{2,1,0:T(8,128)(2,1)S(1)} custom-call(bf16[8,160,128]{2,1,0:T(8,128)(2,1)S(1)} %collective-permute-done.4.low_ref, bf16[8,160,128]{2,1,0:T(8,128)(2,1)S(1)} %bitcast.24, bf16[8,160,128]{2,1,0:T(8,128)(2,1)S(1)} %collective-permute-done.5.high_ref, bf16[3,8,80,128]{3,2,1,0:T(8,128)(2,1)S(1)} %collective-permute-done.6.other_ref, ...), custom_call_target="tpu_custom_call" | custom-call | flops 905969664 | bytes 4194304 | tf_op jit(solution)/shard_map/pallas_call | solution.py:63
  67.2 0.0 collective-permute-done.13.got_ref
  67.3 20.2 %all_to_all.10.packed_ref = bf16[8,32,512]{2,1,0:T(8,128)(2,1)S(1)} all-to-all(bf16[8,32,512]{2,1,0:T(8,128)(2,1)S(1)} %shard_map.55), channel_id=1, replica_groups=mesh['zl'=4,'x'=4,'y'=4,'zh'=2,'core'=2] {'y','zh'}, dimensions={0} | all-to-all | bytes 524288 | tf_op jit(solution)/shard_map/all_to_all | solution.py:303
  87.5 0.7 shard_map.56
  (6 shorter events, 0.1 us)
Async XLA Ops:
  2.6 15.5 %collective-permute-start = (bf16[4,160,128]{2,1,0:T(8,128)(2,1)}, bf16[4,160,128]{2,1,0:T(8,128)(2,1)S(1)}, u32[]{:S(2)}, u32[]{:S(2)}) collective-permute-start(bf16[4,160,128]{2,1,0:T(8,128)(2,1)} %get-tuple-element.15), channel_id=1, source_target_pairs={{0,2},{2,0},{1,3},{3,1},{4,6},{6,4},{5,7},{7,5},{8,10},{10,8},{9,1... | collective-permute-start | bytes 491528 | tf_op jit(solution)/shard_map/ppermute | solution.py:254
  9.0 14.8 %all-to-all-start = ((bf16[8,4,16,128]{3,2,1,0:T(8,128)(2,1)}), bf16[8,4,16,128]{3,2,1,0:T(8,128)(2,1)S(1)}, u32[]{:S(2)}, u32[]{:S(2)}) async-start(bf16[8,4,16,128]{3,2,1,0:T(8,128)(2,1)} %get-tuple-element.20), calls=%async_computation | async-start | bytes 262144 | tf_op jit(solution)/shard_map/all_to_all | solution.py:255
  18.1 0.9 %copy-start = (bf16[4,160,128]{2,1,0:T(8,128)(2,1)S(1)}, bf16[4,160,128]{2,1,0:T(8,128)(2,1)}, u32[]{:S(2)}) copy-start(bf16[4,160,128]{2,1,0:T(8,128)(2,1)} %get-tuple-element.14.keep_ref) | copy-start | bytes 491524
  19.1 8.6 %collective-permute-start.1 = (bf16[2,160,128]{2,1,0:T(8,128)(2,1)S(1)}, bf16[2,160,128]{2,1,0:T(8,128)(2,1)S(1)}, u32[]{:S(2)}, u32[]{:S(2)}) collective-permute-start(bf16[2,160,128]{2,1,0:T(8,128)(2,1)S(1)} %get-tuple-element.17), channel_id=1, source_target_pairs={{0,12},{4,0},{8,4},{12,8},{1,13},{5,1},{9,5},{13,9},{2,14},{6,2},{... | collective-permute-start | bytes 245768 | tf_op jit(solution)/shard_map/ppermute | solution.py:259
  22.2 6.9 %collective-permute-start.2 = (bf16[2,160,128]{2,1,0:T(8,128)(2,1)S(1)}, bf16[2,160,128]{2,1,0:T(8,128)(2,1)S(1)}, u32[]{:S(2)}, u32[]{:S(2)}) collective-permute-start(bf16[2,160,128]{2,1,0:T(8,128)(2,1)S(1)} %get-tuple-element.18), channel_id=1, source_target_pairs={{0,8},{4,12},{8,0},{12,4},{1,9},{5,13},{9,1},{13,5},{2,10},{6,14},... | collective-permute-start | bytes 245768 | tf_op jit(solution)/shard_map/ppermute | solution.py:259
  22.8 8.1 %collective-permute-start.3 = (bf16[2,160,128]{2,1,0:T(8,128)(2,1)S(1)}, bf16[2,160,128]{2,1,0:T(8,128)(2,1)S(1)}, u32[]{:S(2)}, u32[]{:S(2)}) collective-permute-start(bf16[2,160,128]{2,1,0:T(8,128)(2,1)S(1)} %get-tuple-element.19), channel_id=1, source_target_pairs={{0,4},{4,8},{8,12},{12,0},{1,5},{5,9},{9,13},{13,1},{2,6},{6,10},{... | collective-permute-start | bytes 245768 | tf_op jit(solution)/shard_map/ppermute | solution.py:259
  24.1 14.8 %collective-permute-start.7 = (bf16[4,7,16,128]{3,2,1,0:T(8,128)(2,1)S(1)}, bf16[4,7,16,128]{3,2,1,0:T(8,128)(2,1)S(1)}, u32[]{:S(2)}, u32[]{:S(2)}) collective-permute-start(bf16[4,7,16,128]{3,2,1,0:T(8,128)(2,1)S(1)} %shard_map.52), channel_id=1, source_target_pairs={{0,48},{1,13},{2,50},{3,15},{4,52},{5,1},{6,54},{7,3},{8,56},{9,5}... | collective-permute-start | bytes 344072 | tf_op jit(solution)/shard_map/ppermute | solution.py:264
  26.9 12.0 %collective-permute-start.8 = (bf16[4,7,16,128]{3,2,1,0:T(8,128)(2,1)S(1)}, bf16[4,7,16,128]{3,2,1,0:T(8,128)(2,1)S(1)}, u32[]{:S(2)}, u32[]{:S(2)}) collective-permute-start(bf16[4,7,16,128]{3,2,1,0:T(8,128)(2,1)S(1)} %shard_map.52), channel_id=1, source_target_pairs={{0,32},{1,9},{2,34},{3,11},{4,36},{5,13},{6,38},{7,15},{8,40},{9,1... | collective-permute-start | bytes 344072 | tf_op jit(solution)/shard_map/ppermute | solution.py:264
  27.7 11.2 %collective-permute-start.9 = (bf16[4,7,16,128]{3,2,1,0:T(8,128)(2,1)S(1)}, bf16[4,7,16,128]{3,2,1,0:T(8,128)(2,1)S(1)}, u32[]{:S(2)}, u32[]{:S(2)}) collective-permute-start(bf16[4,7,16,128]{3,2,1,0:T(8,128)(2,1)S(1)} %shard_map.52), channel_id=1, source_target_pairs={{0,16},{1,5},{2,18},{3,7},{4,20},{5,9},{6,22},{7,11},{8,24},{9,13}... | collective-permute-start | bytes 344072 | tf_op jit(solution)/shard_map/ppermute | solution.py:264
  30.9 20.2 %collective-permute-start.4 = (bf16[8,160,128]{2,1,0:T(8,128)(2,1)S(1)}, bf16[8,160,128]{2,1,0:T(8,128)(2,1)S(1)}, u32[]{:S(2)}, u32[]{:S(2)}) collective-permute-start(bf16[8,160,128]{2,1,0:T(8,128)(2,1)S(1)} %bitcast.20), channel_id=1, source_target_pairs={{0,16},{16,32},{32,48},{48,64},{64,80},{80,96},{96,112},{112,128},... | collective-permute-start | bytes 983048 | tf_op jit(solution)/shard_map/ppermute | solution.py:270
  34.3 16.8 %collective-permute-start.5 = (bf16[8,160,128]{2,1,0:T(8,128)(2,1)S(1)}, bf16[8,160,128]{2,1,0:T(8,128)(2,1)S(1)}, u32[]{:S(2)}, u32[]{:S(2)}) collective-permute-start(bf16[8,160,128]{2,1,0:T(8,128)(2,1)S(1)} %bitcast.21), channel_id=1, source_target_pairs={{16,0},{32,16},{48,32},{64,48},{80,64},{96,80},{112,96},{128,112},... | collective-permute-start | bytes 983048 | tf_op jit(solution)/shard_map/ppermute | solution.py:271
  39.0 16.5 %collective-permute-start.10 = (bf16[4,4,7,16,128]{4,3,2,1,0:T(8,128)(2,1)S(1)}, bf16[4,4,7,16,128]{4,3,2,1,0:T(8,128)(2,1)S(1)}, u32[]{:S(2)}, u32[]{:S(2)}) collective-permute-start(bf16[4,4,7,16,128]{4,3,2,1,0:T(8,128)(2,1)S(1)} %pad_maximum_fusion.1.part_0), channel_id=1, source_target_pairs={{0,12},{1,49},{2,14},{3,51},{4,0},{5,53},{6,2},{7,55},{8,4},{9,57}... | collective-permute-start | bytes 1376264 | tf_op jit(solution)/shard_map/ppermute | solution.py:264
  46.2 11.4 %collective-permute-start.11 = (bf16[4,4,7,16,128]{4,3,2,1,0:T(8,128)(2,1)S(1)}, bf16[4,4,7,16,128]{4,3,2,1,0:T(8,128)(2,1)S(1)}, u32[]{:S(2)}, u32[]{:S(2)}) collective-permute-start(bf16[4,4,7,16,128]{4,3,2,1,0:T(8,128)(2,1)S(1)} %pad_maximum_fusion.1.part_0), channel_id=1, source_target_pairs={{0,8},{1,33},{2,10},{3,35},{4,12},{5,37},{6,14},{7,39},{8,0},{9,41... | collective-permute-start | bytes 1376264 | tf_op jit(solution)/shard_map/ppermute | solution.py:264
  51.1 11.4 %collective-permute-start.12 = (bf16[4,4,7,16,128]{4,3,2,1,0:T(8,128)(2,1)S(1)}, bf16[4,4,7,16,128]{4,3,2,1,0:T(8,128)(2,1)S(1)}, u32[]{:S(2)}, u32[]{:S(2)}) collective-permute-start(bf16[4,4,7,16,128]{4,3,2,1,0:T(8,128)(2,1)S(1)} %pad_maximum_fusion.1.part_0), channel_id=1, source_target_pairs={{0,4},{1,17},{2,6},{3,19},{4,8},{5,21},{6,10},{7,23},{8,12},{9,25}... | collective-permute-start | bytes 1376264 | tf_op jit(solution)/shard_map/ppermute | solution.py:264
  51.2 14.5 %collective-permute-start.6 = (bf16[3,8,80,128]{3,2,1,0:T(8,128)(2,1)S(1)}, bf16[3,8,80,128]{3,2,1,0:T(8,128)(2,1)S(1)}, u32[]{:S(2)}, u32[]{:S(2)}) collective-permute-start(bf16[3,8,80,128]{3,2,1,0:T(8,128)(2,1)S(1)} %pad_maximum_fusion), channel_id=1, source_target_pairs={{0,1},{1,0},{2,3},{3,2},{4,5},{5,4},{6,7},{7,6},{8,9},{9,8},{10,11... | collective-permute-start | bytes 1474568 | tf_op jit(solution)/shard_map/ppermute | solution.py:272
  65.6 1.6 %collective-permute-start.13 = (f32[8,16,512]{2,1,0:T(8,128)S(1)}, f32[8,16,512]{2,1,0:T(8,128)S(1)}, u32[]{:S(2)}, u32[]{:S(2)}) collective-permute-start(f32[8,16,512]{2,1,0:T(8,128)S(1)} %get-tuple-element.23), channel_id=1, source_target_pairs={{0,1},{1,0},{2,3},{3,2},{4,5},{5,4},{6,7},{7,6},{8,9},{9,8},{10,11... | collective-permute-start | bytes 786440 | tf_op jit(solution)/shard_map/ppermute | solution.py:286

commit v7 on v6

--- a/solution.py
+++ b/solution.py
@@ -115,6 +115,11 @@
             out_ref[zl, outer] = jnp.concatenate(pieces, axis=1)
 
 
+def stack_kernel(part_0, part_1, part_2, part_3, out_ref):
+    for k, ref in enumerate((part_0, part_1, part_2, part_3)):
+        out_ref[2 * k : 2 * k + 2] = ref[...]
+
+
 def shifted(pieces):
     whole = jnp.concatenate(pieces, axis=0)
     middle = pltpu.roll(whole.astype(F32), 640 - 64, 1).astype(BF16)
@@ -131,9 +136,14 @@
     return jnp.concatenate([value[:, 128 - by :], value[:, : 128 - by]], axis=1)
 
 
-def assemble(parts, weights_ref):
+def assemble(parts, first_ref, weights_ref):
     lane = lax.broadcasted_iota(jnp.int32, (PART * 16, 128), 1)
     half, even = lane < 64, lane % 64 < 32
+
+    def block(late, early):
+        if late == 1:
+            return first_ref if early == 3 else parts[1].at[early]
+        return parts[late].at[early]
 
     def turn(pick):
         for zl in range(4):
@@ -154,11 +164,11 @@
 
     @pl.when(lax.axis_index("core") == 0)
     def _():
-        turn(lambda y, x: parts[y].at[x])
+        turn(lambda y, x: block(y, x))
 
     @pl.when(lax.axis_index("core") == 1)
     def _():
-        turn(lambda y, x: parts[x].at[y])
+        turn(lambda y, x: block(x, y))
 
 
 def combine(before, middle, after):
@@ -169,10 +179,10 @@
 
 
 def grad_kernel(
-    low_ref, own_ref, high_ref, part_0, part_1, part_2, part_3,
+    low_ref, own_ref, high_ref, part_0, first_ref, part_1, part_2, part_3,
     keep_ref, send_ref, weights_ref, stack_ref, result_ref,
 ):
-    assemble((part_0, part_1, part_2, part_3), weights_ref)
+    assemble((part_0, part_1, part_2, part_3), first_ref, weights_ref)
     for dx, ref in enumerate((high_ref, own_ref, low_ref)):
         above, same, below = shifted([block_of(ref, g, ROWS) for g in range(GROUPS)])
         for dy, value in enumerate((below, same, above)):
@@ -257,14 +267,27 @@
     own = [routed[0]]
     for step in (1, 2, 3):
         own.append(lax.ppermute(routed[step], "y", [(i, (i - step) % 4) for i in range(4)]))
-    own = jnp.stack(own).reshape(GROUPS, 2 * ROWS, 128)
     unit = run(regroup_kernel, jax.ShapeDtypeStruct((4, PART, 16, 128), BF16), packed)
 
     def gather(block, pairs):
         return [block] + [lax.ppermute(block, AXES, pairs(step)) for step in (1, 2, 3)]
 
     unit = jnp.stack(gather(unit, functools.partial(along, True)))
-    parts = gather(unit, functools.partial(along, False))
+    parts = [unit]
+    for step in (1, 2, 3):
+        pairs = along(False, step)
+        if step == 1:
+            first = lax.ppermute(unit[3], AXES, pairs)
+            *own, first = lax.optimization_barrier((*own, first))
+            parts += [first, lax.ppermute(unit[:3], AXES, pairs)]
+        else:
+            parts.append(lax.ppermute(unit, AXES, pairs))
+    own = run(
+        stack_kernel,
+        jax.ShapeDtypeStruct((GROUPS, 2 * ROWS, 128), BF16),
+        *own,
+        byte_count=32 << 20,
+    )
     up = [(i, i + 1) for i in range(15)]
     down = [(b, a) for a, b in up]
     low = lax.ppermute(own, SPACE, up)

time: 88.5 us -> 83.6 us (0.945)
  blocking collectives: 20.2 us -> 15.5 us
  starting transfers between devices: 40.1 us -> 37.1 us
  waiting for transfers between devices: 18.3 us -> 20.9 us
    ppermute x6 -> x3, starting transfers between devices: 16.6 us -> 5.13 us  [gather(): lax.ppermute(block, AXES, pairs(step))]
    ppermute x6 -> x3, waiting for transfers between devices: 11.2 us -> 0.01 us  [gather(): lax.ppermute(block, AXES, pairs(step))]
    ppermute x0 -> x4, starting transfers between devices: none -> 7.78 us  [the longest x1 3.74 us: local(): parts += [first, lax.ppermute(unit[:3], AXES, pairs)]]
    all_to_all x1, waiting for transfers between devices: 0.01 us -> 6.39 us  [local(): packed = lax.all_to_all(packed, ('zl', 'zh'), 0, 0)]
    ppermute x1, waiting for transfers between devices: 0.01 us -> 6.32 us  [local(): low = lax.ppermute(own, SPACE, up)]
    ppermute x1, waiting for transfers between devices: 4.84 us -> 0.01 us  [local(): got = lax.ppermute(send, 'zh', swap)]
    all_to_all x1, blocking collectives: 20.2 us -> 15.5 us  [local(): merged = lax.all_to_all(merged, ('y', 'zh'), 0, 0)]
    ppermute x0 -> x4, waiting for transfers between devices: none -> 4.32 us  [the longest x1 4.31 us: local(): first = lax.ppermute(unit[3], AXES, pairs)]
  transfers between devices with their start and end apart: 15 -> 16, of which waited for: 6 -> 6; matrix products, arithmetic and copies ran while one was open for 0% -> 0% of each run, Pallas kernels for 6% -> 6%
where the time goes in v7:
time: 83.6 us; the launch traced here: 83.3 us
  starting transfers between devices  37.1 us (44%)
  waiting for transfers between devices  20.9 us (25%)
  blocking collectives  15.5 us (19%)
  Pallas kernels  7.89 us (9%)
  local copies, waits for them, and re-layouts  0.95 us (1%)
    all_to_all x1, blocking collectives, local(): merged = lax.all_to_all(merged, ('y', 'zh'), 0, 0)  15.5 us
    all_to_all x1, starting transfers between devices, local(): packed = lax.all_to_all(packed, ('zl', 'zh'), 0, 0)  8.58 us
    all_to_all x1, waiting for transfers between devices, local(): packed = lax.all_to_all(packed, ('zl', 'zh'), 0, 0)  6.39 us
    ppermute x1, waiting for transfers between devices, local(): low = lax.ppermute(own, SPACE, up)  6.32 us
    pallas_call x7, Pallas kernels, run(): call(kernel, out_shape, **options)(in_specs=[VMEM] * len(args))(*args)  5.9 us
    ppermute x3, starting transfers between devices, gather(): lax.ppermute(block, AXES, pairs(step))  5.13 us
    ppermute x3, starting transfers between devices, local(): lax.ppermute(routed[step], 'y', [(i, (i - step) % 4) for i in range(4)])  4.69 us
    ppermute x1, starting transfers between devices, local(): got = lax.ppermute(send, 'zh', swap)  4.47 us
  transfers between devices with their start and end apart: 16, of which 6 were waited for; matrix products, arithmetic and copies ran while one was open for 0% of the time, Pallas kernels for 6%

profile of v7, /device:TPU:32, one launch (start us, length us, event | category | flops | bytes accessed | tf_op | source)
XLA Modules:
  0.0 83.3 jit_solution(5463984101955340672)
XLA Ops:
  0.6 2.0 %shard_map.50 = (bf16[8,4,16,128]{3,2,1,0:T(8,128)(2,1)}, bf16[4,160,128]{2,1,0:T(8,128)(2,1)}, bf16[4,160,128]{2,1,0:T(8,128)(2,1)}) custom-call(bf16[16,4096]{1,0:T(8,128)(2,1)} %bitcast.21, bf16[16,4096]{1,0:T(8,128)(2,1)} %bitcast.22, bf16[27,16,16]{2,1,0:T(8,128)(2,1)} %bitcast.24), custom_call_target="tpu_custom_call" | custom-call | bytes 1048576 | tf_op jit(solution)/shard_map/pallas_call | solution.py:248
  2.6 8.6 %all-to-all-start = ((bf16[8,4,16,128]{3,2,1,0:T(8,128)(2,1)}), bf16[8,4,16,128]{3,2,1,0:T(8,128)(2,1)S(1)}, u32[]{:S(2)}, u32[]{:S(2)}) async-start(bf16[8,4,16,128]{3,2,1,0:T(8,128)(2,1)} %get-tuple-element.25), calls=%async_computation | async-start | bytes 262144 | tf_op jit(solution)/shard_map/all_to_all | solution.py:265
  11.2 4.5 %collective-permute-start = (bf16[4,160,128]{2,1,0:T(8,128)(2,1)}, bf16[4,160,128]{2,1,0:T(8,128)(2,1)S(1)}, u32[]{:S(2)}, u32[]{:S(2)}) collective-permute-start(bf16[4,160,128]{2,1,0:T(8,128)(2,1)} %get-tuple-element.20), channel_id=1, source_target_pairs={{0,2},{2,0},{1,3},{3,1},{4,6},{6,4},{5,7},{7,5},{8,10},{10,8},{9,1... | collective-permute-start | bytes 491528 | tf_op jit(solution)/shard_map/ppermute | solution.py:264
  15.7 6.4 %all-to-all-done.packed_ref = bf16[8,4,16,128]{3,2,1,0:T(8,128)(2,1)S(1)} async-done(((bf16[8,4,16,128]{3,2,1,0:T(8,128)(2,1)}), bf16[8,4,16,128]{3,2,1,0:T(8,128)(2,1)S(1)}, u32[]{:S(2)}, u32[]{:S(2)}) %all-to-all-start) | async-done | bytes 131104 | tf_op jit(solution)/shard_map/all_to_all | solution.py:265
  22.1 0.3 shard_map.52
  22.4 1.6 %collective-permute-start.4 = (bf16[4,7,16,128]{3,2,1,0:T(8,128)(2,1)S(1)}, bf16[4,7,16,128]{3,2,1,0:T(8,128)(2,1)S(1)}, u32[]{:S(2)}, u32[]{:S(2)}) collective-permute-start(bf16[4,7,16,128]{3,2,1,0:T(8,128)(2,1)S(1)} %shard_map.52), channel_id=1, source_target_pairs={{0,16},{1,5},{2,18},{3,7},{4,20},{5,9},{6,22},{7,11},{8,24},{9,13}... | collective-permute-start | bytes 344072 | tf_op jit(solution)/shard_map/ppermute | solution.py:273
  23.9 1.7 %collective-permute-start.9 = (bf16[4,7,16,128]{3,2,1,0:T(8,128)(2,1)S(1)}, bf16[4,7,16,128]{3,2,1,0:T(8,128)(2,1)S(1)}, u32[]{:S(2)}, u32[]{:S(2)}) collective-permute-start(bf16[4,7,16,128]{3,2,1,0:T(8,128)(2,1)S(1)} %shard_map.52), channel_id=1, source_target_pairs={{0,48},{1,13},{2,50},{3,15},{4,52},{5,1},{6,54},{7,3},{8,56},{9,5}... | collective-permute-start | bytes 344072 | tf_op jit(solution)/shard_map/ppermute | solution.py:273
  25.7 1.8 %collective-permute-start.10 = (bf16[4,7,16,128]{3,2,1,0:T(8,128)(2,1)S(1)}, bf16[4,7,16,128]{3,2,1,0:T(8,128)(2,1)S(1)}, u32[]{:S(2)}, u32[]{:S(2)}) collective-permute-start(bf16[4,7,16,128]{3,2,1,0:T(8,128)(2,1)S(1)} %shard_map.52), channel_id=1, source_target_pairs={{0,32},{1,9},{2,34},{3,11},{4,36},{5,13},{6,38},{7,15},{8,40},{9,1... | collective-permute-start | bytes 344072 | tf_op jit(solution)/shard_map/ppermute | solution.py:273
  27.5 0.0 collective-permute-done.got_ref
  27.5 0.0 copy-start
  27.5 0.9 %copy-done = bf16[4,160,128]{2,1,0:T(8,128)(2,1)S(1)} copy-done((bf16[4,160,128]{2,1,0:T(8,128)(2,1)S(1)}, bf16[4,160,128]{2,1,0:T(8,128)(2,1)}, u32[]{:S(2)}) %copy-start) | copy-done | bytes 163864
  28.4 3.1 %collective-permute-start.1 = (bf16[2,160,128]{2,1,0:T(8,128)(2,1)S(1)}, bf16[2,160,128]{2,1,0:T(8,128)(2,1)S(1)}, u32[]{:S(2)}, u32[]{:S(2)}) collective-permute-start(bf16[2,160,128]{2,1,0:T(8,128)(2,1)S(1)} %get-tuple-element.22), channel_id=1, source_target_pairs={{0,12},{4,0},{8,4},{12,8},{1,13},{5,1},{9,5},{13,9},{2,14},{6,2},{... | collective-permute-start | bytes 245768 | tf_op jit(solution)/shard_map/ppermute | solution.py:269
  31.5 0.6 collective-permute-start.2
  32.2 0.0 collective-permute-done.4
  32.2 1.0 %collective-permute-start.3 = (bf16[2,160,128]{2,1,0:T(8,128)(2,1)S(1)}, bf16[2,160,128]{2,1,0:T(8,128)(2,1)S(1)}, u32[]{:S(2)}, u32[]{:S(2)}) collective-permute-start(bf16[2,160,128]{2,1,0:T(8,128)(2,1)S(1)} %get-tuple-element.24), channel_id=1, source_target_pairs={{0,4},{4,8},{8,12},{12,0},{1,5},{5,9},{9,13},{13,1},{2,6},{6,10},{... | collective-permute-start | bytes 245768 | tf_op jit(solution)/shard_map/ppermute | solution.py:269
  33.1 0.0 collective-permute-done.9
  33.1 2.3 %collective-permute-start.5 = (bf16[4,7,16,128]{3,2,1,0:T(8,128)(2,1)S(1)}, bf16[4,7,16,128]{3,2,1,0:T(8,128)(2,1)S(1)}, u32[]{:S(2)}, u32[]{:S(2)}) collective-permute-start(bf16[4,7,16,128]{3,2,1,0:T(8,128)(2,1)S(1)} %collective-permute-done.4), channel_id=1, source_target_pairs={{0,12},{1,49},{2,14},{3,51},{4,0},{5,53},{6,2},{7,55},{8,4},{9,57}... | collective-permute-start | bytes 344072 | tf_op jit(solution)/shard_map/ppermute | solution.py:280
  35.4 0.0 collective-permute-done.10
  35.4 0.1 pad_maximum_fusion.1.part_0
  35.5 1.8 %collective-permute-start.12 = (bf16[4,4,7,16,128]{4,3,2,1,0:T(8,128)(2,1)S(1)}, bf16[4,4,7,16,128]{4,3,2,1,0:T(8,128)(2,1)S(1)}, u32[]{:S(2)}, u32[]{:S(2)}) collective-permute-start(bf16[4,4,7,16,128]{4,3,2,1,0:T(8,128)(2,1)S(1)} %pad_maximum_fusion.1.part_0), channel_id=1, source_target_pairs={{0,8},{1,33},{2,10},{3,35},{4,12},{5,37},{6,14},{7,39},{8,0},{9,41... | collective-permute-start | bytes 1376264 | tf_op jit(solution)/shard_map/ppermute | solution.py:284
  37.2 0.0 collective-permute-done.1.part_1
  37.2 0.0 collective-permute-start.13
  37.2 0.3 collective-permute-done.2.part_2
  37.5 0.8 collective-permute-done.3.part_3
  38.3 4.3 %collective-permute-done.5.first_ref = bf16[4,7,16,128]{3,2,1,0:T(8,128)(2,1)S(1)} collective-permute-done((bf16[4,7,16,128]{3,2,1,0:T(8,128)(2,1)S(1)}, bf16[4,7,16,128]{3,2,1,0:T(8,128)(2,1)S(1)}, u32[]{:S(2)}, u32[]{:S(2)}) %collective-permute-start.5) | collective-permute-done | bytes 114720 | tf_op jit(solution)/shard_map/ppermute | solution.py:280
  42.7 3.9 %collective-permute-start.7 = (bf16[8,160,128]{2,1,0:T(8,128)(2,1)S(1)}, bf16[8,160,128]{2,1,0:T(8,128)(2,1)S(1)}, u32[]{:S(2)}, u32[]{:S(2)}) collective-permute-start(bf16[8,160,128]{2,1,0:T(8,128)(2,1)S(1)} %shard_map.53.own_ref), channel_id=1, source_target_pairs={{16,0},{32,16},{48,32},{64,48},{80,64},{96,80},{112,96},{128,112},... | collective-permute-start | bytes 983048 | tf_op jit(solution)/shard_map/ppermute | solution.py:294
  46.7 3.7 %collective-permute-start.11 = (bf16[3,4,7,16,128]{4,3,2,1,0:T(8,128)(2,1)S(1)}, bf16[3,4,7,16,128]{4,3,2,1,0:T(8,128)(2,1)S(1)}, u32[]{:S(2)}, u32[]{:S(2)}) collective-permute-start(bf16[3,4,7,16,128]{4,3,2,1,0:T(8,128)(2,1)S(1)} %pad_maximum_fusion.2), channel_id=1, source_target_pairs={{0,12},{1,49},{2,14},{3,51},{4,0},{5,53},{6,2},{7,55},{8,4},{9,57}... | collective-permute-start | bytes 1032200 | tf_op jit(solution)/shard_map/ppermute | solution.py:282
  50.4 1.9 %collective-permute-start.6 = (bf16[8,160,128]{2,1,0:T(8,128)(2,1)S(1)}, bf16[8,160,128]{2,1,0:T(8,128)(2,1)S(1)}, u32[]{:S(2)}, u32[]{:S(2)}) collective-permute-start(bf16[8,160,128]{2,1,0:T(8,128)(2,1)S(1)} %shard_map.53.own_ref), channel_id=1, source_target_pairs={{0,16},{16,32},{32,48},{48,64},{64,80},{80,96},{96,112},{112,128},... | collective-permute-start | bytes 983048 | tf_op jit(solution)/shard_map/ppermute | solution.py:293
  52.3 2.8 %collective-permute-done.7.high_ref = bf16[8,160,128]{2,1,0:T(8,128)(2,1)S(1)} collective-permute-done((bf16[8,160,128]{2,1,0:T(8,128)(2,1)S(1)}, bf16[8,160,128]{2,1,0:T(8,128)(2,1)S(1)}, u32[]{:S(2)}, u32[]{:S(2)}) %collective-permute-start.7) | collective-permute-done | bytes 327712 | tf_op jit(solution)/shard_map/ppermute | solution.py:294
  55.1 6.3 %collective-permute-done.6.low_ref = bf16[8,160,128]{2,1,0:T(8,128)(2,1)S(1)} collective-permute-done((bf16[8,160,128]{2,1,0:T(8,128)(2,1)S(1)}, bf16[8,160,128]{2,1,0:T(8,128)(2,1)S(1)}, u32[]{:S(2)}, u32[]{:S(2)}) %collective-permute-start.6) | collective-permute-done | bytes 327712 | tf_op jit(solution)/shard_map/ppermute | solution.py:293
  61.5 0.1 pad_maximum_fusion
  61.5 0.1 collective-permute-start.8
  61.6 0.0 collective-permute-done.11.part_1
  61.7 0.0 collective-permute-done.12.part_2
  61.7 0.0 collective-permute-done.13.part_3
  61.7 3.4 %shard_map.54 = (f32[8,16,512]{2,1,0:T(8,128)S(1)}, f32[8,16,512]{2,1,0:T(8,128)S(1)}, bf16[28,256,128]{2,1,0:T(8,128)(2,1)S(1)}) custom-call(bf16[8,160,128]{2,1,0:T(8,128)(2,1)S(1)} %collective-permute-done.6.low_ref, bf16[8,160,128]{2,1,0:T(8,128)(2,1)S(1)} %shard_map.53.own_ref, bf16[8,160,128]{2,1,0:T(8,128)(2,1)S(1)} %collective-permute-done.7.high_ref, ...), custom_call_target="tpu_custom_call" | custom-call | flops 905969664 | bytes 4194304 | tf_op jit(solution)/shard_map/pallas_call | solution.py:63
  65.0 0.6 collective-permute-start.14
  65.6 0.0 collective-permute-done.8.other_ref
  65.6 1.5 %shard_map.55.output_ref = bf16[8,16,512]{2,1,0:T(8,128)(2,1)S(1)} custom-call(bf16[8,160,128]{2,1,0:T(8,128)(2,1)S(1)} %collective-permute-done.6.low_ref, bf16[8,160,128]{2,1,0:T(8,128)(2,1)S(1)} %shard_map.53.own_ref, bf16[8,160,128]{2,1,0:T(8,128)(2,1)S(1)} %collective-permute-done.7.high_ref, ...), custom_call_target="tpu_custom_call" | custom-call | flops 905969664 | bytes 4194304 | tf_op jit(solution)/shard_map/pallas_call | solution.py:63
  67.1 0.0 collective-permute-done.14.got_ref
  67.2 15.5 %all_to_all.10.packed_ref = bf16[8,32,512]{2,1,0:T(8,128)(2,1)S(1)} all-to-all(bf16[8,32,512]{2,1,0:T(8,128)(2,1)S(1)} %shard_map.56), channel_id=1, replica_groups=mesh['zl'=4,'x'=4,'y'=4,'zh'=2,'core'=2] {'y','zh'}, dimensions={0} | all-to-all | bytes 524288 | tf_op jit(solution)/shard_map/all_to_all | solution.py:326
  82.6 0.7 shard_map.57
  (7 shorter events, 0.2 us)
Async XLA Ops:
  2.6 19.4 %all-to-all-start = ((bf16[8,4,16,128]{3,2,1,0:T(8,128)(2,1)}), bf16[8,4,16,128]{3,2,1,0:T(8,128)(2,1)S(1)}, u32[]{:S(2)}, u32[]{:S(2)}) async-start(bf16[8,4,16,128]{3,2,1,0:T(8,128)(2,1)} %get-tuple-element.25), calls=%async_computation | async-start | bytes 262144 | tf_op jit(solution)/shard_map/all_to_all | solution.py:265
  11.2 16.3 %collective-permute-start = (bf16[4,160,128]{2,1,0:T(8,128)(2,1)}, bf16[4,160,128]{2,1,0:T(8,128)(2,1)S(1)}, u32[]{:S(2)}, u32[]{:S(2)}) collective-permute-start(bf16[4,160,128]{2,1,0:T(8,128)(2,1)} %get-tuple-element.20), channel_id=1, source_target_pairs={{0,2},{2,0},{1,3},{3,1},{4,6},{6,4},{5,7},{7,5},{8,10},{10,8},{9,1... | collective-permute-start | bytes 491528 | tf_op jit(solution)/shard_map/ppermute | solution.py:264
  22.4 9.8 %collective-permute-start.4 = (bf16[4,7,16,128]{3,2,1,0:T(8,128)(2,1)S(1)}, bf16[4,7,16,128]{3,2,1,0:T(8,128)(2,1)S(1)}, u32[]{:S(2)}, u32[]{:S(2)}) collective-permute-start(bf16[4,7,16,128]{3,2,1,0:T(8,128)(2,1)S(1)} %shard_map.52), channel_id=1, source_target_pairs={{0,16},{1,5},{2,18},{3,7},{4,20},{5,9},{6,22},{7,11},{8,24},{9,13}... | collective-permute-start | bytes 344072 | tf_op jit(solution)/shard_map/ppermute | solution.py:273
  23.9 9.2 %collective-permute-start.9 = (bf16[4,7,16,128]{3,2,1,0:T(8,128)(2,1)S(1)}, bf16[4,7,16,128]{3,2,1,0:T(8,128)(2,1)S(1)}, u32[]{:S(2)}, u32[]{:S(2)}) collective-permute-start(bf16[4,7,16,128]{3,2,1,0:T(8,128)(2,1)S(1)} %shard_map.52), channel_id=1, source_target_pairs={{0,48},{1,13},{2,50},{3,15},{4,52},{5,1},{6,54},{7,3},{8,56},{9,5}... | collective-permute-start | bytes 344072 | tf_op jit(solution)/shard_map/ppermute | solution.py:273
  25.7 9.7 %collective-permute-start.10 = (bf16[4,7,16,128]{3,2,1,0:T(8,128)(2,1)S(1)}, bf16[4,7,16,128]{3,2,1,0:T(8,128)(2,1)S(1)}, u32[]{:S(2)}, u32[]{:S(2)}) collective-permute-start(bf16[4,7,16,128]{3,2,1,0:T(8,128)(2,1)S(1)} %shard_map.52), channel_id=1, source_target_pairs={{0,32},{1,9},{2,34},{3,11},{4,36},{5,13},{6,38},{7,15},{8,40},{9,1... | collective-permute-start | bytes 344072 | tf_op jit(solution)/shard_map/ppermute | solution.py:273
  27.5 0.9 %copy-start = (bf16[4,160,128]{2,1,0:T(8,128)(2,1)S(1)}, bf16[4,160,128]{2,1,0:T(8,128)(2,1)}, u32[]{:S(2)}) copy-start(bf16[4,160,128]{2,1,0:T(8,128)(2,1)} %get-tuple-element.19.keep_ref) | copy-start | bytes 491524
  28.4 8.8 %collective-permute-start.1 = (bf16[2,160,128]{2,1,0:T(8,128)(2,1)S(1)}, bf16[2,160,128]{2,1,0:T(8,128)(2,1)S(1)}, u32[]{:S(2)}, u32[]{:S(2)}) collective-permute-start(bf16[2,160,128]{2,1,0:T(8,128)(2,1)S(1)} %get-tuple-element.22), channel_id=1, source_target_pairs={{0,12},{4,0},{8,4},{12,8},{1,13},{5,1},{9,5},{13,9},{2,14},{6,2},{... | collective-permute-start | bytes 245768 | tf_op jit(solution)/shard_map/ppermute | solution.py:269
  31.5 6.0 %collective-permute-start.2 = (bf16[2,160,128]{2,1,0:T(8,128)(2,1)S(1)}, bf16[2,160,128]{2,1,0:T(8,128)(2,1)S(1)}, u32[]{:S(2)}, u32[]{:S(2)}) collective-permute-start(bf16[2,160,128]{2,1,0:T(8,128)(2,1)S(1)} %get-tuple-element.23), channel_id=1, source_target_pairs={{0,8},{4,12},{8,0},{12,4},{1,9},{5,13},{9,1},{13,5},{2,10},{6,14},... | collective-permute-start | bytes 245768 | tf_op jit(solution)/shard_map/ppermute | solution.py:269
  32.2 6.2 %collective-permute-start.3 = (bf16[2,160,128]{2,1,0:T(8,128)(2,1)S(1)}, bf16[2,160,128]{2,1,0:T(8,128)(2,1)S(1)}, u32[]{:S(2)}, u32[]{:S(2)}) collective-permute-start(bf16[2,160,128]{2,1,0:T(8,128)(2,1)S(1)} %get-tuple-element.24), channel_id=1, source_target_pairs={{0,4},{4,8},{8,12},{12,0},{1,5},{5,9},{9,13},{13,1},{2,6},{6,10},{... | collective-permute-start | bytes 245768 | tf_op jit(solution)/shard_map/ppermute | solution.py:269
  33.1 9.5 %collective-permute-start.5 = (bf16[4,7,16,128]{3,2,1,0:T(8,128)(2,1)S(1)}, bf16[4,7,16,128]{3,2,1,0:T(8,128)(2,1)S(1)}, u32[]{:S(2)}, u32[]{:S(2)}) collective-permute-start(bf16[4,7,16,128]{3,2,1,0:T(8,128)(2,1)S(1)} %collective-permute-done.4), channel_id=1, source_target_pairs={{0,12},{1,49},{2,14},{3,51},{4,0},{5,53},{6,2},{7,55},{8,4},{9,57}... | collective-permute-start | bytes 344072 | tf_op jit(solution)/shard_map/ppermute | solution.py:280
  35.5 26.2 %collective-permute-start.12 = (bf16[4,4,7,16,128]{4,3,2,1,0:T(8,128)(2,1)S(1)}, bf16[4,4,7,16,128]{4,3,2,1,0:T(8,128)(2,1)S(1)}, u32[]{:S(2)}, u32[]{:S(2)}) collective-permute-start(bf16[4,4,7,16,128]{4,3,2,1,0:T(8,128)(2,1)S(1)} %pad_maximum_fusion.1.part_0), channel_id=1, source_target_pairs={{0,8},{1,33},{2,10},{3,35},{4,12},{5,37},{6,14},{7,39},{8,0},{9,41... | collective-permute-start | bytes 1376264 | tf_op jit(solution)/shard_map/ppermute | solution.py:284
  37.2 24.4 %collective-permute-start.13 = (bf16[4,4,7,16,128]{4,3,2,1,0:T(8,128)(2,1)S(1)}, bf16[4,4,7,16,128]{4,3,2,1,0:T(8,128)(2,1)S(1)}, u32[]{:S(2)}, u32[]{:S(2)}) collective-permute-start(bf16[4,4,7,16,128]{4,3,2,1,0:T(8,128)(2,1)S(1)} %pad_maximum_fusion.1.part_0), channel_id=1, source_target_pairs={{0,4},{1,17},{2,6},{3,19},{4,8},{5,21},{6,10},{7,23},{8,12},{9,25}... | collective-permute-start | bytes 1376264 | tf_op jit(solution)/shard_map/ppermute | solution.py:284
  42.7 12.4 %collective-permute-start.7 = (bf16[8,160,128]{2,1,0:T(8,128)(2,1)S(1)}, bf16[8,160,128]{2,1,0:T(8,128)(2,1)S(1)}, u32[]{:S(2)}, u32[]{:S(2)}) collective-permute-start(bf16[8,160,128]{2,1,0:T(8,128)(2,1)S(1)} %shard_map.53.own_ref), channel_id=1, source_target_pairs={{16,0},{32,16},{48,32},{64,48},{80,64},{96,80},{112,96},{128,112},... | collective-permute-start | bytes 983048 | tf_op jit(solution)/shard_map/ppermute | solution.py:294
  46.7 15.0 %collective-permute-start.11 = (bf16[3,4,7,16,128]{4,3,2,1,0:T(8,128)(2,1)S(1)}, bf16[3,4,7,16,128]{4,3,2,1,0:T(8,128)(2,1)S(1)}, u32[]{:S(2)}, u32[]{:S(2)}) collective-permute-start(bf16[3,4,7,16,128]{4,3,2,1,0:T(8,128)(2,1)S(1)} %pad_maximum_fusion.2), channel_id=1, source_target_pairs={{0,12},{1,49},{2,14},{3,51},{4,0},{5,53},{6,2},{7,55},{8,4},{9,57}... | collective-permute-start | bytes 1032200 | tf_op jit(solution)/shard_map/ppermute | solution.py:282
  50.4 11.1 %collective-permute-start.6 = (bf16[8,160,128]{2,1,0:T(8,128)(2,1)S(1)}, bf16[8,160,128]{2,1,0:T(8,128)(2,1)S(1)}, u32[]{:S(2)}, u32[]{:S(2)}) collective-permute-start(bf16[8,160,128]{2,1,0:T(8,128)(2,1)S(1)} %shard_map.53.own_ref), channel_id=1, source_target_pairs={{0,16},{16,32},{32,48},{48,64},{64,80},{80,96},{96,112},{112,128},... | collective-permute-start | bytes 983048 | tf_op jit(solution)/shard_map/ppermute | solution.py:293
  61.5 4.1 %collective-permute-start.8 = (bf16[3,8,80,128]{3,2,1,0:T(8,128)(2,1)S(1)}, bf16[3,8,80,128]{3,2,1,0:T(8,128)(2,1)S(1)}, u32[]{:S(2)}, u32[]{:S(2)}) collective-permute-start(bf16[3,8,80,128]{3,2,1,0:T(8,128)(2,1)S(1)} %pad_maximum_fusion), channel_id=1, source_target_pairs={{0,1},{1,0},{2,3},{3,2},{4,5},{5,4},{6,7},{7,6},{8,9},{9,8},{10,11... | collective-permute-start | bytes 1474568 | tf_op jit(solution)/shard_map/ppermute | solution.py:295
  65.0 2.1 %collective-permute-start.14 = (f32[8,16,512]{2,1,0:T(8,128)S(1)}, f32[8,16,512]{2,1,0:T(8,128)S(1)}, u32[]{:S(2)}, u32[]{:S(2)}) collective-permute-start(f32[8,16,512]{2,1,0:T(8,128)S(1)} %get-tuple-element.33), channel_id=1, source_target_pairs={{0,1},{1,0},{2,3},{3,2},{4,5},{5,4},{6,7},{7,6},{8,9},{9,8},{10,11... | collective-permute-start | bytes 786440 | tf_op jit(solution)/shard_map/ppermute | solution.py:309

commit v8 on v6

--- a/solution.py
+++ b/solution.py
@@ -64,7 +64,7 @@
 
 
 def pack_kernel(
-    volume_ref, cotangent_ref, filters_ref, packed_ref, keep_ref, send_ref,
+    volume_ref, cotangent_ref, filters_ref, packed_ref, send_ref,
     volume, cotangent, filters, slabs_ref, sems,
 ):
     pairs = ((filters_ref, filters), (volume_ref, volume), (cotangent_ref, cotangent))
@@ -93,8 +93,25 @@
                 slabs_ref[slab, row : row + 16, :] = pieces[4 * slab + chunk]
     zh = lax.axis_index("zh")
     for y in range(4):
+        send_ref[y] = slabs_ref[2 * y + 1 - zh]
+
+
+def keep_kernel(volume, cotangent, keep_ref, slabs_ref):
+    lane = lax.broadcasted_iota(jnp.int32, (16, 128), 1)
+    for part, ref in enumerate((volume, cotangent)):
+        whole = pltpu.roll(ref[...].astype(F32), 64, 1)
+        edge = whole[:, :128]
+        pieces = [jnp.where(lane < 64, 0.0, edge)]
+        pieces += [whole[:, 128 * j : 128 * (j + 1)] for j in range(1, 32)]
+        pieces += [jnp.where(lane < 64, edge, 0.0)]
+        pieces = [piece.astype(BF16) for piece in pieces]
+        for slab in range(GROUPS):
+            for chunk in range(CHUNKS):
+                row = part * ROWS + chunk * 16
+                slabs_ref[slab, row : row + 16, :] = pieces[4 * slab + chunk]
+    zh = lax.axis_index("zh")
+    for y in range(4):
         keep_ref[y] = slabs_ref[2 * y + zh]
-        send_ref[y] = slabs_ref[2 * y + 1 - zh]
 
 
 def route_kernel(keep_ref, got_ref, *out_refs):
@@ -168,11 +185,13 @@
     return middle + left + right
 
 
+def assemble_kernel(part_0, part_1, part_2, part_3, weights_ref):
+    assemble((part_0, part_1, part_2, part_3), weights_ref)
+
+
 def grad_kernel(
-    low_ref, own_ref, high_ref, part_0, part_1, part_2, part_3,
-    keep_ref, send_ref, weights_ref, stack_ref, result_ref,
+    low_ref, own_ref, high_ref, weights_ref, keep_ref, send_ref, stack_ref, result_ref,
 ):
-    assemble((part_0, part_1, part_2, part_3), weights_ref)
     for dx, ref in enumerate((high_ref, own_ref, low_ref)):
         above, same, below = shifted([block_of(ref, g, ROWS) for g in range(GROUPS)])
         for dy, value in enumerate((below, same, above)):
@@ -235,9 +254,9 @@
 def local(volume, filters, cotangent):
     swap = [(0, 1), (1, 0)]
     half = jax.ShapeDtypeStruct((4, 2 * ROWS, 128), BF16)
-    packed, keep, send = call(
+    packed, send = call(
         pack_kernel,
-        [jax.ShapeDtypeStruct((8, 4, 16, 128), BF16), half, half],
+        [jax.ShapeDtypeStruct((8, 4, 16, 128), BF16), half],
         scratch=[
             pltpu.VMEM((16, 4096), BF16),
             pltpu.VMEM((16, 4096), BF16),
@@ -252,6 +271,13 @@
         filters.reshape(OFFSETS, 16, 16),
     )
     got = lax.ppermute(send, "zh", swap)
+    keep = run(
+        keep_kernel,
+        half,
+        volume.reshape(16, 4096),
+        cotangent.reshape(16, 4096),
+        scratch=[pltpu.VMEM((GROUPS, 2 * ROWS, 128), BF16)],
+    )
     packed = lax.all_to_all(packed, ("zl", "zh"), 0, 0)
     routed = run(route_kernel, [jax.ShapeDtypeStruct((2, 2 * ROWS, 128), BF16)] * 4, keep, got)
     own = [routed[0]]
@@ -264,6 +290,7 @@
         return [block] + [lax.ppermute(block, AXES, pairs(step)) for step in (1, 2, 3)]
 
     unit = jnp.stack(gather(unit, functools.partial(along, True)))
+    own, _ = lax.optimization_barrier((own, unit))
     parts = gather(unit, functools.partial(along, False))
     up = [(i, i + 1) for i in range(15)]
     down = [(b, a) for a, b in up]
@@ -272,13 +299,19 @@
     other = lax.ppermute(jnp.stack([low[:, :ROWS], own[:, :ROWS], high[:, :ROWS]]), "core", swap)
     flops = 2 * 27 * 256 * 128 * CELLS
     piece = jax.ShapeDtypeStruct((GROUPS, 16, CELLS), F32)
-    keep, send, weights = run(
+    weights = run(
+        assemble_kernel,
+        jax.ShapeDtypeStruct((4 * PART, 256, 128), BF16),
+        *parts,
+        byte_count=64 << 20,
+    )
+    keep, send = run(
         grad_kernel,
-        [piece, piece, jax.ShapeDtypeStruct((4 * PART, 256, 128), BF16)],
+        [piece, piece],
         low,
         own,
         high,
-        *parts,
+        weights,
         flops=flops,
         byte_count=4 << 20,
         scratch=[pltpu.VMEM((9 * 128, CELLS), BF16), pltpu.VMEM((GROUPS, 2, 16, CELLS), F32)],

time: 88.5 us -> 82.5 us (0.932)
  starting transfers between devices: 40.1 us -> 33.8 us
  waiting for transfers between devices: 18.3 us -> 16.8 us
  blocking collectives: 20.2 us -> 21.1 us
  local copies, waits for them, and re-layouts: 0.95 us -> 1.84 us
    ppermute x1, waiting for transfers between devices: 0.01 us -> 8.6 us  [local(): low = lax.ppermute(own, SPACE, up)]
    ppermute x6, waiting for transfers between devices: 11.2 us -> 4.63 us  [gather(): lax.ppermute(block, AXES, pairs(step))]
    ppermute x6, starting transfers between devices: 16.6 us -> 11 us  [gather(): lax.ppermute(block, AXES, pairs(step))]
    ppermute x3, waiting for transfers between devices: 2.28 us -> 0.01 us  [local(): lax.ppermute(routed[step], 'y', [(i, (i - step) % 4) for i in range(4)])]
    ppermute x1, waiting for transfers between devices: 4.84 us -> 2.86 us  [local(): got = lax.ppermute(send, 'zh', swap)]
    ppermute x1, starting transfers between devices: 3.4 us -> 1.91 us  [local(): low = lax.ppermute(own, SPACE, up)]
    unnamed x2 -> x4, local copies, waits for them, and re-layouts: 0.92 us -> 1.81 us
    pallas_call x6 -> x8, Pallas kernels: 5.69 us -> 5.86 us  [run(): call(kernel, out_shape, **options)(in_specs=[VMEM] * len(args))(*args)]
  transfers between devices with their start and end apart: 15 -> 15, of which waited for: 6 -> 5; matrix products, arithmetic and copies ran while one was open for 0% -> 0% of each run, Pallas kernels for 6% -> 6%
where the time goes in v8:
time: 82.5 us; the launch traced here: 82.2 us
  starting transfers between devices  33.8 us (41%)
  blocking collectives  21.1 us (26%)
  waiting for transfers between devices  16.8 us (20%)
  Pallas kernels  7.78 us (9%)
  local copies, waits for them, and re-layouts  1.84 us (2%)
    all_to_all x1, blocking collectives, local(): merged = lax.all_to_all(merged, ('y', 'zh'), 0, 0)  21.1 us
    ppermute x6, starting transfers between devices, gather(): lax.ppermute(block, AXES, pairs(step))  11 us
    ppermute x1, waiting for transfers between devices, local(): low = lax.ppermute(own, SPACE, up)  8.6 us
    ppermute x1, starting transfers between devices, local(): got = lax.ppermute(send, 'zh', swap)  6.37 us
    pallas_call x8, Pallas kernels, run(): call(kernel, out_shape, **options)(in_specs=[VMEM] * len(args))(*args)  5.86 us
    ppermute x1, starting transfers between devices, local(): high = lax.ppermute(own, SPACE, down)  5.29 us
    ppermute x3, starting transfers between devices, local(): lax.ppermute(routed[step], 'y', [(i, (i - step) % 4) for i in range(4)])  4.69 us
    ppermute x6, waiting for transfers between devices, gather(): lax.ppermute(block, AXES, pairs(step))  4.63 us
  transfers between devices with their start and end apart: 15, of which 5 were waited for; matrix products, arithmetic and copies ran while one was open for 0% of the time, Pallas kernels for 6%

profile of v8, /device:TPU:32, one launch (start us, length us, event | category | flops | bytes accessed | tf_op | source)
XLA Modules:
  0.0 82.2 jit_solution(10159353316374826850)
XLA Ops:
  0.6 1.9 %shard_map.51 = (bf16[8,4,16,128]{3,2,1,0:T(8,128)(2,1)}, bf16[4,160,128]{2,1,0:T(8,128)(2,1)}) custom-call(bf16[16,4096]{1,0:T(8,128)(2,1)} %bitcast.25, bf16[16,4096]{1,0:T(8,128)(2,1)} %bitcast.27, bf16[27,16,16]{2,1,0:T(8,128)(2,1)} %bitcast.34), custom_call_target="tpu_custom_call" | custom-call | bytes 1048576 | tf_op jit(solution)/shard_map/pallas_call | solution.py:257
  2.6 6.4 %collective-permute-start = (bf16[4,160,128]{2,1,0:T(8,128)(2,1)}, bf16[4,160,128]{2,1,0:T(8,128)(2,1)S(1)}, u32[]{:S(2)}, u32[]{:S(2)}) collective-permute-start(bf16[4,160,128]{2,1,0:T(8,128)(2,1)} %get-tuple-element.13), channel_id=1, source_target_pairs={{0,2},{2,0},{1,3},{3,1},{4,6},{6,4},{5,7},{7,5},{8,10},{10,8},{9,1... | collective-permute-start | bytes 491528 | tf_op jit(solution)/shard_map/ppermute | solution.py:273
  8.9 4.3 %all-to-all-start = ((bf16[8,4,16,128]{3,2,1,0:T(8,128)(2,1)}), bf16[8,4,16,128]{3,2,1,0:T(8,128)(2,1)S(1)}, u32[]{:S(2)}, u32[]{:S(2)}) async-start(bf16[8,4,16,128]{3,2,1,0:T(8,128)(2,1)} %get-tuple-element.18), calls=%async_computation | async-start | bytes 262144 | tf_op jit(solution)/shard_map/all_to_all | solution.py:281
  13.2 0.0 copy-start
  13.2 0.9 %copy-done = bf16[16,1,4096]{2,0,1:T(8,128)(2,1)S(1)} copy-done((bf16[16,1,4096]{2,0,1:T(8,128)(2,1)S(1)}, bf16[16,1,4096]{2,0,1:T(8,128)(2,1)}, u32[]{:S(2)}) %copy-start) | copy-done | bytes 131096
  14.1 0.0 copy-start.1
  14.1 0.9 %copy-done.1 = bf16[16,1,4096]{2,0,1:T(8,128)(2,1)S(1)} copy-done((bf16[16,1,4096]{2,0,1:T(8,128)(2,1)S(1)}, bf16[16,1,4096]{2,0,1:T(8,128)(2,1)}, u32[]{:S(2)}) %copy-start.1) | copy-done | bytes 131096
  15.0 0.2 shard_map.50.keep_ref
  15.2 2.9 %collective-permute-done.got_ref = bf16[4,160,128]{2,1,0:T(8,128)(2,1)S(1)} collective-permute-done((bf16[4,160,128]{2,1,0:T(8,128)(2,1)}, bf16[4,160,128]{2,1,0:T(8,128)(2,1)S(1)}, u32[]{:S(2)}, u32[]{:S(2)}) %collective-permute-start) | collective-permute-done | bytes 163872 | tf_op jit(solution)/shard_map/ppermute | solution.py:273
  18.1 3.1 %collective-permute-start.1 = (bf16[2,160,128]{2,1,0:T(8,128)(2,1)S(1)}, bf16[2,160,128]{2,1,0:T(8,128)(2,1)S(1)}, u32[]{:S(2)}, u32[]{:S(2)}) collective-permute-start(bf16[2,160,128]{2,1,0:T(8,128)(2,1)S(1)} %get-tuple-element.15), channel_id=1, source_target_pairs={{0,12},{4,0},{8,4},{12,8},{1,13},{5,1},{9,5},{13,9},{2,14},{6,2},{... | collective-permute-start | bytes 245768 | tf_op jit(solution)/shard_map/ppermute | solution.py:285
  21.2 0.6 collective-permute-start.2
  21.8 1.0 %collective-permute-start.3 = (bf16[2,160,128]{2,1,0:T(8,128)(2,1)S(1)}, bf16[2,160,128]{2,1,0:T(8,128)(2,1)S(1)}, u32[]{:S(2)}, u32[]{:S(2)}) collective-permute-start(bf16[2,160,128]{2,1,0:T(8,128)(2,1)S(1)} %get-tuple-element.17), channel_id=1, source_target_pairs={{0,4},{4,8},{8,12},{12,0},{1,5},{5,9},{9,13},{13,1},{2,6},{6,10},{... | collective-permute-start | bytes 245768 | tf_op jit(solution)/shard_map/ppermute | solution.py:285
  22.8 0.0 all-to-all-done.packed_ref
  22.8 0.3 shard_map.53
  23.1 3.1 %collective-permute-start.5 = (bf16[4,7,16,128]{3,2,1,0:T(8,128)(2,1)S(1)}, bf16[4,7,16,128]{3,2,1,0:T(8,128)(2,1)S(1)}, u32[]{:S(2)}, u32[]{:S(2)}) collective-permute-start(bf16[4,7,16,128]{3,2,1,0:T(8,128)(2,1)S(1)} %shard_map.53), channel_id=1, source_target_pairs={{0,32},{1,9},{2,34},{3,11},{4,36},{5,13},{6,38},{7,15},{8,40},{9,1... | collective-permute-start | bytes 344072 | tf_op jit(solution)/shard_map/ppermute | solution.py:290
  26.2 0.6 collective-permute-start.6
  26.8 0.0 collective-permute-done.1
  26.8 2.6 %collective-permute-start.4 = (bf16[4,7,16,128]{3,2,1,0:T(8,128)(2,1)S(1)}, bf16[4,7,16,128]{3,2,1,0:T(8,128)(2,1)S(1)}, u32[]{:S(2)}, u32[]{:S(2)}) collective-permute-start(bf16[4,7,16,128]{3,2,1,0:T(8,128)(2,1)S(1)} %shard_map.53), channel_id=1, source_target_pairs={{0,48},{1,13},{2,50},{3,15},{4,52},{5,1},{6,54},{7,3},{8,56},{9,5}... | collective-permute-start | bytes 344072 | tf_op jit(solution)/shard_map/ppermute | solution.py:290
  29.4 0.0 collective-permute-done.2
  29.4 0.0 collective-permute-done.3
  29.5 0.0 collective-permute-done.5
  29.5 2.7 %collective-permute-done.6 = bf16[4,7,16,128]{3,2,1,0:T(8,128)(2,1)S(1)} collective-permute-done((bf16[4,7,16,128]{3,2,1,0:T(8,128)(2,1)S(1)}, bf16[4,7,16,128]{3,2,1,0:T(8,128)(2,1)S(1)}, u32[]{:S(2)}, u32[]{:S(2)}) %collective-permute-start.6) | collective-permute-done | bytes 114720 | tf_op jit(solution)/shard_map/ppermute | solution.py:290
  32.2 0.0 collective-permute-done.4
  32.2 0.1 pad_maximum_fusion.1.part_0
  32.2 5.3 %collective-permute-start.8 = (bf16[8,160,128]{2,1,0:T(8,128)(2,1)S(1)}, bf16[8,160,128]{2,1,0:T(8,128)(2,1)S(1)}, u32[]{:S(2)}, u32[]{:S(2)}) collective-permute-start(bf16[8,160,128]{2,1,0:T(8,128)(2,1)S(1)} %bitcast.20), channel_id=1, source_target_pairs={{16,0},{32,16},{48,32},{64,48},{80,64},{96,80},{112,96},{128,112},... | collective-permute-start | bytes 983048 | tf_op jit(solution)/shard_map/ppermute | solution.py:298
  37.5 3.1 %collective-permute-start.10 = (bf16[4,4,7,16,128]{4,3,2,1,0:T(8,128)(2,1)S(1)}, bf16[4,4,7,16,128]{4,3,2,1,0:T(8,128)(2,1)S(1)}, u32[]{:S(2)}, u32[]{:S(2)}) collective-permute-start(bf16[4,4,7,16,128]{4,3,2,1,0:T(8,128)(2,1)S(1)} %pad_maximum_fusion.1.part_0), channel_id=1, source_target_pairs={{0,12},{1,49},{2,14},{3,51},{4,0},{5,53},{6,2},{7,55},{8,4},{9,57}... | collective-permute-start | bytes 1376264 | tf_op jit(solution)/shard_map/ppermute | solution.py:290
  40.6 0.6 collective-permute-start.11
  41.3 1.0 %collective-permute-start.12 = (bf16[4,4,7,16,128]{4,3,2,1,0:T(8,128)(2,1)S(1)}, bf16[4,4,7,16,128]{4,3,2,1,0:T(8,128)(2,1)S(1)}, u32[]{:S(2)}, u32[]{:S(2)}) collective-permute-start(bf16[4,4,7,16,128]{4,3,2,1,0:T(8,128)(2,1)S(1)} %pad_maximum_fusion.1.part_0), channel_id=1, source_target_pairs={{0,4},{1,17},{2,6},{3,19},{4,8},{5,21},{6,10},{7,23},{8,12},{9,25}... | collective-permute-start | bytes 1376264 | tf_op jit(solution)/shard_map/ppermute | solution.py:290
  42.2 1.9 %collective-permute-start.7 = (bf16[8,160,128]{2,1,0:T(8,128)(2,1)S(1)}, bf16[8,160,128]{2,1,0:T(8,128)(2,1)S(1)}, u32[]{:S(2)}, u32[]{:S(2)}) collective-permute-start(bf16[8,160,128]{2,1,0:T(8,128)(2,1)S(1)} %bitcast.21), channel_id=1, source_target_pairs={{0,16},{16,32},{32,48},{48,64},{64,80},{80,96},{96,112},{112,128},... | collective-permute-start | bytes 983048 | tf_op jit(solution)/shard_map/ppermute | solution.py:297
  44.2 0.6 collective-permute-done.8.high_ref
  44.8 8.6 %collective-permute-done.7.low_ref = bf16[8,160,128]{2,1,0:T(8,128)(2,1)S(1)} collective-permute-done((bf16[8,160,128]{2,1,0:T(8,128)(2,1)S(1)}, bf16[8,160,128]{2,1,0:T(8,128)(2,1)S(1)}, u32[]{:S(2)}, u32[]{:S(2)}) %collective-permute-start.7) | collective-permute-done | bytes 327712 | tf_op jit(solution)/shard_map/ppermute | solution.py:297
  53.4 0.1 pad_maximum_fusion
  53.5 0.1 collective-permute-start.9
  53.6 0.0 collective-permute-done.10.part_1
  53.6 0.0 collective-permute-done.11.part_2
  53.6 1.9 %collective-permute-done.12.part_3 = bf16[4,4,7,16,128]{4,3,2,1,0:T(8,128)(2,1)S(1)} collective-permute-done((bf16[4,4,7,16,128]{4,3,2,1,0:T(8,128)(2,1)S(1)}, bf16[4,4,7,16,128]{4,3,2,1,0:T(8,128)(2,1)S(1)}, u32[]{:S(2)}, u32[]{:S(2)}) %collective-permute-start.12) | collective-permute-done | bytes 458784 | tf_op jit(solution)/shard_map/ppermute | solution.py:290
  55.5 1.9 %shard_map.54.weights_ref = bf16[28,256,128]{2,1,0:T(8,128)(2,1)S(1)} custom-call(bf16[4,4,7,16,128]{4,3,2,1,0:T(8,128)(2,1)S(1)} %pad_maximum_fusion.1.part_0, bf16[4,4,7,16,128]{4,3,2,1,0:T(8,128)(2,1)S(1)} %collective-permute-done.10.part_1, bf16[4,4,7,16,128]{4,3,2,1,0:T(8,128)(2,1)S(1)} %collective-permute-done.11.part_2, ...), custom_call_target="tpu_custom_call" | custom-call | bytes 67108864 | tf_op jit(solution)/shard_map/pallas_call | solution.py:63
  57.4 1.3 %shard_map.56 = (f32[8,16,512]{2,1,0:T(8,128)S(1)}, f32[8,16,512]{2,1,0:T(8,128)S(1)}) custom-call(bf16[8,160,128]{2,1,0:T(8,128)(2,1)S(1)} %collective-permute-done.7.low_ref, bf16[8,160,128]{2,1,0:T(8,128)(2,1)S(1)} %bitcast.23, bf16[8,160,128]{2,1,0:T(8,128)(2,1)S(1)} %collective-permute-done.8.high_ref, bf16[28,256,128]{2,1,0:T(8,128)(2,1)S(1)} %shard_map.54.weights_ref), custom_call_target="tpu_custom_call" | custom-call | flops 905969664 | bytes 4194304 | tf_op jit(solution)/shard_map/pallas_call | solution.py:63
  58.7 0.1 collective-permute-start.13
  58.8 0.0 collective-permute-done.9.other_ref
  58.8 1.5 %shard_map.55.output_ref = bf16[8,16,512]{2,1,0:T(8,128)(2,1)S(1)} custom-call(bf16[8,160,128]{2,1,0:T(8,128)(2,1)S(1)} %collective-permute-done.7.low_ref, bf16[8,160,128]{2,1,0:T(8,128)(2,1)S(1)} %bitcast.24, bf16[8,160,128]{2,1,0:T(8,128)(2,1)S(1)} %collective-permute-done.8.high_ref, bf16[3,8,80,128]{3,2,1,0:T(8,128)(2,1)S(1)} %collective-permute-done.9.other_ref, ...), custom_call_target="tpu_custom_call" | custom-call | flops 905969664 | bytes 4194304 | tf_op jit(solution)/shard_map/pallas_call | solution.py:63
  60.3 0.0 collective-permute-done.13.got_ref
  60.4 21.1 %all_to_all.10.packed_ref = bf16[8,32,512]{2,1,0:T(8,128)(2,1)S(1)} all-to-all(bf16[8,32,512]{2,1,0:T(8,128)(2,1)S(1)} %shard_map.57), channel_id=1, replica_groups=mesh['zl'=4,'x'=4,'y'=4,'zh'=2,'core'=2] {'y','zh'}, dimensions={0} | all-to-all | bytes 524288 | tf_op jit(solution)/shard_map/all_to_all | solution.py:336
  81.5 0.7 shard_map.58
  (6 shorter events, 0.1 us)
Async XLA Ops:
  2.6 15.5 %collective-permute-start = (bf16[4,160,128]{2,1,0:T(8,128)(2,1)}, bf16[4,160,128]{2,1,0:T(8,128)(2,1)S(1)}, u32[]{:S(2)}, u32[]{:S(2)}) collective-permute-start(bf16[4,160,128]{2,1,0:T(8,128)(2,1)} %get-tuple-element.13), channel_id=1, source_target_pairs={{0,2},{2,0},{1,3},{3,1},{4,6},{6,4},{5,7},{7,5},{8,10},{10,8},{9,1... | collective-permute-start | bytes 491528 | tf_op jit(solution)/shard_map/ppermute | solution.py:273
  8.9 13.9 %all-to-all-start = ((bf16[8,4,16,128]{3,2,1,0:T(8,128)(2,1)}), bf16[8,4,16,128]{3,2,1,0:T(8,128)(2,1)S(1)}, u32[]{:S(2)}, u32[]{:S(2)}) async-start(bf16[8,4,16,128]{3,2,1,0:T(8,128)(2,1)} %get-tuple-element.18), calls=%async_computation | async-start | bytes 262144 | tf_op jit(solution)/shard_map/all_to_all | solution.py:281
  13.2 0.9 %copy-start = (bf16[16,1,4096]{2,0,1:T(8,128)(2,1)S(1)}, bf16[16,1,4096]{2,0,1:T(8,128)(2,1)}, u32[]{:S(2)}) copy-start(bf16[16,1,4096]{2,0,1:T(8,128)(2,1)} %param.3) | copy-start | bytes 393220
  14.1 0.9 %copy-start.1 = (bf16[16,1,4096]{2,0,1:T(8,128)(2,1)S(1)}, bf16[16,1,4096]{2,0,1:T(8,128)(2,1)}, u32[]{:S(2)}) copy-start(bf16[16,1,4096]{2,0,1:T(8,128)(2,1)} %param.5) | copy-start | bytes 393220
  18.1 8.7 %collective-permute-start.1 = (bf16[2,160,128]{2,1,0:T(8,128)(2,1)S(1)}, bf16[2,160,128]{2,1,0:T(8,128)(2,1)S(1)}, u32[]{:S(2)}, u32[]{:S(2)}) collective-permute-start(bf16[2,160,128]{2,1,0:T(8,128)(2,1)S(1)} %get-tuple-element.15), channel_id=1, source_target_pairs={{0,12},{4,0},{8,4},{12,8},{1,13},{5,1},{9,5},{13,9},{2,14},{6,2},{... | collective-permute-start | bytes 245768 | tf_op jit(solution)/shard_map/ppermute | solution.py:285
  21.2 8.2 %collective-permute-start.2 = (bf16[2,160,128]{2,1,0:T(8,128)(2,1)S(1)}, bf16[2,160,128]{2,1,0:T(8,128)(2,1)S(1)}, u32[]{:S(2)}, u32[]{:S(2)}) collective-permute-start(bf16[2,160,128]{2,1,0:T(8,128)(2,1)S(1)} %get-tuple-element.16), channel_id=1, source_target_pairs={{0,8},{4,12},{8,0},{12,4},{1,9},{5,13},{9,1},{13,5},{2,10},{6,14},... | collective-permute-start | bytes 245768 | tf_op jit(solution)/shard_map/ppermute | solution.py:285
  21.8 7.6 %collective-permute-start.3 = (bf16[2,160,128]{2,1,0:T(8,128)(2,1)S(1)}, bf16[2,160,128]{2,1,0:T(8,128)(2,1)S(1)}, u32[]{:S(2)}, u32[]{:S(2)}) collective-permute-start(bf16[2,160,128]{2,1,0:T(8,128)(2,1)S(1)} %get-tuple-element.17), channel_id=1, source_target_pairs={{0,4},{4,8},{8,12},{12,0},{1,5},{5,9},{9,13},{13,1},{2,6},{6,10},{... | collective-permute-start | bytes 245768 | tf_op jit(solution)/shard_map/ppermute | solution.py:285
  23.1 6.4 %collective-permute-start.5 = (bf16[4,7,16,128]{3,2,1,0:T(8,128)(2,1)S(1)}, bf16[4,7,16,128]{3,2,1,0:T(8,128)(2,1)S(1)}, u32[]{:S(2)}, u32[]{:S(2)}) collective-permute-start(bf16[4,7,16,128]{3,2,1,0:T(8,128)(2,1)S(1)} %shard_map.53), channel_id=1, source_target_pairs={{0,32},{1,9},{2,34},{3,11},{4,36},{5,13},{6,38},{7,15},{8,40},{9,1... | collective-permute-start | bytes 344072 | tf_op jit(solution)/shard_map/ppermute | solution.py:290
  26.2 6.0 %collective-permute-start.6 = (bf16[4,7,16,128]{3,2,1,0:T(8,128)(2,1)S(1)}, bf16[4,7,16,128]{3,2,1,0:T(8,128)(2,1)S(1)}, u32[]{:S(2)}, u32[]{:S(2)}) collective-permute-start(bf16[4,7,16,128]{3,2,1,0:T(8,128)(2,1)S(1)} %shard_map.53), channel_id=1, source_target_pairs={{0,16},{1,5},{2,18},{3,7},{4,20},{5,9},{6,22},{7,11},{8,24},{9,13}... | collective-permute-start | bytes 344072 | tf_op jit(solution)/shard_map/ppermute | solution.py:290
  26.8 5.4 %collective-permute-start.4 = (bf16[4,7,16,128]{3,2,1,0:T(8,128)(2,1)S(1)}, bf16[4,7,16,128]{3,2,1,0:T(8,128)(2,1)S(1)}, u32[]{:S(2)}, u32[]{:S(2)}) collective-permute-start(bf16[4,7,16,128]{3,2,1,0:T(8,128)(2,1)S(1)} %shard_map.53), channel_id=1, source_target_pairs={{0,48},{1,13},{2,50},{3,15},{4,52},{5,1},{6,54},{7,3},{8,56},{9,5}... | collective-permute-start | bytes 344072 | tf_op jit(solution)/shard_map/ppermute | solution.py:290
  32.2 12.5 %collective-permute-start.8 = (bf16[8,160,128]{2,1,0:T(8,128)(2,1)S(1)}, bf16[8,160,128]{2,1,0:T(8,128)(2,1)S(1)}, u32[]{:S(2)}, u32[]{:S(2)}) collective-permute-start(bf16[8,160,128]{2,1,0:T(8,128)(2,1)S(1)} %bitcast.20), channel_id=1, source_target_pairs={{16,0},{32,16},{48,32},{64,48},{80,64},{96,80},{112,96},{128,112},... | collective-permute-start | bytes 983048 | tf_op jit(solution)/shard_map/ppermute | solution.py:298
  37.5 16.0 %collective-permute-start.10 = (bf16[4,4,7,16,128]{4,3,2,1,0:T(8,128)(2,1)S(1)}, bf16[4,4,7,16,128]{4,3,2,1,0:T(8,128)(2,1)S(1)}, u32[]{:S(2)}, u32[]{:S(2)}) collective-permute-start(bf16[4,4,7,16,128]{4,3,2,1,0:T(8,128)(2,1)S(1)} %pad_maximum_fusion.1.part_0), channel_id=1, source_target_pairs={{0,12},{1,49},{2,14},{3,51},{4,0},{5,53},{6,2},{7,55},{8,4},{9,57}... | collective-permute-start | bytes 1376264 | tf_op jit(solution)/shard_map/ppermute | solution.py:290
  40.6 13.0 %collective-permute-start.11 = (bf16[4,4,7,16,128]{4,3,2,1,0:T(8,128)(2,1)S(1)}, bf16[4,4,7,16,128]{4,3,2,1,0:T(8,128)(2,1)S(1)}, u32[]{:S(2)}, u32[]{:S(2)}) collective-permute-start(bf16[4,4,7,16,128]{4,3,2,1,0:T(8,128)(2,1)S(1)} %pad_maximum_fusion.1.part_0), channel_id=1, source_target_pairs={{0,8},{1,33},{2,10},{3,35},{4,12},{5,37},{6,14},{7,39},{8,0},{9,41... | collective-permute-start | bytes 1376264 | tf_op jit(solution)/shard_map/ppermute | solution.py:290
  41.3 14.3 %collective-permute-start.12 = (bf16[4,4,7,16,128]{4,3,2,1,0:T(8,128)(2,1)S(1)}, bf16[4,4,7,16,128]{4,3,2,1,0:T(8,128)(2,1)S(1)}, u32[]{:S(2)}, u32[]{:S(2)}) collective-permute-start(bf16[4,4,7,16,128]{4,3,2,1,0:T(8,128)(2,1)S(1)} %pad_maximum_fusion.1.part_0), channel_id=1, source_target_pairs={{0,4},{1,17},{2,6},{3,19},{4,8},{5,21},{6,10},{7,23},{8,12},{9,25}... | collective-permute-start | bytes 1376264 | tf_op jit(solution)/shard_map/ppermute | solution.py:290
  42.2 11.2 %collective-permute-start.7 = (bf16[8,160,128]{2,1,0:T(8,128)(2,1)S(1)}, bf16[8,160,128]{2,1,0:T(8,128)(2,1)S(1)}, u32[]{:S(2)}, u32[]{:S(2)}) collective-permute-start(bf16[8,160,128]{2,1,0:T(8,128)(2,1)S(1)} %bitcast.21), channel_id=1, source_target_pairs={{0,16},{16,32},{32,48},{48,64},{64,80},{80,96},{96,112},{112,128},... | collective-permute-start | bytes 983048 | tf_op jit(solution)/shard_map/ppermute | solution.py:297
  53.5 5.3 %collective-permute-start.9 = (bf16[3,8,80,128]{3,2,1,0:T(8,128)(2,1)S(1)}, bf16[3,8,80,128]{3,2,1,0:T(8,128)(2,1)S(1)}, u32[]{:S(2)}, u32[]{:S(2)}) collective-permute-start(bf16[3,8,80,128]{3,2,1,0:T(8,128)(2,1)S(1)} %pad_maximum_fusion), channel_id=1, source_target_pairs={{0,1},{1,0},{2,3},{3,2},{4,5},{5,4},{6,7},{7,6},{8,9},{9,8},{10,11... | collective-permute-start | bytes 1474568 | tf_op jit(solution)/shard_map/ppermute | solution.py:299
  58.7 1.6 %collective-permute-start.13 = (f32[8,16,512]{2,1,0:T(8,128)S(1)}, f32[8,16,512]{2,1,0:T(8,128)S(1)}, u32[]{:S(2)}, u32[]{:S(2)}) collective-permute-start(f32[8,16,512]{2,1,0:T(8,128)S(1)} %get-tuple-element.21), channel_id=1, source_target_pairs={{0,1},{1,0},{2,3},{3,2},{4,5},{5,4},{6,7},{7,6},{8,9},{9,8},{10,11... | collective-permute-start | bytes 786440 | tf_op jit(solution)/shard_map/ppermute | solution.py:319

commit v9 on v8

--- a/solution.py
+++ b/solution.py
@@ -296,7 +296,6 @@
     down = [(b, a) for a, b in up]
     low = lax.ppermute(own, SPACE, up)
     high = lax.ppermute(own, SPACE, down)
-    other = lax.ppermute(jnp.stack([low[:, :ROWS], own[:, :ROWS], high[:, :ROWS]]), "core", swap)
     flops = 2 * 27 * 256 * 128 * CELLS
     piece = jax.ShapeDtypeStruct((GROUPS, 16, CELLS), F32)
     weights = run(
@@ -305,6 +304,8 @@
         *parts,
         byte_count=64 << 20,
     )
+    low, high, weights = lax.optimization_barrier((low, high, weights))
+    other = lax.ppermute(jnp.stack([low[:, :ROWS], own[:, :ROWS], high[:, :ROWS]]), "core", swap)
     keep, send = run(
         grad_kernel,
         [piece, piece],

time: 82.5 us -> 76.4 us (0.926)
  waiting for transfers between devices: 16.8 us -> 9.07 us
  starting transfers between devices: 33.8 us -> 38 us
  blocking collectives: 21.1 us -> 18.2 us
    ppermute x1, waiting for transfers between devices: 8.6 us -> 0.01 us  [local(): low = lax.ppermute(own, SPACE, up)]
    all_to_all x1, waiting for transfers between devices: 0.01 us -> 6.39 us  [local(): packed = lax.all_to_all(packed, ('zl', 'zh'), 0, 0)]
    all_to_all x1, starting transfers between devices: 4.29 us -> 8.58 us  [local(): packed = lax.all_to_all(packed, ('zl', 'zh'), 0, 0)]
    ppermute x6, waiting for transfers between devices: 4.63 us -> 1.67 us  [gather(): lax.ppermute(block, AXES, pairs(step))]
    all_to_all x1, blocking collectives: 21.1 us -> 18.2 us  [local(): merged = lax.all_to_all(merged, ('y', 'zh'), 0, 0)]
    ppermute x1, waiting for transfers between devices: 2.86 us -> 0.01 us  [local(): got = lax.ppermute(send, 'zh', swap)]
    ppermute x1, starting transfers between devices: 6.37 us -> 4.47 us  [local(): got = lax.ppermute(send, 'zh', swap)]
  transfers between devices with their start and end apart: 15 -> 15, of which waited for: 5 -> 3; matrix products, arithmetic and copies ran while one was open for 0% -> 0% of each run, Pallas kernels for 6% -> 7%
where the time goes in v9:
time: 76.4 us; the launch traced here: 75.8 us
  starting transfers between devices  38 us (50%)
  blocking collectives  18.2 us (24%)
  waiting for transfers between devices  9.07 us (12%)
  Pallas kernels  7.8 us (10%)
  local copies, waits for them, and re-layouts  1.84 us (2%)
  between operations  0.79 us (1%)
    all_to_all x1, blocking collectives, local(): merged = lax.all_to_all(merged, ('y', 'zh'), 0, 0)  18.2 us
    ppermute x6, starting transfers between devices, gather(): lax.ppermute(block, AXES, pairs(step))  11.6 us
    all_to_all x1, starting transfers between devices, local(): packed = lax.all_to_all(packed, ('zl', 'zh'), 0, 0)  8.58 us
    all_to_all x1, waiting for transfers between devices, local(): packed = lax.all_to_all(packed, ('zl', 'zh'), 0, 0)  6.39 us
    ppermute x1, starting transfers between devices, local(): high = lax.ppermute(own, SPACE, down)  6.03 us
    pallas_call x8, Pallas kernels, run(): call(kernel, out_shape, **options)(in_specs=[VMEM] * len(args))(*args)  5.88 us
    ppermute x3, starting transfers between devices, local(): lax.ppermute(routed[step], 'y', [(i, (i - step) % 4) for i in range(4)])  4.69 us
    ppermute x1, starting transfers between devices, local(): got = lax.ppermute(send, 'zh', swap)  4.47 us
  transfers between devices with their start and end apart: 15, of which 3 were waited for; matrix products, arithmetic and copies ran while one was open for 0% of the time, Pallas kernels for 7%

profile of v9, /device:TPU:32, one launch (start us, length us, event | category | flops | bytes accessed | tf_op | source)
XLA Modules:
  0.0 75.8 jit_solution(2239930650848066378)
XLA Ops:
  0.6 1.9 %shard_map.51 = (bf16[8,4,16,128]{3,2,1,0:T(8,128)(2,1)}, bf16[4,160,128]{2,1,0:T(8,128)(2,1)}) custom-call(bf16[16,4096]{1,0:T(8,128)(2,1)} %bitcast.25, bf16[16,4096]{1,0:T(8,128)(2,1)} %bitcast.27, bf16[27,16,16]{2,1,0:T(8,128)(2,1)} %bitcast.34), custom_call_target="tpu_custom_call" | custom-call | bytes 1048576 | tf_op jit(solution)/shard_map/pallas_call | solution.py:257
  2.6 8.6 %all-to-all-start = ((bf16[8,4,16,128]{3,2,1,0:T(8,128)(2,1)}), bf16[8,4,16,128]{3,2,1,0:T(8,128)(2,1)S(1)}, u32[]{:S(2)}, u32[]{:S(2)}) async-start(bf16[8,4,16,128]{3,2,1,0:T(8,128)(2,1)} %get-tuple-element.21), calls=%async_computation | async-start | bytes 262144 | tf_op jit(solution)/shard_map/all_to_all | solution.py:281
  11.1 4.5 %collective-permute-start = (bf16[4,160,128]{2,1,0:T(8,128)(2,1)}, bf16[4,160,128]{2,1,0:T(8,128)(2,1)S(1)}, u32[]{:S(2)}, u32[]{:S(2)}) collective-permute-start(bf16[4,160,128]{2,1,0:T(8,128)(2,1)} %get-tuple-element.16), channel_id=1, source_target_pairs={{0,2},{2,0},{1,3},{3,1},{4,6},{6,4},{5,7},{7,5},{8,10},{10,8},{9,1... | collective-permute-start | bytes 491528 | tf_op jit(solution)/shard_map/ppermute | solution.py:273
  15.6 6.4 %all-to-all-done.packed_ref = bf16[8,4,16,128]{3,2,1,0:T(8,128)(2,1)S(1)} async-done(((bf16[8,4,16,128]{3,2,1,0:T(8,128)(2,1)}), bf16[8,4,16,128]{3,2,1,0:T(8,128)(2,1)S(1)}, u32[]{:S(2)}, u32[]{:S(2)}) %all-to-all-start) | async-done | bytes 131104 | tf_op jit(solution)/shard_map/all_to_all | solution.py:281
  22.0 0.3 shard_map.53
  22.3 3.1 %collective-permute-start.5 = (bf16[4,7,16,128]{3,2,1,0:T(8,128)(2,1)S(1)}, bf16[4,7,16,128]{3,2,1,0:T(8,128)(2,1)S(1)}, u32[]{:S(2)}, u32[]{:S(2)}) collective-permute-start(bf16[4,7,16,128]{3,2,1,0:T(8,128)(2,1)S(1)} %shard_map.53), channel_id=1, source_target_pairs={{0,32},{1,9},{2,34},{3,11},{4,36},{5,13},{6,38},{7,15},{8,40},{9,1... | collective-permute-start | bytes 344072 | tf_op jit(solution)/shard_map/ppermute | solution.py:290
  25.4 0.6 collective-permute-start.6
  26.0 2.6 %collective-permute-start.4 = (bf16[4,7,16,128]{3,2,1,0:T(8,128)(2,1)S(1)}, bf16[4,7,16,128]{3,2,1,0:T(8,128)(2,1)S(1)}, u32[]{:S(2)}, u32[]{:S(2)}) collective-permute-start(bf16[4,7,16,128]{3,2,1,0:T(8,128)(2,1)S(1)} %shard_map.53), channel_id=1, source_target_pairs={{0,48},{1,13},{2,50},{3,15},{4,52},{5,1},{6,54},{7,3},{8,56},{9,5}... | collective-permute-start | bytes 344072 | tf_op jit(solution)/shard_map/ppermute | solution.py:290
  28.6 0.0 copy-start
  28.6 0.9 %copy-done = bf16[16,1,4096]{2,0,1:T(8,128)(2,1)S(1)} copy-done((bf16[16,1,4096]{2,0,1:T(8,128)(2,1)S(1)}, bf16[16,1,4096]{2,0,1:T(8,128)(2,1)}, u32[]{:S(2)}) %copy-start) | copy-done | bytes 131096
  29.5 0.0 copy-start.1
  29.5 0.9 %copy-done.1 = bf16[16,1,4096]{2,0,1:T(8,128)(2,1)S(1)} copy-done((bf16[16,1,4096]{2,0,1:T(8,128)(2,1)S(1)}, bf16[16,1,4096]{2,0,1:T(8,128)(2,1)}, u32[]{:S(2)}) %copy-start.1) | copy-done | bytes 131096
  30.4 0.2 shard_map.50.keep_ref
  30.6 0.0 collective-permute-done.got_ref
  30.7 3.1 %collective-permute-start.1 = (bf16[2,160,128]{2,1,0:T(8,128)(2,1)S(1)}, bf16[2,160,128]{2,1,0:T(8,128)(2,1)S(1)}, u32[]{:S(2)}, u32[]{:S(2)}) collective-permute-start(bf16[2,160,128]{2,1,0:T(8,128)(2,1)S(1)} %get-tuple-element.18), channel_id=1, source_target_pairs={{0,12},{4,0},{8,4},{12,8},{1,13},{5,1},{9,5},{13,9},{2,14},{6,2},{... | collective-permute-start | bytes 245768 | tf_op jit(solution)/shard_map/ppermute | solution.py:285
  33.8 0.6 collective-permute-start.2
  34.4 0.0 collective-permute-done.5
  34.4 1.0 %collective-permute-start.3 = (bf16[2,160,128]{2,1,0:T(8,128)(2,1)S(1)}, bf16[2,160,128]{2,1,0:T(8,128)(2,1)S(1)}, u32[]{:S(2)}, u32[]{:S(2)}) collective-permute-start(bf16[2,160,128]{2,1,0:T(8,128)(2,1)S(1)} %get-tuple-element.20), channel_id=1, source_target_pairs={{0,4},{4,8},{8,12},{12,0},{1,5},{5,9},{9,13},{13,1},{2,6},{6,10},{... | collective-permute-start | bytes 245768 | tf_op jit(solution)/shard_map/ppermute | solution.py:285
  35.4 0.0 collective-permute-done.6
  35.4 0.0 collective-permute-done.4
  35.4 0.1 pad_maximum_fusion.1.part_0
  35.4 2.0 %collective-permute-start.10 = (bf16[4,4,7,16,128]{4,3,2,1,0:T(8,128)(2,1)S(1)}, bf16[4,4,7,16,128]{4,3,2,1,0:T(8,128)(2,1)S(1)}, u32[]{:S(2)}, u32[]{:S(2)}) collective-permute-start(bf16[4,4,7,16,128]{4,3,2,1,0:T(8,128)(2,1)S(1)} %pad_maximum_fusion.1.part_0), channel_id=1, source_target_pairs={{0,8},{1,33},{2,10},{3,35},{4,12},{5,37},{6,14},{7,39},{8,0},{9,41... | collective-permute-start | bytes 1376264 | tf_op jit(solution)/shard_map/ppermute | solution.py:290
  37.5 1.2 %collective-permute-start.11 = (bf16[4,4,7,16,128]{4,3,2,1,0:T(8,128)(2,1)S(1)}, bf16[4,4,7,16,128]{4,3,2,1,0:T(8,128)(2,1)S(1)}, u32[]{:S(2)}, u32[]{:S(2)}) collective-permute-start(bf16[4,4,7,16,128]{4,3,2,1,0:T(8,128)(2,1)S(1)} %pad_maximum_fusion.1.part_0), channel_id=1, source_target_pairs={{0,4},{1,17},{2,6},{3,19},{4,8},{5,21},{6,10},{7,23},{8,12},{9,25}... | collective-permute-start | bytes 1376264 | tf_op jit(solution)/shard_map/ppermute | solution.py:290
  38.6 0.0 collective-permute-done.1
  38.6 2.1 %collective-permute-start.9 = (bf16[4,4,7,16,128]{4,3,2,1,0:T(8,128)(2,1)S(1)}, bf16[4,4,7,16,128]{4,3,2,1,0:T(8,128)(2,1)S(1)}, u32[]{:S(2)}, u32[]{:S(2)}) collective-permute-start(bf16[4,4,7,16,128]{4,3,2,1,0:T(8,128)(2,1)S(1)} %pad_maximum_fusion.1.part_0), channel_id=1, source_target_pairs={{0,12},{1,49},{2,14},{3,51},{4,0},{5,53},{6,2},{7,55},{8,4},{9,57}... | collective-permute-start | bytes 1376264 | tf_op jit(solution)/shard_map/ppermute | solution.py:290
  40.7 0.0 collective-permute-done.2
  40.7 0.0 collective-permute-done.3
  40.8 1.9 %collective-permute-start.7 = (bf16[8,160,128]{2,1,0:T(8,128)(2,1)S(1)}, bf16[8,160,128]{2,1,0:T(8,128)(2,1)S(1)}, u32[]{:S(2)}, u32[]{:S(2)}) collective-permute-start(bf16[8,160,128]{2,1,0:T(8,128)(2,1)S(1)} %bitcast.20), channel_id=1, source_target_pairs={{0,16},{16,32},{32,48},{48,64},{64,80},{80,96},{96,112},{112,128},... | collective-permute-start | bytes 983048 | tf_op jit(solution)/shard_map/ppermute | solution.py:297
  42.7 6.0 %collective-permute-start.8 = (bf16[8,160,128]{2,1,0:T(8,128)(2,1)S(1)}, bf16[8,160,128]{2,1,0:T(8,128)(2,1)S(1)}, u32[]{:S(2)}, u32[]{:S(2)}) collective-permute-start(bf16[8,160,128]{2,1,0:T(8,128)(2,1)S(1)} %bitcast.21), channel_id=1, source_target_pairs={{16,0},{32,16},{48,32},{64,48},{80,64},{96,80},{112,96},{128,112},... | collective-permute-start | bytes 983048 | tf_op jit(solution)/shard_map/ppermute | solution.py:298
  48.7 0.0 collective-permute-done.10.part_2
  48.8 1.7 %collective-permute-done.11.part_3 = bf16[4,4,7,16,128]{4,3,2,1,0:T(8,128)(2,1)S(1)} collective-permute-done((bf16[4,4,7,16,128]{4,3,2,1,0:T(8,128)(2,1)S(1)}, bf16[4,4,7,16,128]{4,3,2,1,0:T(8,128)(2,1)S(1)}, u32[]{:S(2)}, u32[]{:S(2)}) %collective-permute-start.11) | collective-permute-done | bytes 458784 | tf_op jit(solution)/shard_map/ppermute | solution.py:290
  50.4 0.0 collective-permute-done.9.part_1
  50.4 1.9 %shard_map.54.weights_ref = bf16[28,256,128]{2,1,0:T(8,128)(2,1)S(1)} custom-call(bf16[4,4,7,16,128]{4,3,2,1,0:T(8,128)(2,1)S(1)} %pad_maximum_fusion.1.part_0, bf16[4,4,7,16,128]{4,3,2,1,0:T(8,128)(2,1)S(1)} %collective-permute-done.9.part_1, bf16[4,4,7,16,128]{4,3,2,1,0:T(8,128)(2,1)S(1)} %collective-permute-done.10.part_2, ...), custom_call_target="tpu_custom_call" | custom-call | bytes 67108864 | tf_op jit(solution)/shard_map/pallas_call | solution.py:63
  52.3 0.0 collective-permute-done.7.low_ref
  52.3 1.0 %collective-permute-done.8.high_ref = bf16[8,160,128]{2,1,0:T(8,128)(2,1)S(1)} collective-permute-done((bf16[8,160,128]{2,1,0:T(8,128)(2,1)S(1)}, bf16[8,160,128]{2,1,0:T(8,128)(2,1)S(1)}, u32[]{:S(2)}, u32[]{:S(2)}) %collective-permute-start.8) | collective-permute-done | bytes 327712 | tf_op jit(solution)/shard_map/ppermute | solution.py:298
  53.3 0.1 pad_maximum_fusion
  53.4 0.1 collective-permute-start.12
  53.5 1.3 %shard_map.56 = (f32[8,16,512]{2,1,0:T(8,128)S(1)}, f32[8,16,512]{2,1,0:T(8,128)S(1)}) custom-call(bf16[8,160,128]{2,1,0:T(8,128)(2,1)S(1)} %collective-permute-done.7.low_ref, bf16[8,160,128]{2,1,0:T(8,128)(2,1)S(1)} %bitcast.23, bf16[8,160,128]{2,1,0:T(8,128)(2,1)S(1)} %collective-permute-done.8.high_ref, bf16[28,256,128]{2,1,0:T(8,128)(2,1)S(1)} %shard_map.54.weights_ref), custom_call_target="tpu_custom_call" | custom-call | flops 905969664 | bytes 4194304 | tf_op jit(solution)/shard_map/pallas_call | solution.py:63
  54.8 0.6 collective-permute-start.13
  55.4 0.0 collective-permute-done.12.other_ref
  55.4 1.5 %shard_map.55.output_ref = bf16[8,16,512]{2,1,0:T(8,128)(2,1)S(1)} custom-call(bf16[8,160,128]{2,1,0:T(8,128)(2,1)S(1)} %collective-permute-done.7.low_ref, bf16[8,160,128]{2,1,0:T(8,128)(2,1)S(1)} %bitcast.24, bf16[8,160,128]{2,1,0:T(8,128)(2,1)S(1)} %collective-permute-done.8.high_ref, bf16[3,8,80,128]{3,2,1,0:T(8,128)(2,1)S(1)} %collective-permute-done.12.other_ref, ...), custom_call_target="tpu_custom_call" | custom-call | flops 905969664 | bytes 4194304 | tf_op jit(solution)/shard_map/pallas_call | solution.py:63
  56.9 0.0 collective-permute-done.13.got_ref
  56.9 18.2 %all_to_all.10.packed_ref = bf16[8,32,512]{2,1,0:T(8,128)(2,1)S(1)} all-to-all(bf16[8,32,512]{2,1,0:T(8,128)(2,1)S(1)} %shard_map.57), channel_id=1, replica_groups=mesh['zl'=4,'x'=4,'y'=4,'zh'=2,'core'=2] {'y','zh'}, dimensions={0} | all-to-all | bytes 524288 | tf_op jit(solution)/shard_map/all_to_all | solution.py:337
  75.1 0.7 shard_map.58
  (5 shorter events, 0.2 us)
Async XLA Ops:
  2.6 19.4 %all-to-all-start = ((bf16[8,4,16,128]{3,2,1,0:T(8,128)(2,1)}), bf16[8,4,16,128]{3,2,1,0:T(8,128)(2,1)S(1)}, u32[]{:S(2)}, u32[]{:S(2)}) async-start(bf16[8,4,16,128]{3,2,1,0:T(8,128)(2,1)} %get-tuple-element.21), calls=%async_computation | async-start | bytes 262144 | tf_op jit(solution)/shard_map/all_to_all | solution.py:281
  11.1 19.5 %collective-permute-start = (bf16[4,160,128]{2,1,0:T(8,128)(2,1)}, bf16[4,160,128]{2,1,0:T(8,128)(2,1)S(1)}, u32[]{:S(2)}, u32[]{:S(2)}) collective-permute-start(bf16[4,160,128]{2,1,0:T(8,128)(2,1)} %get-tuple-element.16), channel_id=1, source_target_pairs={{0,2},{2,0},{1,3},{3,1},{4,6},{6,4},{5,7},{7,5},{8,10},{10,8},{9,1... | collective-permute-start | bytes 491528 | tf_op jit(solution)/shard_map/ppermute | solution.py:273
  22.3 12.1 %collective-permute-start.5 = (bf16[4,7,16,128]{3,2,1,0:T(8,128)(2,1)S(1)}, bf16[4,7,16,128]{3,2,1,0:T(8,128)(2,1)S(1)}, u32[]{:S(2)}, u32[]{:S(2)}) collective-permute-start(bf16[4,7,16,128]{3,2,1,0:T(8,128)(2,1)S(1)} %shard_map.53), channel_id=1, source_target_pairs={{0,32},{1,9},{2,34},{3,11},{4,36},{5,13},{6,38},{7,15},{8,40},{9,1... | collective-permute-start | bytes 344072 | tf_op jit(solution)/shard_map/ppermute | solution.py:290
  25.4 10.0 %collective-permute-start.6 = (bf16[4,7,16,128]{3,2,1,0:T(8,128)(2,1)S(1)}, bf16[4,7,16,128]{3,2,1,0:T(8,128)(2,1)S(1)}, u32[]{:S(2)}, u32[]{:S(2)}) collective-permute-start(bf16[4,7,16,128]{3,2,1,0:T(8,128)(2,1)S(1)} %shard_map.53), channel_id=1, source_target_pairs={{0,16},{1,5},{2,18},{3,7},{4,20},{5,9},{6,22},{7,11},{8,24},{9,13}... | collective-permute-start | bytes 344072 | tf_op jit(solution)/shard_map/ppermute | solution.py:290
  26.0 9.4 %collective-permute-start.4 = (bf16[4,7,16,128]{3,2,1,0:T(8,128)(2,1)S(1)}, bf16[4,7,16,128]{3,2,1,0:T(8,128)(2,1)S(1)}, u32[]{:S(2)}, u32[]{:S(2)}) collective-permute-start(bf16[4,7,16,128]{3,2,1,0:T(8,128)(2,1)S(1)} %shard_map.53), channel_id=1, source_target_pairs={{0,48},{1,13},{2,50},{3,15},{4,52},{5,1},{6,54},{7,3},{8,56},{9,5}... | collective-permute-start | bytes 344072 | tf_op jit(solution)/shard_map/ppermute | solution.py:290
  28.6 0.9 %copy-start = (bf16[16,1,4096]{2,0,1:T(8,128)(2,1)S(1)}, bf16[16,1,4096]{2,0,1:T(8,128)(2,1)}, u32[]{:S(2)}) copy-start(bf16[16,1,4096]{2,0,1:T(8,128)(2,1)} %param.3) | copy-start | bytes 393220
  29.5 0.9 %copy-start.1 = (bf16[16,1,4096]{2,0,1:T(8,128)(2,1)S(1)}, bf16[16,1,4096]{2,0,1:T(8,128)(2,1)}, u32[]{:S(2)}) copy-start(bf16[16,1,4096]{2,0,1:T(8,128)(2,1)} %param.5) | copy-start | bytes 393220
  30.7 8.0 %collective-permute-start.1 = (bf16[2,160,128]{2,1,0:T(8,128)(2,1)S(1)}, bf16[2,160,128]{2,1,0:T(8,128)(2,1)S(1)}, u32[]{:S(2)}, u32[]{:S(2)}) collective-permute-start(bf16[2,160,128]{2,1,0:T(8,128)(2,1)S(1)} %get-tuple-element.18), channel_id=1, source_target_pairs={{0,12},{4,0},{8,4},{12,8},{1,13},{5,1},{9,5},{13,9},{2,14},{6,2},{... | collective-permute-start | bytes 245768 | tf_op jit(solution)/shard_map/ppermute | solution.py:285
  33.8 7.0 %collective-permute-start.2 = (bf16[2,160,128]{2,1,0:T(8,128)(2,1)S(1)}, bf16[2,160,128]{2,1,0:T(8,128)(2,1)S(1)}, u32[]{:S(2)}, u32[]{:S(2)}) collective-permute-start(bf16[2,160,128]{2,1,0:T(8,128)(2,1)S(1)} %get-tuple-element.19), channel_id=1, source_target_pairs={{0,8},{4,12},{8,0},{12,4},{1,9},{5,13},{9,1},{13,5},{2,10},{6,14},... | collective-permute-start | bytes 245768 | tf_op jit(solution)/shard_map/ppermute | solution.py:285
  34.4 6.3 %collective-permute-start.3 = (bf16[2,160,128]{2,1,0:T(8,128)(2,1)S(1)}, bf16[2,160,128]{2,1,0:T(8,128)(2,1)S(1)}, u32[]{:S(2)}, u32[]{:S(2)}) collective-permute-start(bf16[2,160,128]{2,1,0:T(8,128)(2,1)S(1)} %get-tuple-element.20), channel_id=1, source_target_pairs={{0,4},{4,8},{8,12},{12,0},{1,5},{5,9},{9,13},{13,1},{2,6},{6,10},{... | collective-permute-start | bytes 245768 | tf_op jit(solution)/shard_map/ppermute | solution.py:285
  35.4 13.3 %collective-permute-start.10 = (bf16[4,4,7,16,128]{4,3,2,1,0:T(8,128)(2,1)S(1)}, bf16[4,4,7,16,128]{4,3,2,1,0:T(8,128)(2,1)S(1)}, u32[]{:S(2)}, u32[]{:S(2)}) collective-permute-start(bf16[4,4,7,16,128]{4,3,2,1,0:T(8,128)(2,1)S(1)} %pad_maximum_fusion.1.part_0), channel_id=1, source_target_pairs={{0,8},{1,33},{2,10},{3,35},{4,12},{5,37},{6,14},{7,39},{8,0},{9,41... | collective-permute-start | bytes 1376264 | tf_op jit(solution)/shard_map/ppermute | solution.py:290
  37.5 13.0 %collective-permute-start.11 = (bf16[4,4,7,16,128]{4,3,2,1,0:T(8,128)(2,1)S(1)}, bf16[4,4,7,16,128]{4,3,2,1,0:T(8,128)(2,1)S(1)}, u32[]{:S(2)}, u32[]{:S(2)}) collective-permute-start(bf16[4,4,7,16,128]{4,3,2,1,0:T(8,128)(2,1)S(1)} %pad_maximum_fusion.1.part_0), channel_id=1, source_target_pairs={{0,4},{1,17},{2,6},{3,19},{4,8},{5,21},{6,10},{7,23},{8,12},{9,25}... | collective-permute-start | bytes 1376264 | tf_op jit(solution)/shard_map/ppermute | solution.py:290
  38.6 11.8 %collective-permute-start.9 = (bf16[4,4,7,16,128]{4,3,2,1,0:T(8,128)(2,1)S(1)}, bf16[4,4,7,16,128]{4,3,2,1,0:T(8,128)(2,1)S(1)}, u32[]{:S(2)}, u32[]{:S(2)}) collective-permute-start(bf16[4,4,7,16,128]{4,3,2,1,0:T(8,128)(2,1)S(1)} %pad_maximum_fusion.1.part_0), channel_id=1, source_target_pairs={{0,12},{1,49},{2,14},{3,51},{4,0},{5,53},{6,2},{7,55},{8,4},{9,57}... | collective-permute-start | bytes 1376264 | tf_op jit(solution)/shard_map/ppermute | solution.py:290
  40.8 11.5 %collective-permute-start.7 = (bf16[8,160,128]{2,1,0:T(8,128)(2,1)S(1)}, bf16[8,160,128]{2,1,0:T(8,128)(2,1)S(1)}, u32[]{:S(2)}, u32[]{:S(2)}) collective-permute-start(bf16[8,160,128]{2,1,0:T(8,128)(2,1)S(1)} %bitcast.20), channel_id=1, source_target_pairs={{0,16},{16,32},{32,48},{48,64},{64,80},{80,96},{96,112},{112,128},... | collective-permute-start | bytes 983048 | tf_op jit(solution)/shard_map/ppermute | solution.py:297
  42.7 10.6 %collective-permute-start.8 = (bf16[8,160,128]{2,1,0:T(8,128)(2,1)S(1)}, bf16[8,160,128]{2,1,0:T(8,128)(2,1)S(1)}, u32[]{:S(2)}, u32[]{:S(2)}) collective-permute-start(bf16[8,160,128]{2,1,0:T(8,128)(2,1)S(1)} %bitcast.21), channel_id=1, source_target_pairs={{16,0},{32,16},{48,32},{64,48},{80,64},{96,80},{112,96},{128,112},... | collective-permute-start | bytes 983048 | tf_op jit(solution)/shard_map/ppermute | solution.py:298
  53.4 2.0 %collective-permute-start.12 = (bf16[3,8,80,128]{3,2,1,0:T(8,128)(2,1)S(1)}, bf16[3,8,80,128]{3,2,1,0:T(8,128)(2,1)S(1)}, u32[]{:S(2)}, u32[]{:S(2)}) collective-permute-start(bf16[3,8,80,128]{3,2,1,0:T(8,128)(2,1)S(1)} %pad_maximum_fusion), channel_id=1, source_target_pairs={{0,1},{1,0},{2,3},{3,2},{4,5},{5,4},{6,7},{7,6},{8,9},{9,8},{10,11... | collective-permute-start | bytes 1474568 | tf_op jit(solution)/shard_map/ppermute | solution.py:308
  54.8 2.1 %collective-permute-start.13 = (f32[8,16,512]{2,1,0:T(8,128)S(1)}, f32[8,16,512]{2,1,0:T(8,128)S(1)}, u32[]{:S(2)}, u32[]{:S(2)}) collective-permute-start(f32[8,16,512]{2,1,0:T(8,128)S(1)} %get-tuple-element.27), channel_id=1, source_target_pairs={{0,1},{1,0},{2,3},{3,2},{4,5},{5,4},{6,7},{7,6},{8,9},{9,8},{10,11... | collective-permute-start | bytes 786440 | tf_op jit(solution)/shard_map/ppermute | solution.py:320

commit v10 on v9

--- a/solution.py
+++ b/solution.py
@@ -287,7 +287,8 @@
     unit = run(regroup_kernel, jax.ShapeDtypeStruct((4, PART, 16, 128), BF16), packed)
 
     def gather(block, pairs):
-        return [block] + [lax.ppermute(block, AXES, pairs(step)) for step in (1, 2, 3)]
+        got = {step: lax.ppermute(block, AXES, pairs(step)) for step in (2, 1, 3)}
+        return [block, got[1], got[2], got[3]]
 
     unit = jnp.stack(gather(unit, functools.partial(along, True)))
     own, _ = lax.optimization_barrier((own, unit))

time: 76.4 us -> 76.4 us (level)
  no operation moved by 1% of the time
where the time goes in v10:
time: 76.4 us; the launch traced here: 75.8 us
  starting transfers between devices  38 us (50%)
  blocking collectives  18.2 us (24%)
  waiting for transfers between devices  9.07 us (12%)
  Pallas kernels  7.8 us (10%)
  local copies, waits for them, and re-layouts  1.84 us (2%)
  between operations  0.79 us (1%)
    all_to_all x1, blocking collectives, local(): merged = lax.all_to_all(merged, ('y', 'zh'), 0, 0)  18.2 us
    ppermute x6, starting transfers between devices, gather(): got = {step: lax.ppermute(block, AXES, pairs(step)) for step in (2, 1, 3)}  11.6 us
    all_to_all x1, starting transfers between devices, local(): packed = lax.all_to_all(packed, ('zl', 'zh'), 0, 0)  8.58 us
    all_to_all x1, waiting for transfers between devices, local(): packed = lax.all_to_all(packed, ('zl', 'zh'), 0, 0)  6.39 us
    ppermute x1, starting transfers between devices, local(): high = lax.ppermute(own, SPACE, down)  6.03 us
    pallas_call x8, Pallas kernels, run(): call(kernel, out_shape, **options)(in_specs=[VMEM] * len(args))(*args)  5.88 us
    ppermute x3, starting transfers between devices, local(): lax.ppermute(routed[step], 'y', [(i, (i - step) % 4) for i in range(4)])  4.69 us
    ppermute x1, starting transfers between devices, local(): got = lax.ppermute(send, 'zh', swap)  4.47 us
  transfers between devices with their start and end apart: 15, of which 3 were waited for; matrix products, arithmetic and copies ran while one was open for 0% of the time, Pallas kernels for 7%

profile of v10, /device:TPU:32, one launch (start us, length us, event | category | flops | bytes accessed | tf_op | source)
XLA Modules:
  0.0 75.8 jit_solution(2239930650848066378)
XLA Ops:
  0.6 1.9 %shard_map.51 = (bf16[8,4,16,128]{3,2,1,0:T(8,128)(2,1)}, bf16[4,160,128]{2,1,0:T(8,128)(2,1)}) custom-call(bf16[16,4096]{1,0:T(8,128)(2,1)} %bitcast.25, bf16[16,4096]{1,0:T(8,128)(2,1)} %bitcast.27, bf16[27,16,16]{2,1,0:T(8,128)(2,1)} %bitcast.34), custom_call_target="tpu_custom_call" | custom-call | bytes 1048576 | tf_op jit(solution)/shard_map/pallas_call | solution.py:257
  2.6 8.6 %all-to-all-start = ((bf16[8,4,16,128]{3,2,1,0:T(8,128)(2,1)}), bf16[8,4,16,128]{3,2,1,0:T(8,128)(2,1)S(1)}, u32[]{:S(2)}, u32[]{:S(2)}) async-start(bf16[8,4,16,128]{3,2,1,0:T(8,128)(2,1)} %get-tuple-element.21), calls=%async_computation | async-start | bytes 262144 | tf_op jit(solution)/shard_map/all_to_all | solution.py:281
  11.1 4.5 %collective-permute-start = (bf16[4,160,128]{2,1,0:T(8,128)(2,1)}, bf16[4,160,128]{2,1,0:T(8,128)(2,1)S(1)}, u32[]{:S(2)}, u32[]{:S(2)}) collective-permute-start(bf16[4,160,128]{2,1,0:T(8,128)(2,1)} %get-tuple-element.16), channel_id=1, source_target_pairs={{0,2},{2,0},{1,3},{3,1},{4,6},{6,4},{5,7},{7,5},{8,10},{10,8},{9,1... | collective-permute-start | bytes 491528 | tf_op jit(solution)/shard_map/ppermute | solution.py:273
  15.6 6.4 %all-to-all-done.packed_ref = bf16[8,4,16,128]{3,2,1,0:T(8,128)(2,1)S(1)} async-done(((bf16[8,4,16,128]{3,2,1,0:T(8,128)(2,1)}), bf16[8,4,16,128]{3,2,1,0:T(8,128)(2,1)S(1)}, u32[]{:S(2)}, u32[]{:S(2)}) %all-to-all-start) | async-done | bytes 131104 | tf_op jit(solution)/shard_map/all_to_all | solution.py:281
  22.0 0.3 shard_map.53
  22.3 3.1 %collective-permute-start.5 = (bf16[4,7,16,128]{3,2,1,0:T(8,128)(2,1)S(1)}, bf16[4,7,16,128]{3,2,1,0:T(8,128)(2,1)S(1)}, u32[]{:S(2)}, u32[]{:S(2)}) collective-permute-start(bf16[4,7,16,128]{3,2,1,0:T(8,128)(2,1)S(1)} %shard_map.53), channel_id=1, source_target_pairs={{0,32},{1,9},{2,34},{3,11},{4,36},{5,13},{6,38},{7,15},{8,40},{9,1... | collective-permute-start | bytes 344072 | tf_op jit(solution)/shard_map/ppermute | solution.py:290
  25.4 0.6 collective-permute-start.6
  26.0 2.6 %collective-permute-start.4 = (bf16[4,7,16,128]{3,2,1,0:T(8,128)(2,1)S(1)}, bf16[4,7,16,128]{3,2,1,0:T(8,128)(2,1)S(1)}, u32[]{:S(2)}, u32[]{:S(2)}) collective-permute-start(bf16[4,7,16,128]{3,2,1,0:T(8,128)(2,1)S(1)} %shard_map.53), channel_id=1, source_target_pairs={{0,48},{1,13},{2,50},{3,15},{4,52},{5,1},{6,54},{7,3},{8,56},{9,5}... | collective-permute-start | bytes 344072 | tf_op jit(solution)/shard_map/ppermute | solution.py:290
  28.6 0.0 copy-start
  28.6 0.9 %copy-done = bf16[16,1,4096]{2,0,1:T(8,128)(2,1)S(1)} copy-done((bf16[16,1,4096]{2,0,1:T(8,128)(2,1)S(1)}, bf16[16,1,4096]{2,0,1:T(8,128)(2,1)}, u32[]{:S(2)}) %copy-start) | copy-done | bytes 131096
  29.5 0.0 copy-start.1
  29.5 0.9 %copy-done.1 = bf16[16,1,4096]{2,0,1:T(8,128)(2,1)S(1)} copy-done((bf16[16,1,4096]{2,0,1:T(8,128)(2,1)S(1)}, bf16[16,1,4096]{2,0,1:T(8,128)(2,1)}, u32[]{:S(2)}) %copy-start.1) | copy-done | bytes 131096
  30.4 0.2 shard_map.50.keep_ref
  30.6 0.0 collective-permute-done.got_ref
  30.7 3.1 %collective-permute-start.1 = (bf16[2,160,128]{2,1,0:T(8,128)(2,1)S(1)}, bf16[2,160,128]{2,1,0:T(8,128)(2,1)S(1)}, u32[]{:S(2)}, u32[]{:S(2)}) collective-permute-start(bf16[2,160,128]{2,1,0:T(8,128)(2,1)S(1)} %get-tuple-element.18), channel_id=1, source_target_pairs={{0,12},{4,0},{8,4},{12,8},{1,13},{5,1},{9,5},{13,9},{2,14},{6,2},{... | collective-permute-start | bytes 245768 | tf_op jit(solution)/shard_map/ppermute | solution.py:285
  33.8 0.6 collective-permute-start.2
  34.4 0.0 collective-permute-done.5
  34.4 1.0 %collective-permute-start.3 = (bf16[2,160,128]{2,1,0:T(8,128)(2,1)S(1)}, bf16[2,160,128]{2,1,0:T(8,128)(2,1)S(1)}, u32[]{:S(2)}, u32[]{:S(2)}) collective-permute-start(bf16[2,160,128]{2,1,0:T(8,128)(2,1)S(1)} %get-tuple-element.20), channel_id=1, source_target_pairs={{0,4},{4,8},{8,12},{12,0},{1,5},{5,9},{9,13},{13,1},{2,6},{6,10},{... | collective-permute-start | bytes 245768 | tf_op jit(solution)/shard_map/ppermute | solution.py:285
  35.4 0.0 collective-permute-done.6
  35.4 0.0 collective-permute-done.4
  35.4 0.1 pad_maximum_fusion.1.part_0
  35.4 2.0 %collective-permute-start.10 = (bf16[4,4,7,16,128]{4,3,2,1,0:T(8,128)(2,1)S(1)}, bf16[4,4,7,16,128]{4,3,2,1,0:T(8,128)(2,1)S(1)}, u32[]{:S(2)}, u32[]{:S(2)}) collective-permute-start(bf16[4,4,7,16,128]{4,3,2,1,0:T(8,128)(2,1)S(1)} %pad_maximum_fusion.1.part_0), channel_id=1, source_target_pairs={{0,8},{1,33},{2,10},{3,35},{4,12},{5,37},{6,14},{7,39},{8,0},{9,41... | collective-permute-start | bytes 1376264 | tf_op jit(solution)/shard_map/ppermute | solution.py:290
  37.5 1.2 %collective-permute-start.11 = (bf16[4,4,7,16,128]{4,3,2,1,0:T(8,128)(2,1)S(1)}, bf16[4,4,7,16,128]{4,3,2,1,0:T(8,128)(2,1)S(1)}, u32[]{:S(2)}, u32[]{:S(2)}) collective-permute-start(bf16[4,4,7,16,128]{4,3,2,1,0:T(8,128)(2,1)S(1)} %pad_maximum_fusion.1.part_0), channel_id=1, source_target_pairs={{0,4},{1,17},{2,6},{3,19},{4,8},{5,21},{6,10},{7,23},{8,12},{9,25}... | collective-permute-start | bytes 1376264 | tf_op jit(solution)/shard_map/ppermute | solution.py:290
  38.6 0.0 collective-permute-done.1
  38.6 2.1 %collective-permute-start.9 = (bf16[4,4,7,16,128]{4,3,2,1,0:T(8,128)(2,1)S(1)}, bf16[4,4,7,16,128]{4,3,2,1,0:T(8,128)(2,1)S(1)}, u32[]{:S(2)}, u32[]{:S(2)}) collective-permute-start(bf16[4,4,7,16,128]{4,3,2,1,0:T(8,128)(2,1)S(1)} %pad_maximum_fusion.1.part_0), channel_id=1, source_target_pairs={{0,12},{1,49},{2,14},{3,51},{4,0},{5,53},{6,2},{7,55},{8,4},{9,57}... | collective-permute-start | bytes 1376264 | tf_op jit(solution)/shard_map/ppermute | solution.py:290
  40.7 0.0 collective-permute-done.2
  40.7 0.0 collective-permute-done.3
  40.8 1.9 %collective-permute-start.7 = (bf16[8,160,128]{2,1,0:T(8,128)(2,1)S(1)}, bf16[8,160,128]{2,1,0:T(8,128)(2,1)S(1)}, u32[]{:S(2)}, u32[]{:S(2)}) collective-permute-start(bf16[8,160,128]{2,1,0:T(8,128)(2,1)S(1)} %bitcast.20), channel_id=1, source_target_pairs={{0,16},{16,32},{32,48},{48,64},{64,80},{80,96},{96,112},{112,128},... | collective-permute-start | bytes 983048 | tf_op jit(solution)/shard_map/ppermute | solution.py:298
  42.7 6.0 %collective-permute-start.8 = (bf16[8,160,128]{2,1,0:T(8,128)(2,1)S(1)}, bf16[8,160,128]{2,1,0:T(8,128)(2,1)S(1)}, u32[]{:S(2)}, u32[]{:S(2)}) collective-permute-start(bf16[8,160,128]{2,1,0:T(8,128)(2,1)S(1)} %bitcast.21), channel_id=1, source_target_pairs={{16,0},{32,16},{48,32},{64,48},{80,64},{96,80},{112,96},{128,112},... | collective-permute-start | bytes 983048 | tf_op jit(solution)/shard_map/ppermute | solution.py:299
  48.7 0.0 collective-permute-done.10.part_2
  48.8 1.7 %collective-permute-done.11.part_3 = bf16[4,4,7,16,128]{4,3,2,1,0:T(8,128)(2,1)S(1)} collective-permute-done((bf16[4,4,7,16,128]{4,3,2,1,0:T(8,128)(2,1)S(1)}, bf16[4,4,7,16,128]{4,3,2,1,0:T(8,128)(2,1)S(1)}, u32[]{:S(2)}, u32[]{:S(2)}) %collective-permute-start.11) | collective-permute-done | bytes 458784 | tf_op jit(solution)/shard_map/ppermute | solution.py:290
  50.4 0.0 collective-permute-done.9.part_1
  50.4 1.9 %shard_map.54.weights_ref = bf16[28,256,128]{2,1,0:T(8,128)(2,1)S(1)} custom-call(bf16[4,4,7,16,128]{4,3,2,1,0:T(8,128)(2,1)S(1)} %pad_maximum_fusion.1.part_0, bf16[4,4,7,16,128]{4,3,2,1,0:T(8,128)(2,1)S(1)} %collective-permute-done.9.part_1, bf16[4,4,7,16,128]{4,3,2,1,0:T(8,128)(2,1)S(1)} %collective-permute-done.10.part_2, ...), custom_call_target="tpu_custom_call" | custom-call | bytes 67108864 | tf_op jit(solution)/shard_map/pallas_call | solution.py:63
  52.3 0.0 collective-permute-done.7.low_ref
  52.3 1.0 %collective-permute-done.8.high_ref = bf16[8,160,128]{2,1,0:T(8,128)(2,1)S(1)} collective-permute-done((bf16[8,160,128]{2,1,0:T(8,128)(2,1)S(1)}, bf16[8,160,128]{2,1,0:T(8,128)(2,1)S(1)}, u32[]{:S(2)}, u32[]{:S(2)}) %collective-permute-start.8) | collective-permute-done | bytes 327712 | tf_op jit(solution)/shard_map/ppermute | solution.py:299
  53.3 0.1 pad_maximum_fusion
  53.4 0.1 collective-permute-start.12
  53.5 1.3 %shard_map.56 = (f32[8,16,512]{2,1,0:T(8,128)S(1)}, f32[8,16,512]{2,1,0:T(8,128)S(1)}) custom-call(bf16[8,160,128]{2,1,0:T(8,128)(2,1)S(1)} %collective-permute-done.7.low_ref, bf16[8,160,128]{2,1,0:T(8,128)(2,1)S(1)} %bitcast.23, bf16[8,160,128]{2,1,0:T(8,128)(2,1)S(1)} %collective-permute-done.8.high_ref, bf16[28,256,128]{2,1,0:T(8,128)(2,1)S(1)} %shard_map.54.weights_ref), custom_call_target="tpu_custom_call" | custom-call | flops 905969664 | bytes 4194304 | tf_op jit(solution)/shard_map/pallas_call | solution.py:63
  54.8 0.6 collective-permute-start.13
  55.4 0.0 collective-permute-done.12.other_ref
  55.4 1.5 %shard_map.55.output_ref = bf16[8,16,512]{2,1,0:T(8,128)(2,1)S(1)} custom-call(bf16[8,160,128]{2,1,0:T(8,128)(2,1)S(1)} %collective-permute-done.7.low_ref, bf16[8,160,128]{2,1,0:T(8,128)(2,1)S(1)} %bitcast.24, bf16[8,160,128]{2,1,0:T(8,128)(2,1)S(1)} %collective-permute-done.8.high_ref, bf16[3,8,80,128]{3,2,1,0:T(8,128)(2,1)S(1)} %collective-permute-done.12.other_ref, ...), custom_call_target="tpu_custom_call" | custom-call | flops 905969664 | bytes 4194304 | tf_op jit(solution)/shard_map/pallas_call | solution.py:63
  56.9 0.0 collective-permute-done.13.got_ref
  56.9 18.2 %all_to_all.10.packed_ref = bf16[8,32,512]{2,1,0:T(8,128)(2,1)S(1)} all-to-all(bf16[8,32,512]{2,1,0:T(8,128)(2,1)S(1)} %shard_map.57), channel_id=1, replica_groups=mesh['zl'=4,'x'=4,'y'=4,'zh'=2,'core'=2] {'y','zh'}, dimensions={0} | all-to-all | bytes 524288 | tf_op jit(solution)/shard_map/all_to_all | solution.py:338
  75.1 0.7 shard_map.58
  (5 shorter events, 0.2 us)
Async XLA Ops:
  2.6 19.4 %all-to-all-start = ((bf16[8,4,16,128]{3,2,1,0:T(8,128)(2,1)}), bf16[8,4,16,128]{3,2,1,0:T(8,128)(2,1)S(1)}, u32[]{:S(2)}, u32[]{:S(2)}) async-start(bf16[8,4,16,128]{3,2,1,0:T(8,128)(2,1)} %get-tuple-element.21), calls=%async_computation | async-start | bytes 262144 | tf_op jit(solution)/shard_map/all_to_all | solution.py:281
  11.1 19.5 %collective-permute-start = (bf16[4,160,128]{2,1,0:T(8,128)(2,1)}, bf16[4,160,128]{2,1,0:T(8,128)(2,1)S(1)}, u32[]{:S(2)}, u32[]{:S(2)}) collective-permute-start(bf16[4,160,128]{2,1,0:T(8,128)(2,1)} %get-tuple-element.16), channel_id=1, source_target_pairs={{0,2},{2,0},{1,3},{3,1},{4,6},{6,4},{5,7},{7,5},{8,10},{10,8},{9,1... | collective-permute-start | bytes 491528 | tf_op jit(solution)/shard_map/ppermute | solution.py:273
  22.3 12.1 %collective-permute-start.5 = (bf16[4,7,16,128]{3,2,1,0:T(8,128)(2,1)S(1)}, bf16[4,7,16,128]{3,2,1,0:T(8,128)(2,1)S(1)}, u32[]{:S(2)}, u32[]{:S(2)}) collective-permute-start(bf16[4,7,16,128]{3,2,1,0:T(8,128)(2,1)S(1)} %shard_map.53), channel_id=1, source_target_pairs={{0,32},{1,9},{2,34},{3,11},{4,36},{5,13},{6,38},{7,15},{8,40},{9,1... | collective-permute-start | bytes 344072 | tf_op jit(solution)/shard_map/ppermute | solution.py:290
  25.4 10.0 %collective-permute-start.6 = (bf16[4,7,16,128]{3,2,1,0:T(8,128)(2,1)S(1)}, bf16[4,7,16,128]{3,2,1,0:T(8,128)(2,1)S(1)}, u32[]{:S(2)}, u32[]{:S(2)}) collective-permute-start(bf16[4,7,16,128]{3,2,1,0:T(8,128)(2,1)S(1)} %shard_map.53), channel_id=1, source_target_pairs={{0,16},{1,5},{2,18},{3,7},{4,20},{5,9},{6,22},{7,11},{8,24},{9,13}... | collective-permute-start | bytes 344072 | tf_op jit(solution)/shard_map/ppermute | solution.py:290
  26.0 9.4 %collective-permute-start.4 = (bf16[4,7,16,128]{3,2,1,0:T(8,128)(2,1)S(1)}, bf16[4,7,16,128]{3,2,1,0:T(8,128)(2,1)S(1)}, u32[]{:S(2)}, u32[]{:S(2)}) collective-permute-start(bf16[4,7,16,128]{3,2,1,0:T(8,128)(2,1)S(1)} %shard_map.53), channel_id=1, source_target_pairs={{0,48},{1,13},{2,50},{3,15},{4,52},{5,1},{6,54},{7,3},{8,56},{9,5}... | collective-permute-start | bytes 344072 | tf_op jit(solution)/shard_map/ppermute | solution.py:290
  28.6 0.9 %copy-start = (bf16[16,1,4096]{2,0,1:T(8,128)(2,1)S(1)}, bf16[16,1,4096]{2,0,1:T(8,128)(2,1)}, u32[]{:S(2)}) copy-start(bf16[16,1,4096]{2,0,1:T(8,128)(2,1)} %param.3) | copy-start | bytes 393220
  29.5 0.9 %copy-start.1 = (bf16[16,1,4096]{2,0,1:T(8,128)(2,1)S(1)}, bf16[16,1,4096]{2,0,1:T(8,128)(2,1)}, u32[]{:S(2)}) copy-start(bf16[16,1,4096]{2,0,1:T(8,128)(2,1)} %param.5) | copy-start | bytes 393220
  30.7 8.0 %collective-permute-start.1 = (bf16[2,160,128]{2,1,0:T(8,128)(2,1)S(1)}, bf16[2,160,128]{2,1,0:T(8,128)(2,1)S(1)}, u32[]{:S(2)}, u32[]{:S(2)}) collective-permute-start(bf16[2,160,128]{2,1,0:T(8,128)(2,1)S(1)} %get-tuple-element.18), channel_id=1, source_target_pairs={{0,12},{4,0},{8,4},{12,8},{1,13},{5,1},{9,5},{13,9},{2,14},{6,2},{... | collective-permute-start | bytes 245768 | tf_op jit(solution)/shard_map/ppermute | solution.py:285
  33.8 7.0 %collective-permute-start.2 = (bf16[2,160,128]{2,1,0:T(8,128)(2,1)S(1)}, bf16[2,160,128]{2,1,0:T(8,128)(2,1)S(1)}, u32[]{:S(2)}, u32[]{:S(2)}) collective-permute-start(bf16[2,160,128]{2,1,0:T(8,128)(2,1)S(1)} %get-tuple-element.19), channel_id=1, source_target_pairs={{0,8},{4,12},{8,0},{12,4},{1,9},{5,13},{9,1},{13,5},{2,10},{6,14},... | collective-permute-start | bytes 245768 | tf_op jit(solution)/shard_map/ppermute | solution.py:285
  34.4 6.3 %collective-permute-start.3 = (bf16[2,160,128]{2,1,0:T(8,128)(2,1)S(1)}, bf16[2,160,128]{2,1,0:T(8,128)(2,1)S(1)}, u32[]{:S(2)}, u32[]{:S(2)}) collective-permute-start(bf16[2,160,128]{2,1,0:T(8,128)(2,1)S(1)} %get-tuple-element.20), channel_id=1, source_target_pairs={{0,4},{4,8},{8,12},{12,0},{1,5},{5,9},{9,13},{13,1},{2,6},{6,10},{... | collective-permute-start | bytes 245768 | tf_op jit(solution)/shard_map/ppermute | solution.py:285
  35.4 13.3 %collective-permute-start.10 = (bf16[4,4,7,16,128]{4,3,2,1,0:T(8,128)(2,1)S(1)}, bf16[4,4,7,16,128]{4,3,2,1,0:T(8,128)(2,1)S(1)}, u32[]{:S(2)}, u32[]{:S(2)}) collective-permute-start(bf16[4,4,7,16,128]{4,3,2,1,0:T(8,128)(2,1)S(1)} %pad_maximum_fusion.1.part_0), channel_id=1, source_target_pairs={{0,8},{1,33},{2,10},{3,35},{4,12},{5,37},{6,14},{7,39},{8,0},{9,41... | collective-permute-start | bytes 1376264 | tf_op jit(solution)/shard_map/ppermute | solution.py:290
  37.5 13.0 %collective-permute-start.11 = (bf16[4,4,7,16,128]{4,3,2,1,0:T(8,128)(2,1)S(1)}, bf16[4,4,7,16,128]{4,3,2,1,0:T(8,128)(2,1)S(1)}, u32[]{:S(2)}, u32[]{:S(2)}) collective-permute-start(bf16[4,4,7,16,128]{4,3,2,1,0:T(8,128)(2,1)S(1)} %pad_maximum_fusion.1.part_0), channel_id=1, source_target_pairs={{0,4},{1,17},{2,6},{3,19},{4,8},{5,21},{6,10},{7,23},{8,12},{9,25}... | collective-permute-start | bytes 1376264 | tf_op jit(solution)/shard_map/ppermute | solution.py:290
  38.6 11.8 %collective-permute-start.9 = (bf16[4,4,7,16,128]{4,3,2,1,0:T(8,128)(2,1)S(1)}, bf16[4,4,7,16,128]{4,3,2,1,0:T(8,128)(2,1)S(1)}, u32[]{:S(2)}, u32[]{:S(2)}) collective-permute-start(bf16[4,4,7,16,128]{4,3,2,1,0:T(8,128)(2,1)S(1)} %pad_maximum_fusion.1.part_0), channel_id=1, source_target_pairs={{0,12},{1,49},{2,14},{3,51},{4,0},{5,53},{6,2},{7,55},{8,4},{9,57}... | collective-permute-start | bytes 1376264 | tf_op jit(solution)/shard_map/ppermute | solution.py:290
  40.8 11.5 %collective-permute-start.7 = (bf16[8,160,128]{2,1,0:T(8,128)(2,1)S(1)}, bf16[8,160,128]{2,1,0:T(8,128)(2,1)S(1)}, u32[]{:S(2)}, u32[]{:S(2)}) collective-permute-start(bf16[8,160,128]{2,1,0:T(8,128)(2,1)S(1)} %bitcast.20), channel_id=1, source_target_pairs={{0,16},{16,32},{32,48},{48,64},{64,80},{80,96},{96,112},{112,128},... | collective-permute-start | bytes 983048 | tf_op jit(solution)/shard_map/ppermute | solution.py:298
  42.7 10.6 %collective-permute-start.8 = (bf16[8,160,128]{2,1,0:T(8,128)(2,1)S(1)}, bf16[8,160,128]{2,1,0:T(8,128)(2,1)S(1)}, u32[]{:S(2)}, u32[]{:S(2)}) collective-permute-start(bf16[8,160,128]{2,1,0:T(8,128)(2,1)S(1)} %bitcast.21), channel_id=1, source_target_pairs={{16,0},{32,16},{48,32},{64,48},{80,64},{96,80},{112,96},{128,112},... | collective-permute-start | bytes 983048 | tf_op jit(solution)/shard_map/ppermute | solution.py:299
  53.4 2.0 %collective-permute-start.12 = (bf16[3,8,80,128]{3,2,1,0:T(8,128)(2,1)S(1)}, bf16[3,8,80,128]{3,2,1,0:T(8,128)(2,1)S(1)}, u32[]{:S(2)}, u32[]{:S(2)}) collective-permute-start(bf16[3,8,80,128]{3,2,1,0:T(8,128)(2,1)S(1)} %pad_maximum_fusion), channel_id=1, source_target_pairs={{0,1},{1,0},{2,3},{3,2},{4,5},{5,4},{6,7},{7,6},{8,9},{9,8},{10,11... | collective-permute-start | bytes 1474568 | tf_op jit(solution)/shard_map/ppermute | solution.py:309
  54.8 2.1 %collective-permute-start.13 = (f32[8,16,512]{2,1,0:T(8,128)S(1)}, f32[8,16,512]{2,1,0:T(8,128)S(1)}, u32[]{:S(2)}, u32[]{:S(2)}) collective-permute-start(f32[8,16,512]{2,1,0:T(8,128)S(1)} %get-tuple-element.27), channel_id=1, source_target_pairs={{0,1},{1,0},{2,3},{3,2},{4,5},{5,4},{6,7},{7,6},{8,9},{9,8},{10,11... | collective-permute-start | bytes 786440 | tf_op jit(solution)/shard_map/ppermute | solution.py:321
